TPU v7x, 32 devices: a whole 2x2x4 slice. The times are simulated.
32 devices in a mesh: group: 4 (over x, core), leaf: 8 (over z, y).
Axes of the slice: x: 2, y: 2, z: 4, core: 2. Of those that a mesh axis runs over, the one named last changes fastest.
Arguments:
- top_modes: bfloat16 [1024, 512], P('group'), may hold values from -6 to 6
- low_modes: bfloat16 [2048, 512], P(('group', 'leaf')), may hold values from -6 to 6
- anc_top: int32 [32, 8], P(('group', 'leaf')), may hold values from 0 to 15, all different within a row
- anc_low: int32 [32, 8], P(('group', 'leaf')), may hold values from 0 to 7, all different within a row
- coupling: bfloat16 [49152, 1024], P(('group', 'leaf')), may hold values from -0.1875 to 0.1875
- leaf_mass: bfloat16 [49152, 1536], P(('group', 'leaf')), may hold values from -0.15625 to 0.15625
- leaf_modes: bfloat16 [49152, 128], P(('group', 'leaf')), may hold values from -0.5 to 0.5
- leaf_coef: bfloat16 [4096, 512], P(('group', 'leaf')), may hold values from -6 to 6
- kinv_top: float32 [1024, 64], P('group'), may hold values from -0.1875 to 0.1875
- kinv_low: float32 [2048, 64], P(('group', 'leaf')), may hold values from -0.25 to 0.25
Outputs:
- new_top: float32 [1024, 512], P('group')
- new_low: float32 [2048, 512], P(('group', 'leaf'))
- leaf_proj: bfloat16 [4096, 512], P(('group', 'leaf'))
Inputs may be any that keep to these rules, and one draw needn't show every extreme that they name: `anc_top`: each row names 8 different top separator blocks. `anc_low`: each row names 8 different leaf indices of the leaf's own subtree.
All inputs are finite; a program needn't handle non-finite values.
Results may differ from a plain program's by a relative error of at most 0.0057.
Values may be sent and summed in bfloat16 or wider, within the bound.
No kernel may reach another device: no remote copies, remote signals or barrier semaphores. Data moves between devices by JAX's collectives and lax.ppermute only.
A program may use at most 128 MiB of HBM per device.

v0:
```python
import jax
import jax.numpy as jnp
from jax import lax
from jax.sharding import PartitionSpec as P


def per_device(
    top_modes,
    low_modes,
    anc_top,
    anc_low,
    coupling,
    leaf_mass,
    leaf_modes,
    leaf_coef,
    kinv_top,
    kinv_low,
):
    sep_rows = kinv_low.shape[1]
    mode_count = low_modes.shape[1]
    top_slots = anc_top.shape[1]
    low_slots = anc_low.shape[1]
    owned_rows = kinv_top.shape[0]
    tops_all = lax.all_gather(top_modes, "group", axis=0, tiled=True)
    top_count = tops_all.shape[0] // sep_rows
    top_onehot = anc_top[0][:, None] == jnp.arange(top_count, dtype=jnp.int32)[None, :]
    top_sel = jnp.einsum(
        "ab,bsm->asm",
        top_onehot.astype(jnp.bfloat16),
        tops_all.reshape(top_count, sep_rows, mode_count),
        preferred_element_type=jnp.float32,
    )
    shard_rows = lax.all_gather(low_modes, "leaf", axis=0, tiled=True)
    block_count = shard_rows.shape[0] // sep_rows
    chosen = anc_low[0][:, None] == jnp.arange(block_count, dtype=jnp.int32)[None, :]
    low_sel = jnp.einsum(
        "ab,bsm->asm",
        chosen.astype(jnp.bfloat16),
        shard_rows.reshape(block_count, sep_rows, mode_count),
        preferred_element_type=jnp.float32,
    )
    stacked = (
        jnp.concatenate([top_sel, low_sel], axis=0).reshape(-1, mode_count).astype(jnp.bfloat16)
    )
    shapes = (
        jnp.dot(leaf_modes, leaf_coef, preferred_element_type=jnp.float32)
        - jnp.dot(coupling, stacked, preferred_element_type=jnp.float32)
    ).astype(jnp.bfloat16)
    weighted = jnp.dot(leaf_mass, shapes, preferred_element_type=jnp.float32).astype(jnp.bfloat16)
    loads = jnp.einsum("nk,nm->km", coupling, weighted, preferred_element_type=jnp.float32)
    leaf_proj = jnp.einsum(
        "nk,nm->km", leaf_modes, weighted, preferred_element_type=jnp.float32
    ).astype(jnp.bfloat16)
    top_part = loads[: top_slots * sep_rows].reshape(top_slots, sep_rows, mode_count)
    low_part = loads[top_slots * sep_rows :].reshape(low_slots, sep_rows, mode_count)
    top_term = jnp.einsum(
        "ab,asm->bsm", top_onehot.astype(jnp.float32), top_part, precision=lax.Precision.HIGHEST
    ).reshape(top_count * sep_rows, mode_count)
    summed = lax.psum(top_term, ("group", "leaf"))
    owned = lax.dynamic_slice_in_dim(summed, lax.axis_index("group") * owned_rows, owned_rows, 0)
    block_count = sep_rows * lax.axis_size("leaf") // sep_rows
    chosen = anc_low[0][:, None] == jnp.arange(block_count, dtype=jnp.int32)[None, :]
    low_loads = lax.psum_scatter(
        jnp.einsum(
            "ab,asm->bsm", chosen.astype(jnp.float32), low_part, precision=lax.Precision.HIGHEST
        ).reshape(sep_rows * lax.axis_size("leaf"), mode_count),
        "leaf",
        scatter_dimension=0,
        tiled=True,
    )
    new_top = jnp.einsum(
        "brs,bsm->brm",
        kinv_top.reshape(-1, sep_rows, sep_rows),
        owned.reshape(-1, sep_rows, mode_count),
        precision=lax.Precision.HIGHEST,
    ).reshape(owned_rows, mode_count)
    new_low = jnp.dot(kinv_low, low_loads, precision=lax.Precision.HIGHEST)
    return (new_top, new_low, leaf_proj)


def solution(mesh):
    return jax.shard_map(
        per_device,
        mesh=mesh,
        in_specs=(
            P("group", None),
            P(("group", "leaf"), None),
            P(("group", "leaf"), None),
            P(("group", "leaf"), None),
            P(("group", "leaf"), None),
            P(("group", "leaf"), None),
            P(("group", "leaf"), None),
            P(("group", "leaf"), None),
            P("group", None),
            P(("group", "leaf"), None),
        ),
        out_specs=(P("group", None), P(("group", "leaf"), None), P(("group", "leaf"), None)),
        check_vma=False,
    )
```

profile of v0, /device:TPU:0, one launch (start us, length us, event | category | flops | bytes accessed | tf_op | source)
XLA Modules:
  0.0 280.0 jit_solution(12716725043273122388)
XLA Ops:
  7.2 0.7 all-gather.2.cloned.1.call-update
  8.0 33.4 %all_gather.7 = bf16[512,512]{1,0:T(8,128)(2,1)S(1)} all-gather(bf16[64,512]{1,0:T(8,128)(2,1)} %param.11), channel_id=1, replica_groups=mesh['group'=4,'leaf'=8] {'leaf'}, dimensions={0}, use_global_device_ids=true | all-gather | bytes 589824 | tf_op jit(solution)/shard_map/all_gather | solution.py:33
  41.4 1.9 convolution_convert_fusion.2
  43.3 1.9 convolution_convert_fusion.1
  45.2 1.2 pad_maximum_fusion
  46.4 0.6 copy.21
  47.0 3.4 %convolution_bitcast_fusion = f32[1536,512]{1,0:T(8,128)} fusion(bf16[1536,1024]{1,0:T(8,128)(2,1)S(1)} %copy-done, bf16[1024,512]{1,0:T(8,128)(2,1)S(1)} %bitcast.51), kind=kOutput, calls=%fused_computation.1 | convolution fusion | flops 1610612736 | bytes 7340032 | tf_op jit(solution)/shard_map/dot_general | solution.py:47
  50.4 7.5 %convolution_convert_fusion = bf16[512,1536]{1,0:T(8,128)(2,1)} fusion(bf16[1536,1536]{1,0:T(8,128)(2,1)} %param.15, f32[1536,512]{1,0:T(8,128)} %convolution_bitcast_fusion, bf16[1536,128]{1,0:T(8,128)(2,1)S(1)} %copy-done.1, bf16[128,512]{1,0:T(8,128)(2,1)} %param.17), kind=kOutput, calls=%fused_computation.3 | convolution fusion | flops 2619604992 | bytes 9961472 | tf_op jit(solution)/shard_map/dot_general | solution.py:49
  57.9 3.2 %convolution_bitcast_fusion.1 = f32[1024,512]{0,1:T(8,128)S(1)} fusion(bf16[512,1536]{1,0:T(8,128)(2,1)} %convolution_convert_fusion, bf16[1536,1024]{1,0:T(8,128)(2,1)S(1)} %copy-done), kind=kOutput, calls=%fused_computation.4 | convolution fusion | flops 1610612736 | bytes 6815744 | tf_op jit(solution)/shard_map/nk,nm->km/dot_general | solution.py:50
  61.1 1.6 fusion.18
  62.7 2.6 copy.22
  65.3 2.7 fusion.4
  68.0 2.5 copy.24
  70.6 0.2 reduce-scatter.2.cloned.1.call-start
  70.8 2.5 copy.26
  73.3 2.4 fusion.2
  75.7 1.6 copy.28
  77.5 2.1 fusion.1
  79.6 0.8 copy.29
  80.3 125.2 %all-reduce.2.cloned.1.call-done = f32[1024,512]{1,0:T(8,128)} async-done(((f32[1024,512]{1,0:T(8,128)}), f32[1024,512]{1,0:T(8,128)}) %all-reduce.2.cloned.1.call-update) | async-done | bytes 2097168 | tf_op jit(solution)/shard_map/psum | solution.py:59
  205.6 1.1 constant_dynamic-slice_fusion
  206.7 1.4 fusion.19
  208.1 63.6 %reduce-scatter.2.cloned.1.call-done = f32[64,512]{1,0:T(8,128)} async-done(((f32[512,512]{1,0:T(8,128)}), f32[64,512]{1,0:T(8,128)}) %reduce-scatter.2.cloned.1.call-update) | async-done | bytes 131088 | tf_op jit(solution)/shard_map/reduce_scatter | solution.py:63
  271.6 1.8 convolution_bitcast_fusion.2
  (18 shorter events, 0.2 us)
Async XLA Ops:
  7.2 39.8 %copy-start = (bf16[1536,1024]{1,0:T(8,128)(2,1)S(1)}, bf16[1536,1024]{1,0:T(8,128)(2,1)}, u32[]{:S(2)}) copy-start(bf16[1536,1024]{1,0:T(8,128)(2,1)} %param.14) | copy-start | bytes 9437188
  7.2 36.1 %all-gather.2.cloned.1.call-start = ((), (), s32[]{:S(2)}) async-start(), calls=%async_computation.1 | async-start | bytes 1310720 | tf_op jit(solution)/shard_map/all_gather | solution.py:24
  7.9 197.7 %all-reduce.2.cloned.1.call-start = ((), (), s32[]{:S(2)}) async-start(), calls=%async_computation.2 | async-start | bytes 4194304 | tf_op jit(solution)/shard_map/psum | solution.py:59
  47.0 3.5 %copy-start.1 = (bf16[1536,128]{1,0:T(8,128)(2,1)S(1)}, bf16[1536,128]{1,0:T(8,128)(2,1)}, u32[]{:S(2)}) copy-start(bf16[1536,128]{1,0:T(8,128)(2,1)} %param.16) | copy-start | bytes 1179652
  62.7 2.6 copy-start.5
  70.5 2.8 %copy-start.4 = (s32[1,8]{1,0:T(1,128)S(1)}, s32[1,8]{1,0:T(1,128)}, u32[]{:S(2)}) copy-start(s32[1,8]{1,0:T(1,128)} %param.13) | copy-start | bytes 100
  70.6 201.1 %reduce-scatter.2.cloned.1.call-start = ((), (), s32[]{:S(2)}) async-start(), calls=%async_computation.3 | async-start | bytes 1179648 | tf_op jit(solution)/shard_map/reduce_scatter | solution.py:63
  75.7 1.7 copy-start.2
  77.5 194.2 %copy-start.3 = (f32[64,64]{1,0:T(8,128)S(1)}, f32[64,64]{1,0:T(8,128)}, u32[]{:S(2)}) copy-start(f32[64,64]{1,0:T(8,128)} %param.19) | copy-start | bytes 49156
Sparse Core Ops, SparseCore 0:
  9.6 19.4 all-gather.1
  70.7 134.8 all-reduce.1
  209.4 62.2 reduce-scatter.1
where the time goes:
time: 280 us
  waiting for transfers between devices  190 us (68%)
  blocking collectives  33.4 us (12%)
  matrix products  28.3 us (10%)
  between operations  13.9 us (5%)
  local copies, waits for them, and re-layouts  13.4 us (5%)
    psum x1, waiting for transfers between devices, per_device(): summed = lax.psum(top_term, ('group', 'leaf'))  125 us
    reduce_scatter x1, waiting for transfers between devices, per_device(): lax.psum_scatter(jnp.einsum('ab,asm->bsm', chosen.astype(jnp.float32), lo...  63.6 us
    all_gather x1, blocking collectives, per_device(): shard_rows = lax.all_gather(low_modes, 'leaf', axis=0, tiled=True)  33.4 us
    dot_general x1, matrix products, per_device(): jnp.dot(leaf_mass, shapes, preferred_element_type=jnp.float32)  7.5 us
  transfers between devices with their start and end apart: 3, of which 2 were waited for; matrix products, arithmetic and copies ran while one was open for 5% of the time, Pallas kernels for 0%

commit v1 on v0

v1 whole, which is shorter than its diff:
```python
import functools

import jax
import jax.numpy as jnp
from jax import lax
from jax.experimental import pallas as pl
from jax.experimental.pallas import tpu as pltpu
from jax.sharding import PartitionSpec as P

BF16, F32 = jnp.bfloat16, jnp.float32
VMEM = pl.BlockSpec(memory_space=pltpu.VMEM)
SMEM = pl.BlockSpec(memory_space=pltpu.SMEM)
ANY = pl.BlockSpec(memory_space=pl.ANY)
HIGHEST = lax.Precision.HIGHEST


def leaf_factors(leaves):
    inner = 2 if (leaves.bit_length() - 1) % 2 else 4
    outer = []
    stride = leaves
    while stride > inner:
        stride //= 4
        outer.append((4, stride))
    return inner, outer


def params(mib):
    return pltpu.CompilerParams(vmem_limit_bytes=mib * 2**20)


def cost(flops, moved):
    return pl.CostEstimate(flops=flops, bytes_accessed=moved, transcendentals=0)


def send_group(x, k):
    return lax.ppermute(x, "group", [(i, i ^ k) for i in range(lax.axis_size("group"))])


def send_leaf(x, k):
    return lax.ppermute(x, "leaf", [(i, i ^ k) for i in range(lax.axis_size("leaf"))])


def send_both(x, kg, kl):
    groups, leaves = lax.axis_size("group"), lax.axis_size("leaf")
    pairs = [(g * leaves + l, (g ^ kg) * leaves + (l ^ kl)) for g in range(groups) for l in range(leaves)]
    return lax.ppermute(x, ("group", "leaf"), pairs)


def gather_leaf(x, steps):
    held = [(x, [0])]
    for fac, stride in steps:
        if len(held) > 4:
            held = [(jnp.concatenate([a for a, _ in held], axis=0), [r for _, rs in held for r in rs])]
        held = held + [
            (send_leaf(a, k * stride), [r ^ (k * stride) for r in rs]) for k in range(1, fac) for a, rs in held
        ]
    return held


def transpose_kernel(c_ref, m_ref, ct_ref, mt_ref):
    ct_ref[...] = c_ref[...].T
    mt_ref[...] = m_ref[...].T


def transposed(coupling, leaf_modes):
    rows, width = coupling.shape
    modes = leaf_modes.shape[1]
    step = 512
    return pl.pallas_call(
        transpose_kernel,
        grid=(rows // step,),
        in_specs=[pl.BlockSpec((step, width), lambda i: (i, 0)), pl.BlockSpec((step, modes), lambda i: (i, 0))],
        out_specs=[pl.BlockSpec((width, step), lambda i: (0, i)), pl.BlockSpec((modes, step), lambda i: (0, i))],
        out_shape=[jax.ShapeDtypeStruct((width, rows), BF16), jax.ShapeDtypeStruct((modes, rows), BF16)],
        compiler_params=params(24),
        cost_estimate=cost(0, 4 * rows * (width + modes)),
    )(coupling, leaf_modes)


def main_kernel(
    n_top, low_rels, inner, anc_top, anc_low, *refs
):
    n_low = len(low_rels)
    tops, lows = refs[:n_top], refs[n_top : n_top + n_low]
    coupling, mass, modes, coef, ct = refs[n_top + n_low : n_top + n_low + 5]
    send, keep, weighted = refs[n_top + n_low + 5 : n_top + n_low + 8]
    top_v, low_v, c_v, mass_v, modes_v, coef_v, ct_v, stacked, shapes, sem, sem_c, sem_m, sem_t = refs[
        n_top + n_low + 8 :
    ]
    sr = top_v.shape[1]
    per_group = top_v.shape[0] // n_top
    top_slots, low_slots = anc_top.shape[1], anc_low.shape[1]
    group, leaf = lax.axis_index("group"), lax.axis_index("leaf")
    rows = mass.shape[0]
    step = 512
    steps = rows // step

    first = []
    for i, t in enumerate(tops):
        for b in range(per_group):
            first.append((t.at[pl.ds(b * sr, sr)], top_v.at[i * per_group + b]))
    for a, rels in zip(lows, low_rels):
        for p, r in enumerate(rels):
            first.append((a.at[pl.ds(p * sr, sr)], low_v.at[r]))
    first.append((modes, modes_v))
    first.append((coef, coef_v))
    first = [pltpu.make_async_copy(s, d, sem.at[i]) for i, (s, d) in enumerate(first)]
    for c in first:
        c.start()
    c_copies = [
        pltpu.make_async_copy(coupling.at[pl.ds(i * step, step)], c_v.at[pl.ds(i * step, step)], sem_c.at[i])
        for i in range(steps)
    ]
    for c in c_copies:
        c.start()
    m_copies = [
        pltpu.make_async_copy(mass.at[pl.ds(i * step, step)], mass_v.at[pl.ds(i * step, step)], sem_m.at[i])
        for i in range(steps)
    ]
    for c in m_copies:
        c.start()
    t_copy = pltpu.make_async_copy(ct.at[pl.ds(0, top_slots * sr)], ct_v, sem_t)
    t_copy.start()
    send[...] = jnp.zeros(send.shape, send.dtype)
    keep[...] = jnp.zeros(keep.shape, keep.dtype)
    for c in first:
        c.wait()
    for j in range(top_slots):
        b = anc_top[0, j]
        owner = b // per_group
        stacked[pl.ds(j * sr, sr), :] = top_v[(owner ^ group) * per_group + b % per_group]
    for j in range(low_slots):
        stacked[pl.ds((top_slots + j) * sr, sr), :] = low_v[anc_low[0, j] ^ leaf]
    for i in range(steps):
        c_copies[i].wait()
        for h in range(2):
            at = pl.ds(i * step + h * (step // 2), step // 2)
            shapes[at, :] = (
                jnp.dot(modes_v[at, :], coef_v[...], preferred_element_type=F32)
                - jnp.dot(c_v[at, :], stacked[...], preferred_element_type=F32)
            ).astype(BF16)
    for i in range(steps):
        m_copies[i].wait()
        for h in range(2):
            at = pl.ds(i * step + h * (step // 2), step // 2)
            weighted[at, :] = jnp.dot(mass_v[at, :], shapes[...], preferred_element_type=F32).astype(BF16)
    t_copy.wait()
    core, far = group & 1, group >> 1
    width = weighted.shape[1] // inner
    for q in range(inner):
        col = pl.multiple_of(((leaf & (inner - 1)) ^ q) * width, 128)
        for h in range(2):
            half = top_slots // 2
            loads = jnp.dot(
                ct_v[pl.ds(h * half * sr, half * sr), :], weighted[:, pl.ds(col, width)], preferred_element_type=F32
            )
            for j in range(half):
                b = anc_top[0, h * half + j]
                owner = b // per_group
                at = pl.ds(pl.multiple_of((((owner >> 1) ^ far) * per_group + b % per_group) * sr, sr), sr)
                block = loads[j * sr : (j + 1) * sr]

                @pl.when((owner & 1) == core)
                def _():
                    keep[at, q * width : (q + 1) * width] = block

                @pl.when((owner & 1) != core)
                def _():
                    send[at, q * width : (q + 1) * width] = block.astype(BF16)


def main_call(anc_top, anc_low, tops, lows, low_rels, coupling, mass, modes, coef, ct, inner, sr, leaves):
    rows, sw = coupling.shape
    m = coef.shape[1]
    groups = len(tops)
    per_group = tops[0].shape[0] // sr
    half_rows = groups * per_group * sr // 2
    top_rows = anc_top.shape[1] * sr
    n_first = groups * per_group + leaves + 2
    flops = 2 * m * rows * (sw + rows + modes.shape[1] + top_rows)
    return pl.pallas_call(
        functools.partial(main_kernel, groups, low_rels, inner),
        in_specs=[SMEM, SMEM] + [ANY] * (groups + len(lows) + 5),
        out_specs=[VMEM, VMEM, VMEM],
        out_shape=[
            jax.ShapeDtypeStruct((half_rows, m), BF16),
            jax.ShapeDtypeStruct((half_rows, m), F32),
            jax.ShapeDtypeStruct((rows, m), BF16),
        ],
        scratch_shapes=[
            pltpu.VMEM((groups * per_group, sr, m), BF16),
            pltpu.VMEM((leaves, sr, m), BF16),
            pltpu.VMEM((rows, sw), BF16),
            pltpu.VMEM((rows, rows), BF16),
            pltpu.VMEM(modes.shape, BF16),
            pltpu.VMEM(coef.shape, BF16),
            pltpu.VMEM((top_rows, rows), BF16),
            pltpu.VMEM((sw, m), BF16),
            pltpu.VMEM((rows, m), BF16),
            pltpu.SemaphoreType.DMA((n_first,)),
            pltpu.SemaphoreType.DMA((rows // 512,)),
            pltpu.SemaphoreType.DMA((rows // 512,)),
            pltpu.SemaphoreType.DMA,
        ],
        compiler_params=params(40),
        cost_estimate=cost(flops, 2 * rows * (sw + rows)),
    )(anc_top, anc_low, *tops, *lows, coupling, mass, modes, coef, ct)


def low_kernel(inner, anc_low, ct, mt, weighted, proj, keep, *sends):
    slots = anc_low.shape[1]
    sr = ct.shape[0] // slots
    leaf = lax.axis_index("leaf")
    keep[...] = jnp.zeros(keep.shape, keep.dtype)
    for s in sends:
        s[...] = jnp.zeros(s.shape, s.dtype)
    part = 4
    for h in range(slots // part):
        loads = jnp.dot(ct[pl.ds(h * part * sr, part * sr), :], weighted[...], preferred_element_type=F32)
        for j in range(part):
            k = anc_low[0, h * part + j]
            at = pl.ds(pl.multiple_of((k // inner) * sr, sr), sr)
            turn = (k ^ leaf) & (inner - 1)
            block = loads[j * sr : (j + 1) * sr]

            @pl.when(turn == 0)
            def _():
                keep[at, :] = block

            for q, s in enumerate(sends):

                @pl.when(turn == q + 1)
                def _(s=s):
                    s[at, :] = block.astype(BF16)

    proj[...] = jnp.dot(mt[...], weighted[...], preferred_element_type=F32).astype(BF16)


def low_call(anc_low, ct, mt, weighted, inner, sr, leaves):
    rows, m = weighted.shape
    slots = anc_low.shape[1]
    skip = ct.shape[0] // (slots * sr) - 1
    assert ct.shape[0] % (slots * sr) == 0 or True
    kept = leaves // inner * sr
    low_rows = slots * sr
    at = (ct.shape[0] - low_rows) // sr
    del skip
    return pl.pallas_call(
        functools.partial(low_kernel, inner),
        grid=(1,),
        in_specs=[
            SMEM,
            pl.BlockSpec((pl.Element(low_rows), pl.Element(rows)), lambda i: (at * sr, 0)),
            VMEM,
            VMEM,
        ],
        out_specs=[VMEM] * (1 + inner),
        out_shape=[jax.ShapeDtypeStruct((mt.shape[0], m), BF16), jax.ShapeDtypeStruct((kept, m), F32)]
        + [jax.ShapeDtypeStruct((kept, m), BF16)] * (inner - 1),
        compiler_params=params(40),
        cost_estimate=cost(2 * m * rows * (low_rows + mt.shape[0]), 2 * rows * (low_rows + m)),
    )(anc_low, ct, mt, weighted)


def cross_kernel(inner, keep, got, own, *sends):
    rows, width = own.shape
    n = 0
    for far in range(keep.shape[0] // rows):
        for q in range(inner):
            at = (slice(far * rows, (far + 1) * rows), slice(q * width, (q + 1) * width))
            total = keep[at] + got[at].astype(F32)
            if far == 0 and q == 0:
                own[...] = total
            else:
                sends[n][...] = total.astype(BF16)
                n += 1


def cross_call(keep, got, inner):
    rows, width = keep.shape[0] // 2, keep.shape[1] // inner
    return pl.pallas_call(
        functools.partial(cross_kernel, inner),
        in_specs=[VMEM, VMEM],
        out_specs=[VMEM] * (2 * inner),
        out_shape=[jax.ShapeDtypeStruct((rows, width), F32)]
        + [jax.ShapeDtypeStruct((rows, width), BF16)] * (2 * inner - 1),
        compiler_params=params(16),
        cost_estimate=cost(keep.size, 8 * keep.size),
    )(keep, got)


def split_kernel(fac, stride, n_got, keep, *refs):
    got, own, sends = refs[:n_got], refs[n_got], refs[n_got + 1 :]
    rows = own.shape[0]
    digit = (lax.axis_index("leaf") // stride) & (fac - 1)
    for d in range(fac):
        at = pl.ds(pl.multiple_of((digit ^ d) * rows, rows), rows)
        total = keep[at, :]
        for g in got:
            total += g[at, :].astype(F32)
        if d == 0:
            own[...] = total
        else:
            sends[d - 1][...] = total.astype(BF16)


def split_call(keep, got, fac, stride):
    rows = keep.shape[0] // fac
    return pl.pallas_call(
        functools.partial(split_kernel, fac, stride, len(got)),
        in_specs=[VMEM] * (1 + len(got)),
        out_specs=[VMEM] * fac,
        out_shape=[jax.ShapeDtypeStruct((rows, keep.shape[1]), F32)]
        + [jax.ShapeDtypeStruct((rows, keep.shape[1]), BF16)] * (fac - 1),
        compiler_params=params(16),
        cost_estimate=cost(keep.size, 8 * keep.size),
    )(keep, *got)


def add_kernel(keep, *refs):
    total = keep[...]
    for g in refs[:-1]:
        total += g[...].astype(F32)
    refs[-1][...] = total.astype(BF16)


def add_call(keep, got):
    return pl.pallas_call(
        add_kernel,
        in_specs=[VMEM] * (1 + len(got)),
        out_specs=VMEM,
        out_shape=jax.ShapeDtypeStruct(keep.shape, BF16),
        compiler_params=params(16),
        cost_estimate=cost(keep.size, 8 * keep.size),
    )(keep, *got)


def low_end_kernel(keep, *refs):
    got, kinv, out = refs[:-2], refs[-2], refs[-1]
    total = keep[...]
    for g in got:
        total += g[...].astype(F32)
    out[...] = jnp.dot(kinv[...], total, preferred_element_type=F32, precision=HIGHEST)


def low_end_call(keep, got, kinv):
    return pl.pallas_call(
        low_end_kernel,
        in_specs=[VMEM] * (2 + len(got)),
        out_specs=VMEM,
        out_shape=jax.ShapeDtypeStruct(keep.shape, F32),
        compiler_params=params(16),
        cost_estimate=cost(12 * keep.size * 64, 8 * keep.size),
    )(keep, *got, kinv)


def top_end_kernel(rels, inner, outer, kinv, *refs):
    parts, out, loads = refs[:-2], refs[-2], refs[-1]
    leaf = lax.axis_index("leaf")
    rows, m = out.shape
    sr = kinv.shape[1]
    width = m // inner
    for part, rs in zip(parts, rels):
        size = part.shape[0] // len(rs)
        for p, r in enumerate(rs):
            there = leaf ^ r
            row, left = 0, rows
            for fac, stride in outer:
                left //= fac
                row += ((there // stride) & (fac - 1)) * left
            loads[
                pl.ds(pl.multiple_of(row, size), size), pl.ds(pl.multiple_of((there & (inner - 1)) * width, 128), width)
            ] = part[p * size : (p + 1) * size, :]
    for b in range(rows // sr):
        at = slice(b * sr, (b + 1) * sr)
        out[at, :] = jnp.dot(kinv[at, :], loads[at, :].astype(F32), preferred_element_type=F32, precision=HIGHEST)


def top_end_call(held, kinv, m, inner, outer):
    rows = kinv.shape[0]
    return pl.pallas_call(
        functools.partial(top_end_kernel, [r for _, r in held], inner, outer),
        in_specs=[VMEM] * (1 + len(held)),
        out_specs=VMEM,
        out_shape=jax.ShapeDtypeStruct((rows, m), F32),
        scratch_shapes=[pltpu.VMEM((rows, m), BF16)],
        compiler_params=params(16),
        cost_estimate=cost(12 * rows * m * 64, 8 * rows * m),
    )(kinv, *[a for a, _ in held])


def per_device(
    top_modes, low_modes, anc_top, anc_low, coupling, leaf_mass, leaf_modes, leaf_coef, kinv_top, kinv_low
):
    sr = kinv_low.shape[1]
    m = low_modes.shape[1]
    leaves = lax.axis_size("leaf")
    inner, outer = leaf_factors(leaves)
    far_top = send_group(top_modes, 2)
    tops = [top_modes, send_group(top_modes, 1), far_top, send_group(far_top, 1)]
    held = gather_leaf(low_modes, outer + [(inner, 1)])
    ct, mt = transposed(coupling, leaf_modes)
    send, keep, weighted = main_call(
        anc_top,
        anc_low,
        tops,
        [a for a, _ in held],
        [r for _, r in held],
        coupling,
        leaf_mass,
        leaf_modes,
        leaf_coef,
        ct,
        inner,
        sr,
        leaves,
    )
    got = send_group(send, 1)
    leaf_proj, low_keep, *low_sends = low_call(anc_low, ct, mt, weighted, inner, sr, leaves)
    low_got = [send_leaf(s, q + 1) for q, s in enumerate(low_sends)]
    own, *sends = cross_call(keep, got, inner)
    pairs = [(far, q) for far in range(2) for q in range(inner)][1:]
    got = [send_both(s, 2 * far, q) for s, (far, q) in zip(sends, pairs)]
    for fac, stride in outer:
        low_keep, *low_sends = split_call(low_keep, low_got, fac, stride)
        low_got = [send_leaf(s, (d + 1) * stride) for d, s in enumerate(low_sends)]
    for fac, stride in outer:
        own, *sends = split_call(own, got, fac, stride)
        got = [send_leaf(s, (d + 1) * stride) for d, s in enumerate(sends)]
    new_low = low_end_call(low_keep, low_got, kinv_low)
    top_held = gather_leaf(add_call(own, got), outer[::-1] + [(inner, 1)])
    new_top = top_end_call(top_held, kinv_top, m, inner, outer)
    return (new_top, new_low, leaf_proj)


def solution(mesh):
    both = P(("group", "leaf"), None)
    return jax.shard_map(
        per_device,
        mesh=mesh,
        in_specs=(P("group", None), both, both, both, both, both, both, both, P("group", None), both),
        out_specs=(P("group", None), both, both),
        check_vma=False,
    )
```

time: 280 us -> 83.2 us (0.30)
  waiting for transfers between devices: 190 us -> 21.1 us
  starting transfers between devices: 0.3 us -> 36 us
  blocking collectives: 33.4 us -> 0 us
  matrix products: 28.3 us -> 0 us
  Pallas kernels: 0 us -> 18.8 us
  between operations: 13.9 us -> 0.79 us
  local copies, waits for them, and re-layouts: 13.4 us -> 6.27 us
    psum x1 -> x0, waiting for transfers between devices: 125 us -> none  [per_device(): summed = lax.psum(top_term, ('group', 'leaf'))]
    reduce_scatter x1 -> x0, waiting for transfers between devices: 63.6 us -> none  [per_device(): lax.psum_scatter(jnp.einsum('ab,asm->bsm', chosen.astype(jnp.float32), lo...]
    ppermute x0 -> x28, starting transfers between devices: none -> 36 us  [the longest x21 29.4 us: send_leaf(): lax.ppermute(x, 'leaf', [(i, i ^ k) for i in range(lax.axis_size('leaf'))])]
    all_gather x1 -> x0, blocking collectives: 33.4 us -> none  [per_device(): shard_rows = lax.all_gather(low_modes, 'leaf', axis=0, tiled=True)]
    dot_general x10 -> x0, matrix products: 28.3 us -> none  [the longest x1 7.5 us: per_device(): jnp.dot(leaf_mass, shapes, preferred_element_type=jnp.float32)]
    ppermute x0 -> x28, waiting for transfers between devices: none -> 21.1 us  [the longest x21 13.5 us: send_leaf(): lax.ppermute(x, 'leaf', [(i, i ^ k) for i in range(lax.axis_size('leaf'))])]
    pallas_call x0 -> x9, Pallas kernels: none -> 18.8 us  [the longest x1 12.1 us: main_call(): pl.pallas_call(functools.partial(main_kernel, groups, low_rels, inner), i...]
    slice x3 -> x0, local copies, waits for them, and re-layouts: 6.69 us -> none  [the longest x2 4.09 us: per_device(): loads[top_slots * sep_rows:].reshape(low_slots, sep_rows, mode_count)]
  transfers between devices with their start and end apart: 3 -> 28, of which waited for: 2 -> 9; matrix products, arithmetic and copies ran while one was open for 5% -> 0% of each run, Pallas kernels for 0% -> 6%
where the time goes in v1:
time: 83.2 us; the launch traced here: 82.9 us
  starting transfers between devices  36 us (43%)
  waiting for transfers between devices  21.1 us (25%)
  Pallas kernels  18.8 us (23%)
  local copies, waits for them, and re-layouts  6.27 us (8%)
    ppermute x21, starting transfers between devices, send_leaf(): lax.ppermute(x, 'leaf', [(i, i ^ k) for i in range(lax.axis_size('leaf'))])  29.4 us
    ppermute x21, waiting for transfers between devices, send_leaf(): lax.ppermute(x, 'leaf', [(i, i ^ k) for i in range(lax.axis_size('leaf'))])  13.5 us
    pallas_call x1, Pallas kernels, main_call(): pl.pallas_call(functools.partial(main_kernel, groups, low_rels, inner), i...  12.1 us
    ppermute x4, waiting for transfers between devices, send_group(): lax.ppermute(x, 'group', [(i, i ^ k) for i in range(lax.axis_size('group'...  6.52 us
    unnamed x23, local copies, waits for them, and re-layouts  6.27 us
    ppermute x3, starting transfers between devices, send_both(): return lax.ppermute(x, ('group', 'leaf'), pairs)  3.55 us
    ppermute x4, starting transfers between devices, send_group(): lax.ppermute(x, 'group', [(i, i ^ k) for i in range(lax.axis_size('group'...  3.08 us
    pallas_call x1, Pallas kernels, low_call(): pl.pallas_call(functools.partial(low_kernel, inner), grid=(1,), in_specs=...  2.86 us
  transfers between devices with their start and end apart: 28, of which 9 were waited for; matrix products, arithmetic and copies ran while one was open for 0% of the time, Pallas kernels for 6%

profile of v1, /device:TPU:0, one launch (start us, length us, event | category | flops | bytes accessed | tf_op | source)
XLA Modules:
  0.0 82.9 jit_solution(13194590838560976948)
XLA Ops:
  0.6 3.0 %collective-permute-start.1 = (bf16[256,512]{1,0:T(8,128)(2,1)}, bf16[256,512]{1,0:T(8,128)(2,1)S(1)}, u32[]{:S(2)}, u32[]{:S(2)}) collective-permute-start(bf16[256,512]{1,0:T(8,128)(2,1)} %refs_0_.1), channel_id=1, source_target_pairs={{0,16},{8,24},{16,0},{24,8},{1,17},{9,25},{17,1},{25,9},{2,18},{10... | collective-permute-start | bytes 786440 | tf_op jit(solution)/shard_map/ppermute | solution.py:36
  3.6 6.5 %collective-permute-done.1.refs_2_ = bf16[256,512]{1,0:T(8,128)(2,1)S(1)} collective-permute-done((bf16[256,512]{1,0:T(8,128)(2,1)}, bf16[256,512]{1,0:T(8,128)(2,1)S(1)}, u32[]{:S(2)}, u32[]{:S(2)}) %collective-permute-start.1) | collective-permute-done | bytes 262176 | tf_op jit(solution)/shard_map/ppermute | solution.py:36
  10.2 1.8 %collective-permute-start.3 = (bf16[64,512]{1,0:T(8,128)(2,1)}, bf16[64,512]{1,0:T(8,128)(2,1)S(1)}, u32[]{:S(2)}, u32[]{:S(2)}) collective-permute-start(bf16[64,512]{1,0:T(8,128)(2,1)} %refs_4_.1), channel_id=1, source_target_pairs={{0,2},{1,3},{2,0},{3,1},{4,6},{5,7},{6,4},{7,5},{8,10},{9,11},{10,... | collective-permute-start | bytes 196616 | tf_op jit(solution)/shard_map/ppermute | solution.py:40
  12.0 2.6 %collective-permute-start.4 = (bf16[64,512]{1,0:T(8,128)(2,1)}, bf16[64,512]{1,0:T(8,128)(2,1)S(1)}, u32[]{:S(2)}, u32[]{:S(2)}) collective-permute-start(bf16[64,512]{1,0:T(8,128)(2,1)} %refs_4_.1), channel_id=1, source_target_pairs={{0,4},{1,5},{2,6},{3,7},{4,0},{5,1},{6,2},{7,3},{8,12},{9,13},{10,... | collective-permute-start | bytes 196616 | tf_op jit(solution)/shard_map/ppermute | solution.py:40
  15.0 1.7 %collective-permute-start.6 = (bf16[64,512]{1,0:T(8,128)(2,1)}, bf16[64,512]{1,0:T(8,128)(2,1)S(1)}, u32[]{:S(2)}, u32[]{:S(2)}) collective-permute-start(bf16[64,512]{1,0:T(8,128)(2,1)} %refs_4_.1), channel_id=1, source_target_pairs={{0,1},{1,0},{2,3},{3,2},{4,5},{5,4},{6,7},{7,6},{8,9},{9,8},{10,11... | collective-permute-start | bytes 196616 | tf_op jit(solution)/shard_map/ppermute | solution.py:40
  16.6 2.5 %collective-permute-done.4.refs_6_ = bf16[64,512]{1,0:T(8,128)(2,1)S(1)} collective-permute-done((bf16[64,512]{1,0:T(8,128)(2,1)}, bf16[64,512]{1,0:T(8,128)(2,1)S(1)}, u32[]{:S(2)}, u32[]{:S(2)}) %collective-permute-start.4) | collective-permute-done | bytes 65568 | tf_op jit(solution)/shard_map/ppermute | solution.py:40
  19.1 1.5 %collective-permute-start.7 = (bf16[64,512]{1,0:T(8,128)(2,1)S(1)}, bf16[64,512]{1,0:T(8,128)(2,1)S(1)}, u32[]{:S(2)}, u32[]{:S(2)}) collective-permute-start(bf16[64,512]{1,0:T(8,128)(2,1)S(1)} %collective-permute-done.3.refs_5_), channel_id=1, source_target_pairs={{0,1},{1,0},{2,3},{3,2},{4,5},{5,4},{6,7},{7,6},{8,9},{9,8},{10,11... | collective-permute-start | bytes 196616 | tf_op jit(solution)/shard_map/ppermute | solution.py:40
  20.9 1.5 %collective-permute-start.8 = (bf16[64,512]{1,0:T(8,128)(2,1)S(1)}, bf16[64,512]{1,0:T(8,128)(2,1)S(1)}, u32[]{:S(2)}, u32[]{:S(2)}) collective-permute-start(bf16[64,512]{1,0:T(8,128)(2,1)S(1)} %collective-permute-done.4.refs_6_), channel_id=1, source_target_pairs={{0,1},{1,0},{2,3},{3,2},{4,5},{5,4},{6,7},{7,6},{8,9},{9,8},{10,11... | collective-permute-start | bytes 196616 | tf_op jit(solution)/shard_map/ppermute | solution.py:40
  22.9 1.9 %copy-done = bf16[1536,1024]{1,0:T(8,128)(2,1)S(1)} copy-done((bf16[1536,1024]{1,0:T(8,128)(2,1)S(1)}, bf16[1536,1024]{1,0:T(8,128)(2,1)}, u32[]{:S(2)}) %copy-start) | copy-done | bytes 3145752
  25.8 1.3 %shard_map.121 = (bf16[1024,1536]{1,0:T(8,128)(2,1)S(1)}, bf16[128,1536]{1,0:T(8,128)(2,1)S(1)}) custom-call(bf16[1536,1024]{1,0:T(8,128)(2,1)S(1)} %copy-done, bf16[1536,128]{1,0:T(8,128)(2,1)S(1)} %copy-done.2), custom_call_target="tpu_custom_call" | custom-call | bytes 7077888 | tf_op jit(solution)/shard_map/pallas_call | solution.py:69
  30.5 12.1 %shard_map.122 = (bf16[512,512]{1,0:T(8,128)(2,1)S(1)}, f32[512,512]{1,0:T(8,128)S(1)}, bf16[1536,512]{1,0:T(8,128)(2,1)S(1)}) custom-call(s32[1,8]{1,0:T(1,128)S(1)} %copy-done.9, s32[1,8]{1,0:T(1,128)S(1)} %copy-done.5, bf16[256,512]{1,0:T(8,128)(2,1)S(1)} %copy-done.6, bf16[256,512]{1,0:T(8,128)(2,1)S(1)} %collective-permute-done.refs_1_, ...), custom_call_target="tpu_custom_call" | custom-call | flops 5033164800 | bytes 7864320 | tf_op jit(solution)/shard_map/pallas_call | solution.py:181
  42.6 2.9 %shard_map.127 = (bf16[128,512]{1,0:T(8,128)(2,1)}, f32[256,512]{1,0:T(8,128)S(1)}, bf16[256,512]{1,0:T(8,128)(2,1)S(1)}) custom-call(s32[1,8]{1,0:T(1,128)S(1)} %copy-done.5, bf16[1024,1536]{1,0:T(8,128)(2,1)S(1)} %get-tuple-element.23.refs_16_.ct, bf16[128,1536]{1,0:T(8,128)(2,1)S(1)} %get-tuple-element.34.mt, bf16[1536,512]{1,0:T(8,128)(2,1)S(1)} %get-tuple-element.35.weighted), custom_call_target="tpu_custom_call" | custom-call | flops 1006632960 | bytes 3145728 | tf_op jit(solution)/shard_map/pallas_call | solution.py:248
  45.5 1.5 %collective-permute-start.24 = (bf16[256,512]{1,0:T(8,128)(2,1)S(1)}, bf16[256,512]{1,0:T(8,128)(2,1)S(1)}, u32[]{:S(2)}, u32[]{:S(2)}) collective-permute-start(bf16[256,512]{1,0:T(8,128)(2,1)S(1)} %get-tuple-element.37), channel_id=1, source_target_pairs={{0,1},{1,0},{2,3},{3,2},{4,5},{5,4},{6,7},{7,6},{8,9},{9,8},{10,11... | collective-permute-start | bytes 786440 | tf_op jit(solution)/shard_map/ppermute | solution.py:40
  47.7 1.5 %collective-permute-start.12 = (bf16[256,256]{1,0:T(8,128)(2,1)S(1)}, bf16[256,256]{1,0:T(8,128)(2,1)S(1)}, u32[]{:S(2)}, u32[]{:S(2)}) collective-permute-start(bf16[256,256]{1,0:T(8,128)(2,1)S(1)} %get-tuple-element.28), channel_id=1, source_target_pairs={{0,16},{1,17},{2,18},{3,19},{4,20},{5,21},{6,22},{7,23},{8,24},{9,... | collective-permute-start | bytes 393224 | tf_op jit(solution)/shard_map/ppermute | solution.py:46
  49.1 1.5 %collective-permute-start.13 = (bf16[256,256]{1,0:T(8,128)(2,1)S(1)}, bf16[256,256]{1,0:T(8,128)(2,1)S(1)}, u32[]{:S(2)}, u32[]{:S(2)}) collective-permute-start(bf16[256,256]{1,0:T(8,128)(2,1)S(1)} %get-tuple-element.29), channel_id=1, source_target_pairs={{0,17},{1,16},{2,19},{3,18},{4,21},{5,20},{6,23},{7,22},{8,25},{9,... | collective-permute-start | bytes 393224 | tf_op jit(solution)/shard_map/ppermute | solution.py:46
  50.7 6.7 %collective-permute-done.24.refs_0_ = bf16[256,512]{1,0:T(8,128)(2,1)S(1)} collective-permute-done((bf16[256,512]{1,0:T(8,128)(2,1)S(1)}, bf16[256,512]{1,0:T(8,128)(2,1)S(1)}, u32[]{:S(2)}, u32[]{:S(2)}) %collective-permute-start.24) | collective-permute-done | bytes 262176 | tf_op jit(solution)/shard_map/ppermute | solution.py:40
  57.5 1.3 %collective-permute-start.25 = (bf16[64,512]{1,0:T(8,128)(2,1)S(1)}, bf16[64,512]{1,0:T(8,128)(2,1)S(1)}, u32[]{:S(2)}, u32[]{:S(2)}) collective-permute-start(bf16[64,512]{1,0:T(8,128)(2,1)S(1)} %get-tuple-element.39), channel_id=1, source_target_pairs={{0,2},{1,3},{2,0},{3,1},{4,6},{5,7},{6,4},{7,5},{8,10},{9,11},{10,... | collective-permute-start | bytes 196616 | tf_op jit(solution)/shard_map/ppermute | solution.py:40
  59.9 1.3 %collective-permute-start.14 = (bf16[64,256]{1,0:T(8,128)(2,1)S(1)}, bf16[64,256]{1,0:T(8,128)(2,1)S(1)}, u32[]{:S(2)}, u32[]{:S(2)}) collective-permute-start(bf16[64,256]{1,0:T(8,128)(2,1)S(1)} %get-tuple-element.31), channel_id=1, source_target_pairs={{0,2},{1,3},{2,0},{3,1},{4,6},{5,7},{6,4},{7,5},{8,10},{9,11},{10,... | collective-permute-start | bytes 98312 | tf_op jit(solution)/shard_map/ppermute | solution.py:40
  61.2 3.2 %collective-permute-start.15 = (bf16[64,256]{1,0:T(8,128)(2,1)S(1)}, bf16[64,256]{1,0:T(8,128)(2,1)S(1)}, u32[]{:S(2)}, u32[]{:S(2)}) collective-permute-start(bf16[64,256]{1,0:T(8,128)(2,1)S(1)} %get-tuple-element.32), channel_id=1, source_target_pairs={{0,4},{1,5},{2,6},{3,7},{4,0},{5,1},{6,2},{7,3},{8,12},{9,13},{10,... | collective-permute-start | bytes 98312 | tf_op jit(solution)/shard_map/ppermute | solution.py:40
  64.4 1.5 %collective-permute-start.26 = (bf16[64,512]{1,0:T(8,128)(2,1)S(1)}, bf16[64,512]{1,0:T(8,128)(2,1)S(1)}, u32[]{:S(2)}, u32[]{:S(2)}) collective-permute-start(bf16[64,512]{1,0:T(8,128)(2,1)S(1)} %get-tuple-element.40), channel_id=1, source_target_pairs={{0,4},{1,5},{2,6},{3,7},{4,0},{5,1},{6,2},{7,3},{8,12},{9,13},{10,... | collective-permute-start | bytes 196616 | tf_op jit(solution)/shard_map/ppermute | solution.py:40
  65.9 2.3 %collective-permute-start.27 = (bf16[64,512]{1,0:T(8,128)(2,1)S(1)}, bf16[64,512]{1,0:T(8,128)(2,1)S(1)}, u32[]{:S(2)}, u32[]{:S(2)}) collective-permute-start(bf16[64,512]{1,0:T(8,128)(2,1)S(1)} %get-tuple-element.41), channel_id=1, source_target_pairs={{0,6},{1,7},{2,4},{3,5},{4,2},{5,3},{6,0},{7,1},{8,14},{9,15},{10,... | collective-permute-start | bytes 196616 | tf_op jit(solution)/shard_map/ppermute | solution.py:40
  68.3 2.0 %collective-permute-done.16.refs_2_ = bf16[64,256]{1,0:T(8,128)(2,1)S(1)} collective-permute-done((bf16[64,256]{1,0:T(8,128)(2,1)S(1)}, bf16[64,256]{1,0:T(8,128)(2,1)S(1)}, u32[]{:S(2)}, u32[]{:S(2)}) %collective-permute-start.16) | collective-permute-done | bytes 32800 | tf_op jit(solution)/shard_map/ppermute | solution.py:40
  71.6 3.1 %collective-permute-start.19 = (bf16[64,256]{1,0:T(8,128)(2,1)S(1)}, bf16[64,256]{1,0:T(8,128)(2,1)S(1)}, u32[]{:S(2)}, u32[]{:S(2)}) collective-permute-start(bf16[64,256]{1,0:T(8,128)(2,1)S(1)} %shard_map.125.refs_0_), channel_id=1, source_target_pairs={{0,6},{1,7},{2,4},{3,5},{4,2},{5,3},{6,0},{7,1},{8,14},{9,15},{10,... | collective-permute-start | bytes 98312 | tf_op jit(solution)/shard_map/ppermute | solution.py:40
  81.5 1.4 %shard_map.126 = f32[256,512]{1,0:T(8,128)} custom-call(f32[256,64]{1,0:T(8,128)S(1)} %copy.13.kinv, bf16[64,256]{1,0:T(8,128)(2,1)S(1)} %shard_map.125.refs_0_, bf16[64,256]{1,0:T(8,128)(2,1)S(1)} %collective-permute-done.17.refs_1_, bf16[64,256]{1,0:T(8,128)(2,1)S(1)} %collective-permute-done.18.refs_2_, ...), custom_call_target="tpu_custom_call" | custom-call | flops 100663296 | bytes 1048576 | tf_op jit(solution)/shard_map/pallas_call | solution.py:381
  (64 shorter events, 15.5 us)
Async XLA Ops:
  0.6 9.5 %collective-permute-start.1 = (bf16[256,512]{1,0:T(8,128)(2,1)}, bf16[256,512]{1,0:T(8,128)(2,1)S(1)}, u32[]{:S(2)}, u32[]{:S(2)}) collective-permute-start(bf16[256,512]{1,0:T(8,128)(2,1)} %refs_0_.1), channel_id=1, source_target_pairs={{0,16},{8,24},{16,0},{24,8},{1,17},{9,25},{17,1},{25,9},{2,18},{10... | collective-permute-start | bytes 786440 | tf_op jit(solution)/shard_map/ppermute | solution.py:36
  3.6 23.5 %collective-permute-start = (bf16[256,512]{1,0:T(8,128)(2,1)}, bf16[256,512]{1,0:T(8,128)(2,1)S(1)}, u32[]{:S(2)}, u32[]{:S(2)}) collective-permute-start(bf16[256,512]{1,0:T(8,128)(2,1)} %refs_0_.1), channel_id=1, source_target_pairs={{0,8},{8,0},{16,24},{24,16},{1,9},{9,1},{17,25},{25,17},{2,10},{10... | collective-permute-start | bytes 786440 | tf_op jit(solution)/shard_map/ppermute | solution.py:36
  10.2 17.0 %collective-permute-start.2 = (bf16[256,512]{1,0:T(8,128)(2,1)S(1)}, bf16[256,512]{1,0:T(8,128)(2,1)S(1)}, u32[]{:S(2)}, u32[]{:S(2)}) collective-permute-start(bf16[256,512]{1,0:T(8,128)(2,1)S(1)} %collective-permute-done.1.refs_2_), channel_id=1, source_target_pairs={{0,8},{8,0},{16,24},{24,16},{1,9},{9,1},{17,25},{25,17},{2,10},{10... | collective-permute-start | bytes 786440 | tf_op jit(solution)/shard_map/ppermute | solution.py:36
  10.2 4.8 %collective-permute-start.3 = (bf16[64,512]{1,0:T(8,128)(2,1)}, bf16[64,512]{1,0:T(8,128)(2,1)S(1)}, u32[]{:S(2)}, u32[]{:S(2)}) collective-permute-start(bf16[64,512]{1,0:T(8,128)(2,1)} %refs_4_.1), channel_id=1, source_target_pairs={{0,2},{1,3},{2,0},{3,1},{4,6},{5,7},{6,4},{7,5},{8,10},{9,11},{10,... | collective-permute-start | bytes 196616 | tf_op jit(solution)/shard_map/ppermute | solution.py:40
  12.0 7.2 %collective-permute-start.4 = (bf16[64,512]{1,0:T(8,128)(2,1)}, bf16[64,512]{1,0:T(8,128)(2,1)S(1)}, u32[]{:S(2)}, u32[]{:S(2)}) collective-permute-start(bf16[64,512]{1,0:T(8,128)(2,1)} %refs_4_.1), channel_id=1, source_target_pairs={{0,4},{1,5},{2,6},{3,7},{4,0},{5,1},{6,2},{7,3},{8,12},{9,13},{10,... | collective-permute-start | bytes 196616 | tf_op jit(solution)/shard_map/ppermute | solution.py:40
  14.6 6.3 %collective-permute-start.5 = (bf16[64,512]{1,0:T(8,128)(2,1)}, bf16[64,512]{1,0:T(8,128)(2,1)S(1)}, u32[]{:S(2)}, u32[]{:S(2)}) collective-permute-start(bf16[64,512]{1,0:T(8,128)(2,1)} %refs_4_.1), channel_id=1, source_target_pairs={{0,6},{1,7},{2,4},{3,5},{4,2},{5,3},{6,0},{7,1},{8,14},{9,15},{10,... | collective-permute-start | bytes 196616 | tf_op jit(solution)/shard_map/ppermute | solution.py:40
  15.0 7.5 %collective-permute-start.6 = (bf16[64,512]{1,0:T(8,128)(2,1)}, bf16[64,512]{1,0:T(8,128)(2,1)S(1)}, u32[]{:S(2)}, u32[]{:S(2)}) collective-permute-start(bf16[64,512]{1,0:T(8,128)(2,1)} %refs_4_.1), channel_id=1, source_target_pairs={{0,1},{1,0},{2,3},{3,2},{4,5},{5,4},{6,7},{7,6},{8,9},{9,8},{10,11... | collective-permute-start | bytes 196616 | tf_op jit(solution)/shard_map/ppermute | solution.py:40
  19.1 8.0 %collective-permute-start.7 = (bf16[64,512]{1,0:T(8,128)(2,1)S(1)}, bf16[64,512]{1,0:T(8,128)(2,1)S(1)}, u32[]{:S(2)}, u32[]{:S(2)}) collective-permute-start(bf16[64,512]{1,0:T(8,128)(2,1)S(1)} %collective-permute-done.3.refs_5_), channel_id=1, source_target_pairs={{0,1},{1,0},{2,3},{3,2},{4,5},{5,4},{6,7},{7,6},{8,9},{9,8},{10,11... | collective-permute-start | bytes 196616 | tf_op jit(solution)/shard_map/ppermute | solution.py:40
  20.9 6.2 %collective-permute-start.8 = (bf16[64,512]{1,0:T(8,128)(2,1)S(1)}, bf16[64,512]{1,0:T(8,128)(2,1)S(1)}, u32[]{:S(2)}, u32[]{:S(2)}) collective-permute-start(bf16[64,512]{1,0:T(8,128)(2,1)S(1)} %collective-permute-done.4.refs_6_), channel_id=1, source_target_pairs={{0,1},{1,0},{2,3},{3,2},{4,5},{5,4},{6,7},{7,6},{8,9},{9,8},{10,11... | collective-permute-start | bytes 196616 | tf_op jit(solution)/shard_map/ppermute | solution.py:40
  22.4 4.7 %collective-permute-start.9 = (bf16[64,512]{1,0:T(8,128)(2,1)S(1)}, bf16[64,512]{1,0:T(8,128)(2,1)S(1)}, u32[]{:S(2)}, u32[]{:S(2)}) collective-permute-start(bf16[64,512]{1,0:T(8,128)(2,1)S(1)} %collective-permute-done.5.refs_7_), channel_id=1, source_target_pairs={{0,1},{1,0},{2,3},{3,2},{4,5},{5,4},{6,7},{7,6},{8,9},{9,8},{10,11... | collective-permute-start | bytes 196616 | tf_op jit(solution)/shard_map/ppermute | solution.py:40
  45.5 11.9 %collective-permute-start.24 = (bf16[256,512]{1,0:T(8,128)(2,1)S(1)}, bf16[256,512]{1,0:T(8,128)(2,1)S(1)}, u32[]{:S(2)}, u32[]{:S(2)}) collective-permute-start(bf16[256,512]{1,0:T(8,128)(2,1)S(1)} %get-tuple-element.37), channel_id=1, source_target_pairs={{0,1},{1,0},{2,3},{3,2},{4,5},{5,4},{6,7},{7,6},{8,9},{9,8},{10,11... | collective-permute-start | bytes 786440 | tf_op jit(solution)/shard_map/ppermute | solution.py:40
  47.1 12.7 %collective-permute-start.11 = (bf16[256,256]{1,0:T(8,128)(2,1)S(1)}, bf16[256,256]{1,0:T(8,128)(2,1)S(1)}, u32[]{:S(2)}, u32[]{:S(2)}) collective-permute-start(bf16[256,256]{1,0:T(8,128)(2,1)S(1)} %get-tuple-element.27), channel_id=1, source_target_pairs={{0,1},{1,0},{2,3},{3,2},{4,5},{5,4},{6,7},{7,6},{8,9},{9,8},{10,11... | collective-permute-start | bytes 393224 | tf_op jit(solution)/shard_map/ppermute | solution.py:46
  47.7 12.1 %collective-permute-start.12 = (bf16[256,256]{1,0:T(8,128)(2,1)S(1)}, bf16[256,256]{1,0:T(8,128)(2,1)S(1)}, u32[]{:S(2)}, u32[]{:S(2)}) collective-permute-start(bf16[256,256]{1,0:T(8,128)(2,1)S(1)} %get-tuple-element.28), channel_id=1, source_target_pairs={{0,16},{1,17},{2,18},{3,19},{4,20},{5,21},{6,22},{7,23},{8,24},{9,... | collective-permute-start | bytes 393224 | tf_op jit(solution)/shard_map/ppermute | solution.py:46
  49.1 10.7 %collective-permute-start.13 = (bf16[256,256]{1,0:T(8,128)(2,1)S(1)}, bf16[256,256]{1,0:T(8,128)(2,1)S(1)}, u32[]{:S(2)}, u32[]{:S(2)}) collective-permute-start(bf16[256,256]{1,0:T(8,128)(2,1)S(1)} %get-tuple-element.29), channel_id=1, source_target_pairs={{0,17},{1,16},{2,19},{3,18},{4,21},{5,20},{6,23},{7,22},{8,25},{9,... | collective-permute-start | bytes 393224 | tf_op jit(solution)/shard_map/ppermute | solution.py:46
  57.5 14.1 %collective-permute-start.25 = (bf16[64,512]{1,0:T(8,128)(2,1)S(1)}, bf16[64,512]{1,0:T(8,128)(2,1)S(1)}, u32[]{:S(2)}, u32[]{:S(2)}) collective-permute-start(bf16[64,512]{1,0:T(8,128)(2,1)S(1)} %get-tuple-element.39), channel_id=1, source_target_pairs={{0,2},{1,3},{2,0},{3,1},{4,6},{5,7},{6,4},{7,5},{8,10},{9,11},{10,... | collective-permute-start | bytes 196616 | tf_op jit(solution)/shard_map/ppermute | solution.py:40
  59.9 6.1 %collective-permute-start.14 = (bf16[64,256]{1,0:T(8,128)(2,1)S(1)}, bf16[64,256]{1,0:T(8,128)(2,1)S(1)}, u32[]{:S(2)}, u32[]{:S(2)}) collective-permute-start(bf16[64,256]{1,0:T(8,128)(2,1)S(1)} %get-tuple-element.31), channel_id=1, source_target_pairs={{0,2},{1,3},{2,0},{3,1},{4,6},{5,7},{6,4},{7,5},{8,10},{9,11},{10,... | collective-permute-start | bytes 98312 | tf_op jit(solution)/shard_map/ppermute | solution.py:40
  61.2 7.1 %collective-permute-start.15 = (bf16[64,256]{1,0:T(8,128)(2,1)S(1)}, bf16[64,256]{1,0:T(8,128)(2,1)S(1)}, u32[]{:S(2)}, u32[]{:S(2)}) collective-permute-start(bf16[64,256]{1,0:T(8,128)(2,1)S(1)} %get-tuple-element.32), channel_id=1, source_target_pairs={{0,4},{1,5},{2,6},{3,7},{4,0},{5,1},{6,2},{7,3},{8,12},{9,13},{10,... | collective-permute-start | bytes 98312 | tf_op jit(solution)/shard_map/ppermute | solution.py:40
  64.4 5.8 %collective-permute-start.16 = (bf16[64,256]{1,0:T(8,128)(2,1)S(1)}, bf16[64,256]{1,0:T(8,128)(2,1)S(1)}, u32[]{:S(2)}, u32[]{:S(2)}) collective-permute-start(bf16[64,256]{1,0:T(8,128)(2,1)S(1)} %get-tuple-element.33), channel_id=1, source_target_pairs={{0,6},{1,7},{2,4},{3,5},{4,2},{5,3},{6,0},{7,1},{8,14},{9,15},{10,... | collective-permute-start | bytes 98312 | tf_op jit(solution)/shard_map/ppermute | solution.py:40
  64.4 10.3 %collective-permute-start.26 = (bf16[64,512]{1,0:T(8,128)(2,1)S(1)}, bf16[64,512]{1,0:T(8,128)(2,1)S(1)}, u32[]{:S(2)}, u32[]{:S(2)}) collective-permute-start(bf16[64,512]{1,0:T(8,128)(2,1)S(1)} %get-tuple-element.40), channel_id=1, source_target_pairs={{0,4},{1,5},{2,6},{3,7},{4,0},{5,1},{6,2},{7,3},{8,12},{9,13},{10,... | collective-permute-start | bytes 196616 | tf_op jit(solution)/shard_map/ppermute | solution.py:40
  65.9 12.9 %collective-permute-start.27 = (bf16[64,512]{1,0:T(8,128)(2,1)S(1)}, bf16[64,512]{1,0:T(8,128)(2,1)S(1)}, u32[]{:S(2)}, u32[]{:S(2)}) collective-permute-start(bf16[64,512]{1,0:T(8,128)(2,1)S(1)} %get-tuple-element.41), channel_id=1, source_target_pairs={{0,6},{1,7},{2,4},{3,5},{4,2},{5,3},{6,0},{7,1},{8,14},{9,15},{10,... | collective-permute-start | bytes 196616 | tf_op jit(solution)/shard_map/ppermute | solution.py:40
  70.3 5.3 %collective-permute-start.17 = (bf16[64,256]{1,0:T(8,128)(2,1)S(1)}, bf16[64,256]{1,0:T(8,128)(2,1)S(1)}, u32[]{:S(2)}, u32[]{:S(2)}) collective-permute-start(bf16[64,256]{1,0:T(8,128)(2,1)S(1)} %shard_map.125.refs_0_), channel_id=1, source_target_pairs={{0,2},{1,3},{2,0},{3,1},{4,6},{5,7},{6,4},{7,5},{8,10},{9,11},{10,... | collective-permute-start | bytes 98312 | tf_op jit(solution)/shard_map/ppermute | solution.py:40
  70.3 6.4 %collective-permute-start.18 = (bf16[64,256]{1,0:T(8,128)(2,1)S(1)}, bf16[64,256]{1,0:T(8,128)(2,1)S(1)}, u32[]{:S(2)}, u32[]{:S(2)}) collective-permute-start(bf16[64,256]{1,0:T(8,128)(2,1)S(1)} %shard_map.125.refs_0_), channel_id=1, source_target_pairs={{0,4},{1,5},{2,6},{3,7},{4,0},{5,1},{6,2},{7,3},{8,12},{9,13},{10,... | collective-permute-start | bytes 98312 | tf_op jit(solution)/shard_map/ppermute | solution.py:40
  71.6 6.0 %collective-permute-start.19 = (bf16[64,256]{1,0:T(8,128)(2,1)S(1)}, bf16[64,256]{1,0:T(8,128)(2,1)S(1)}, u32[]{:S(2)}, u32[]{:S(2)}) collective-permute-start(bf16[64,256]{1,0:T(8,128)(2,1)S(1)} %shard_map.125.refs_0_), channel_id=1, source_target_pairs={{0,6},{1,7},{2,4},{3,5},{4,2},{5,3},{6,0},{7,1},{8,14},{9,15},{10,... | collective-permute-start | bytes 98312 | tf_op jit(solution)/shard_map/ppermute | solution.py:40
  74.7 5.1 %collective-permute-start.20 = (bf16[64,256]{1,0:T(8,128)(2,1)S(1)}, bf16[64,256]{1,0:T(8,128)(2,1)S(1)}, u32[]{:S(2)}, u32[]{:S(2)}) collective-permute-start(bf16[64,256]{1,0:T(8,128)(2,1)S(1)} %shard_map.125.refs_0_), channel_id=1, source_target_pairs={{0,1},{1,0},{2,3},{3,2},{4,5},{5,4},{6,7},{7,6},{8,9},{9,8},{10,11... | collective-permute-start | bytes 98312 | tf_op jit(solution)/shard_map/ppermute | solution.py:40
  (15 other events, 102.4 us)

commit v2 on v0

v2 whole, which is shorter than its diff:
```python
import functools

import jax
import jax.numpy as jnp
from jax import lax
from jax.experimental import pallas as pl
from jax.experimental.pallas import tpu as pltpu
from jax.sharding import PartitionSpec as P

BF16, F32 = jnp.bfloat16, jnp.float32
VMEM = pl.BlockSpec(memory_space=pltpu.VMEM)
SMEM = pl.BlockSpec(memory_space=pltpu.SMEM)
HBM = pl.BlockSpec(memory_space=pltpu.HBM)
HIGHEST = lax.Precision.HIGHEST


def params(mib):
    return pltpu.CompilerParams(vmem_limit_bytes=mib * 2**20)


def cost(flops, moved):
    return pl.CostEstimate(flops=flops, bytes_accessed=moved, transcendentals=0)


def send_group(x, k):
    return lax.ppermute(x, "group", [(i, i ^ k) for i in range(lax.axis_size("group"))])


def send_leaf(x, k):
    return lax.ppermute(x, "leaf", [(i, i ^ k) for i in range(lax.axis_size("leaf"))])


def send_both(x, kg, kl):
    groups, leaves = lax.axis_size("group"), lax.axis_size("leaf")
    pairs = [(g * leaves + l, (g ^ kg) * leaves + (l ^ kl)) for g in range(groups) for l in range(leaves)]
    return lax.ppermute(x, ("group", "leaf"), pairs)


def gather_leaf(x, got):
    rels = [0]
    for bit in range(lax.axis_size("leaf").bit_length() - 2, 1, -1):
        if len(rels) > 1:
            got = send_leaf(x, 1 << bit)
        x = jnp.concatenate([x, got], axis=0)
        rels = rels + [r ^ (1 << bit) for r in rels]
    return [(x, rels)] + [(send_leaf(x, k), [r ^ k for r in rels]) for k in (2, 3, 1)]


def load_kernel(coupling, mass, modes, c_ref, mass_ref, m_ref, ct_ref, mt_ref, sem):
    copies = [
        pltpu.make_async_copy(src, dst, sem.at[i])
        for i, (src, dst) in enumerate(((coupling, c_ref), (modes, m_ref), (mass, mass_ref)))
    ]
    for copy in copies:
        copy.start()
    step = 512
    copies[0].wait()
    for i in range(c_ref.shape[0] // step):
        at = slice(i * step, (i + 1) * step)
        ct_ref[:, at] = c_ref[at, :].T
    copies[1].wait()
    mt_ref[...] = m_ref[...].T
    copies[2].wait()


def load_call(coupling, mass, modes):
    arrays = (coupling, mass, modes)
    shapes = [a.shape for a in arrays] + [coupling.shape[::-1], modes.shape[::-1]]
    return pl.pallas_call(
        load_kernel,
        in_specs=[HBM] * 3,
        out_specs=[VMEM] * 5,
        out_shape=[pltpu.VMEM(s, BF16) for s in shapes],
        scratch_shapes=[pltpu.SemaphoreType.DMA((3,))],
        compiler_params=params(8),
        cost_estimate=cost(0, 2 * sum(a.size for a in arrays)),
    )(*[pltpu.with_memory_space_constraint(a, pltpu.HBM) for a in arrays])


def main_kernel(n_top, low_rels, anc_top, anc_low, *refs):
    n_low = len(low_rels)
    tops, lows = refs[:n_top], refs[n_top : n_top + n_low]
    coupling, mass, modes, coef, ct = refs[n_top + n_low : n_top + n_low + 5]
    send, keep, weighted = refs[n_top + n_low + 5 : n_top + n_low + 8]
    slot_top, slot_low, stacked, shapes = refs[n_top + n_low + 8 :]
    group, leaf = lax.axis_index("group"), lax.axis_index("leaf")
    top_slots, low_slots = anc_top.shape[1], anc_low.shape[1]
    slots = top_slots + low_slots
    sr = stacked.shape[0] // (slots + 1)
    per_group = tops[0].shape[0] // sr
    rows = mass.shape[0]
    step = 512

    for b in range(slot_top.shape[0]):
        slot_top[b] = slots
    for b in range(slot_low.shape[0]):
        slot_low[b] = slots
    for j in range(top_slots):
        slot_top[anc_top[0, j]] = j
    for j in range(low_slots):
        slot_low[anc_low[0, j]] = top_slots + j
    for r, piece in enumerate(tops):
        for p in range(per_group):
            at = pl.multiple_of(slot_top[(group ^ r) * per_group + p] * sr, sr)
            stacked[pl.ds(at, sr), :] = piece[p * sr : (p + 1) * sr, :]
    for piece, rels in zip(lows, low_rels):
        for p, r in enumerate(rels):
            at = pl.multiple_of(slot_low[leaf ^ r] * sr, sr)
            stacked[pl.ds(at, sr), :] = piece[p * sr : (p + 1) * sr, :]
    send[...] = jnp.zeros(send.shape, send.dtype)
    keep[...] = jnp.zeros(keep.shape, keep.dtype)
    for i in range(rows // step):
        at = slice(i * step, (i + 1) * step)
        shapes[at, :] = (
            jnp.dot(modes[at, :], coef[...], preferred_element_type=F32)
            - jnp.dot(coupling[at, :], stacked[: slots * sr, :], preferred_element_type=F32)
        ).astype(BF16)
    for i in range(rows // step):
        at = slice(i * step, (i + 1) * step)
        weighted[at, :] = jnp.dot(mass[at, :], shapes[...], preferred_element_type=F32).astype(BF16)
    width = weighted.shape[1] // 2
    for q in range(2):
        col = pl.multiple_of(((leaf & 1) ^ q) * width, 128)
        loads = jnp.dot(ct[: top_slots * sr, :], weighted[:, pl.ds(col, width)], preferred_element_type=F32)
        for j in range(top_slots):
            b = anc_top[0, j]
            turn = (b // per_group) ^ group
            row = (turn >> 1) * per_group + ((b % per_group) ^ (((leaf >> 1) & 1) * (per_group // 2)))
            at = pl.ds(pl.multiple_of(row * sr, sr), sr)
            block = loads[j * sr : (j + 1) * sr]

            @pl.when((turn & 1) == 0)
            def _():
                keep[at, q * width : (q + 1) * width] = block

            @pl.when((turn & 1) == 1)
            def _():
                send[at, q * width : (q + 1) * width] = block.astype(BF16)


def main_call(anc_top, anc_low, tops, lows, low_rels, coupling, mass, modes, coef, ct, sr, leaves):
    rows, sw = coupling.shape
    m = coef.shape[1]
    half_rows = len(tops) * tops[0].shape[0] // 2
    top_rows = anc_top.shape[1] * sr
    flops = 2 * m * rows * (sw + rows + modes.shape[1] + top_rows)
    return pl.pallas_call(
        functools.partial(main_kernel, len(tops), low_rels),
        in_specs=[SMEM, SMEM] + [VMEM] * (len(tops) + len(lows) + 5),
        out_specs=[VMEM, VMEM, VMEM],
        out_shape=[
            jax.ShapeDtypeStruct((half_rows, m), BF16),
            jax.ShapeDtypeStruct((half_rows, m), F32),
            jax.ShapeDtypeStruct((rows, m), BF16),
        ],
        scratch_shapes=[
            pltpu.SMEM((len(tops) * tops[0].shape[0] // sr,), jnp.int32),
            pltpu.SMEM((leaves,), jnp.int32),
            pltpu.VMEM((sw + sr, m), BF16),
            pltpu.VMEM((rows, m), BF16),
        ],
        compiler_params=params(12),
        cost_estimate=cost(flops, 2 * rows * (sw + rows)),
    )(anc_top, anc_low, *tops, *lows, coupling, mass, modes, coef, ct)


def low_kernel(leaves, anc_low, ct, weighted, keep, send):
    slots = anc_low.shape[1]
    sr = keep.shape[0] * 2 // leaves
    first = ct.shape[0] - slots * sr
    bits = leaves.bit_length() - 1
    leaf = lax.axis_index("leaf")
    if slots < leaves:
        keep[...] = jnp.zeros(keep.shape, keep.dtype)
        send[...] = jnp.zeros(send.shape, send.dtype)
    part = 8
    for h in range(slots // part):
        at = slice(first + h * part * sr, first + (h + 1) * part * sr)
        loads = jnp.dot(ct[at, :], weighted[...], preferred_element_type=F32)
        for j in range(part):
            turn = anc_low[0, h * part + j] ^ leaf
            row = 0
            for i in range(1, bits):
                row += ((turn >> i) & 1) << (bits - 1 - i)
            at = pl.ds(pl.multiple_of(row * sr, sr), sr)
            block = loads[j * sr : (j + 1) * sr]

            @pl.when((turn & 1) == 0)
            def _():
                keep[at, :] = block

            @pl.when((turn & 1) == 1)
            def _():
                send[at, :] = block.astype(BF16)


def proj_kernel(mt, weighted, proj):
    proj[...] = jnp.dot(mt[...], weighted[...], preferred_element_type=F32).astype(BF16)


def proj_call(mt, weighted):
    (modes, rows), m = mt.shape, weighted.shape[1]
    return pl.pallas_call(
        proj_kernel,
        in_specs=[VMEM] * 2,
        out_specs=VMEM,
        out_shape=jax.ShapeDtypeStruct((modes, m), BF16),
        compiler_params=params(4),
        cost_estimate=cost(2 * m * rows * modes, 2 * rows * m),
    )(mt, weighted)


def low_call(anc_low, ct, weighted, sr, leaves):
    rows, m = weighted.shape
    kept = leaves // 2 * sr
    low_rows = anc_low.shape[1] * sr
    return pl.pallas_call(
        functools.partial(low_kernel, leaves),
        in_specs=[SMEM, VMEM, VMEM],
        out_specs=[VMEM] * 2,
        out_shape=[jax.ShapeDtypeStruct((kept, m), F32), jax.ShapeDtypeStruct((kept, m), BF16)],
        compiler_params=params(12),
        cost_estimate=cost(2 * m * rows * low_rows, 2 * rows * (low_rows + m)),
    )(anc_low, ct, weighted)


def part_kernel(keep, got, *outs):
    height, width = outs[0].shape
    n = 0
    for r in range(keep.shape[0] // height):
        for c in range(keep.shape[1] // width):
            at = (slice(r * height, (r + 1) * height), slice(c * width, (c + 1) * width))
            outs[n][...] = (keep[at] + got[at].astype(F32)).astype(outs[n].dtype)
            n += 1


def part_call(keep, got, high, wide):
    piece = (keep.shape[0] // high, keep.shape[1] // wide)
    return pl.pallas_call(
        part_kernel,
        in_specs=[VMEM] * 2,
        out_specs=[VMEM] * (high * wide),
        out_shape=[jax.ShapeDtypeStruct(piece, F32)] + [jax.ShapeDtypeStruct(piece, BF16)] * (high * wide - 1),
        compiler_params=params(4),
        cost_estimate=cost(keep.size, 8 * keep.size),
    )(keep, got)


def sum_kernel(keep, *refs):
    total = keep[...].astype(F32)
    for got in refs[:-1]:
        total += got[...].astype(F32)
    refs[-1][...] = total.astype(BF16)


def sum_call(keep, got):
    return pl.pallas_call(
        sum_kernel,
        in_specs=[VMEM] * (1 + len(got)),
        out_specs=VMEM,
        out_shape=jax.ShapeDtypeStruct(keep.shape, BF16),
        compiler_params=params(4),
        cost_estimate=cost(keep.size, 8 * keep.size),
    )(keep, *got)


def low_end_kernel(keep, got, kinv, out):
    total = keep[...] + got[...].astype(F32)
    out[...] = jnp.dot(kinv[...], total, preferred_element_type=F32, precision=HIGHEST)


def low_end_call(keep, got, kinv):
    return pl.pallas_call(
        low_end_kernel,
        in_specs=[VMEM] * 3,
        out_specs=VMEM,
        out_shape=jax.ShapeDtypeStruct(keep.shape, F32),
        compiler_params=params(4),
        cost_estimate=cost(12 * keep.size * 64, 8 * keep.size),
    )(keep, got, kinv)


def top_end_kernel(rels, kinv, *refs):
    parts, out, loads = refs[:-2], refs[-2], refs[-1]
    leaf = lax.axis_index("leaf")
    sr = kinv.shape[1]
    for part, r in zip(parts, rels):
        height, width = part.shape
        there = leaf ^ r
        row = pl.multiple_of(((there >> 1) & 1) * height, height)
        col = pl.multiple_of((there & 1) * width, 128)
        loads[pl.ds(row, height), pl.ds(col, width)] = part[...]
    for b in range(out.shape[0] // sr):
        at = slice(b * sr, (b + 1) * sr)
        block = kinv[at, :]
        coarse = block.astype(BF16)
        fine = (block - coarse.astype(F32)).astype(BF16)
        rest = (block - coarse.astype(F32) - fine.astype(F32)).astype(BF16)
        parts = jnp.concatenate([coarse, fine, rest], axis=0)
        product = jnp.dot(parts, loads[at, :], preferred_element_type=F32)
        out[at, :] = product[:sr] + product[sr : 2 * sr] + product[2 * sr :]


def top_end_call(parts, rels, kinv, m):
    rows = kinv.shape[0]
    return pl.pallas_call(
        functools.partial(top_end_kernel, rels),
        in_specs=[VMEM] * (1 + len(parts)),
        out_specs=VMEM,
        out_shape=jax.ShapeDtypeStruct((rows, m), F32),
        scratch_shapes=[pltpu.VMEM((rows, m), BF16)],
        compiler_params=params(8),
        cost_estimate=cost(12 * rows * m * 64, 8 * rows * m),
    )(kinv, *parts)


def per_device(
    top_modes, low_modes, anc_top, anc_low, coupling, leaf_mass, leaf_modes, leaf_coef, kinv_top, kinv_low
):
    sr = kinv_low.shape[1]
    m = low_modes.shape[1]
    leaves = lax.axis_size("leaf")
    far_low = send_leaf(low_modes, leaves // 2)
    far_top = send_group(top_modes, 2)
    loaded = load_call(coupling, leaf_mass, leaf_modes)
    far_low, far_top, *loaded = lax.optimization_barrier((far_low, far_top, *loaded))
    coupling, leaf_mass, leaf_modes, ct, mt = loaded
    held = gather_leaf(low_modes, far_low)
    tops = [top_modes, send_group(top_modes, 1), far_top, send_group(far_top, 1)]
    send, keep, weighted = main_call(
        anc_top,
        anc_low,
        tops,
        [a for a, _ in held],
        [r for _, r in held],
        coupling,
        leaf_mass,
        leaf_modes,
        leaf_coef,
        ct,
        sr,
        leaves,
    )
    got = send_group(send, 1)
    low_keep, low_send = low_call(anc_low, ct, weighted, sr, leaves)
    low_keep, low_send, got = lax.optimization_barrier((low_keep, low_send, got))
    low_got = send_leaf(low_send, 1)
    keep, send = part_call(keep, got, 2, 1)
    got = send_group(send, 2)
    keep, *sends = part_call(keep, got, 2, 2)
    weighted, keep = lax.optimization_barrier((weighted, keep))
    got = [send_leaf(x, k) for x, k in zip(sends, (1, 2, 3))]
    leaf_proj = proj_call(mt, weighted)
    low_keep, got[1] = lax.optimization_barrier((low_keep, got[1]))
    low_keep, low_send = part_call(low_keep, low_got, 2, 1)
    low_got = send_leaf(low_send, 2)
    total = sum_call(keep, got)
    low_keep, total = lax.optimization_barrier((low_keep, total))
    for bit in range(2, leaves.bit_length() - 1):
        low_keep, low_send = part_call(low_keep, low_got, 2, 1)
        low_got = send_leaf(low_send, 1 << bit)
        total = sum_call(total, [send_leaf(total, 1 << bit)])
    rels = (0, 2, 1, 3)
    parts = [total] + [send_leaf(total, r) for r in rels[1:]]
    new_low = low_end_call(low_keep, low_got, kinv_low)
    new_top = top_end_call(parts, rels, kinv_top, m)
    return (new_top, new_low, leaf_proj)


def solution(mesh):
    both = P(("group", "leaf"), None)
    return jax.shard_map(
        per_device,
        mesh=mesh,
        in_specs=(P("group", None), both, both, both, both, both, both, both, P("group", None), both),
        out_specs=(P("group", None), both, both),
        check_vma=False,
    )
```

time: 280 us -> 63.9 us (0.23)
  waiting for transfers between devices: 190 us -> 21 us
  blocking collectives: 33.4 us -> 0 us
  matrix products: 28.3 us -> 0 us
  starting transfers between devices: 0.3 us -> 25.8 us
  Pallas kernels: 0 us -> 16 us
  local copies, waits for them, and re-layouts: 13.4 us -> 0.14 us
  between operations: 13.9 us -> 0.8 us
    psum x1 -> x0, waiting for transfers between devices: 125 us -> none  [per_device(): summed = lax.psum(top_term, ('group', 'leaf'))]
    reduce_scatter x1 -> x0, waiting for transfers between devices: 63.6 us -> none  [per_device(): lax.psum_scatter(jnp.einsum('ab,asm->bsm', chosen.astype(jnp.float32), lo...]
    all_gather x1 -> x0, blocking collectives: 33.4 us -> none  [per_device(): shard_rows = lax.all_gather(low_modes, 'leaf', axis=0, tiled=True)]
    dot_general x10 -> x0, matrix products: 28.3 us -> none  [the longest x1 7.5 us: per_device(): jnp.dot(leaf_mass, shapes, preferred_element_type=jnp.float32)]
    ppermute x0 -> x19, starting transfers between devices: none -> 25.8 us  [the longest x14 21 us: send_leaf(): lax.ppermute(x, 'leaf', [(i, i ^ k) for i in range(lax.axis_size('leaf'))])]
    ppermute x0 -> x19, waiting for transfers between devices: none -> 21 us  [the longest x14 13.8 us: send_leaf(): lax.ppermute(x, 'leaf', [(i, i ^ k) for i in range(lax.axis_size('leaf'))])]
    pallas_call x0 -> x12, Pallas kernels: none -> 16 us  [the longest x1 7.45 us: main_call(): pl.pallas_call(functools.partial(main_kernel, len(tops), low_rels), in_sp...]
    slice x3 -> x0, local copies, waits for them, and re-layouts: 6.69 us -> none  [the longest x2 4.09 us: per_device(): loads[top_slots * sep_rows:].reshape(low_slots, sep_rows, mode_count)]
  transfers between devices with their start and end apart: 3 -> 19, of which waited for: 2 -> 11; matrix products, arithmetic and copies ran while one was open for 5% -> 0% of each run, Pallas kernels for 0% -> 12%
where the time goes in v2:
time: 63.9 us; the launch traced here: 63.7 us
  starting transfers between devices  25.8 us (40%)
  waiting for transfers between devices  21 us (33%)
  Pallas kernels  16 us (25%)
  between operations  0.8 us (1%)
    ppermute x14, starting transfers between devices, send_leaf(): lax.ppermute(x, 'leaf', [(i, i ^ k) for i in range(lax.axis_size('leaf'))])  21 us
    ppermute x14, waiting for transfers between devices, send_leaf(): lax.ppermute(x, 'leaf', [(i, i ^ k) for i in range(lax.axis_size('leaf'))])  13.8 us
    pallas_call x1, Pallas kernels, main_call(): pl.pallas_call(functools.partial(main_kernel, len(tops), low_rels), in_sp...  7.45 us
    ppermute x5, waiting for transfers between devices, send_group(): lax.ppermute(x, 'group', [(i, i ^ k) for i in range(lax.axis_size('group'...  7.18 us
    ppermute x5, starting transfers between devices, send_group(): lax.ppermute(x, 'group', [(i, i ^ k) for i in range(lax.axis_size('group'...  4.75 us
    pallas_call x1, Pallas kernels, load_call(): pl.pallas_call(load_kernel, in_specs=[HBM] * 3, out_specs=[VMEM] * 5, out...  3.44 us
    pallas_call x1, Pallas kernels, low_call(): pl.pallas_call(functools.partial(low_kernel, leaves), in_specs=[SMEM, VME...  1.66 us
  transfers between devices with their start and end apart: 19, of which 11 were waited for; matrix products, arithmetic and copies ran while one was open for 0% of the time, Pallas kernels for 12%

profile of v2, /device:TPU:0, one launch (start us, length us, event | category | flops | bytes accessed | tf_op | source)
XLA Modules:
  0.0 63.7 jit_solution(11422982475460119894)
XLA Ops:
  0.7 3.0 %collective-permute-start.1 = (bf16[256,512]{1,0:T(8,128)(2,1)}, bf16[256,512]{1,0:T(8,128)(2,1)S(1)}, u32[]{:S(2)}, u32[]{:S(2)}) collective-permute-start(bf16[256,512]{1,0:T(8,128)(2,1)} %refs_0_.1), channel_id=1, source_target_pairs={{0,16},{8,24},{16,0},{24,8},{1,17},{9,25},{17,1},{25,9},{2,18},{10... | collective-permute-start | bytes 786440 | tf_op jit(solution)/shard_map/ppermute | solution.py:26
  3.7 2.6 %collective-permute-start = (bf16[64,512]{1,0:T(8,128)(2,1)}, bf16[64,512]{1,0:T(8,128)(2,1)S(1)}, u32[]{:S(2)}, u32[]{:S(2)}) collective-permute-start(bf16[64,512]{1,0:T(8,128)(2,1)} %param.11), channel_id=1, source_target_pairs={{0,4},{1,5},{2,6},{3,7},{4,0},{5,1},{6,2},{7,3},{8,12},{9,13},{10,... | collective-permute-start | bytes 196616 | tf_op jit(solution)/shard_map/ppermute | solution.py:30
  6.3 3.4 %shard_map.121 = (bf16[1536,1024]{1,0:T(8,128)(2,1)S(1)}, bf16[1536,1536]{1,0:T(8,128)(2,1)S(1)}, bf16[1536,128]{1,0:T(8,128)(2,1)S(1)}, bf16[1024,1536]{1,0:T(8,128)(2,1)S(1)}, bf16[128,1536]{1,0:T(8,128)(2,1)S(1)}) custom-call(bf16[1536,1024]{1,0:T(8,128)(2,1)} %coupling.1, bf16[1536,1536]{1,0:T(8,128)(2,1)} %mass.1, bf16[1536,128]{1,0:T(8,128)(2,1)} %modes.1), custom_call_target="tpu_custom_call" | custom-call | bytes 8257536 | tf_op jit(solution)/shard_map/pallas_call | solution.py:69
  10.3 1.8 %collective-permute-start.4 = (bf16[128,512]{1,0:T(8,128)(2,1)S(1)}, bf16[128,512]{1,0:T(8,128)(2,1)S(1)}, u32[]{:S(2)}, u32[]{:S(2)}) collective-permute-start(bf16[128,512]{1,0:T(8,128)(2,1)S(1)} %constant_dynamic-update-slice_fusion.refs_4_), channel_id=1, source_target_pairs={{0,2},{1,3},{2,0},{3,1},{4,6},{5,7},{6,4},{7,5},{8,10},{9,11},{10,... | collective-permute-start | bytes 393224 | tf_op jit(solution)/shard_map/ppermute | solution.py:30
  12.1 1.4 %collective-permute-start.5 = (bf16[128,512]{1,0:T(8,128)(2,1)S(1)}, bf16[128,512]{1,0:T(8,128)(2,1)S(1)}, u32[]{:S(2)}, u32[]{:S(2)}) collective-permute-start(bf16[128,512]{1,0:T(8,128)(2,1)S(1)} %constant_dynamic-update-slice_fusion.refs_4_), channel_id=1, source_target_pairs={{0,3},{1,2},{2,1},{3,0},{4,7},{5,6},{6,5},{7,4},{8,11},{9,10},{10,... | collective-permute-start | bytes 393224 | tf_op jit(solution)/shard_map/ppermute | solution.py:30
  13.9 2.7 %collective-permute-done.4.refs_5_ = bf16[128,512]{1,0:T(8,128)(2,1)S(1)} collective-permute-done((bf16[128,512]{1,0:T(8,128)(2,1)S(1)}, bf16[128,512]{1,0:T(8,128)(2,1)S(1)}, u32[]{:S(2)}, u32[]{:S(2)}) %collective-permute-start.4) | collective-permute-done | bytes 131104 | tf_op jit(solution)/shard_map/ppermute | solution.py:30
  16.6 3.7 %collective-permute-done.5.refs_6_ = bf16[128,512]{1,0:T(8,128)(2,1)S(1)} collective-permute-done((bf16[128,512]{1,0:T(8,128)(2,1)S(1)}, bf16[128,512]{1,0:T(8,128)(2,1)S(1)}, u32[]{:S(2)}, u32[]{:S(2)}) %collective-permute-start.5) | collective-permute-done | bytes 131104 | tf_op jit(solution)/shard_map/ppermute | solution.py:30
  20.3 1.4 %collective-permute-done.6.refs_7_ = bf16[128,512]{1,0:T(8,128)(2,1)S(1)} collective-permute-done((bf16[128,512]{1,0:T(8,128)(2,1)S(1)}, bf16[128,512]{1,0:T(8,128)(2,1)S(1)}, u32[]{:S(2)}, u32[]{:S(2)}) %collective-permute-start.6) | collective-permute-done | bytes 131104 | tf_op jit(solution)/shard_map/ppermute | solution.py:30
  21.7 7.4 %shard_map.122 = (bf16[512,512]{1,0:T(8,128)(2,1)S(1)}, f32[512,512]{1,0:T(8,128)S(1)}, bf16[1536,512]{1,0:T(8,128)(2,1)S(1)}) custom-call(s32[1,8]{1,0:T(1,128)S(1)} %copy-done.4, s32[1,8]{1,0:T(1,128)S(1)} %copy-done.1, bf16[256,512]{1,0:T(8,128)(2,1)S(1)} %copy-done.2, bf16[256,512]{1,0:T(8,128)(2,1)S(1)} %collective-permute-done.2.refs_1_, ...), custom_call_target="tpu_custom_call" | custom-call | flops 5033164800 | bytes 7864320 | tf_op jit(solution)/shard_map/pallas_call | solution.py:147
  29.3 1.7 %shard_map.123 = (f32[256,512]{1,0:T(8,128)S(1)}, bf16[256,512]{1,0:T(8,128)(2,1)S(1)}) custom-call(s32[1,8]{1,0:T(1,128)S(1)} %copy-done.1, bf16[1024,1536]{1,0:T(8,128)(2,1)S(1)} %get-tuple-element.44.refs_12_.ct, bf16[1536,512]{1,0:T(8,128)(2,1)S(1)} %get-tuple-element.74.weighted), custom_call_target="tpu_custom_call" | custom-call | flops 805306368 | bytes 3145728 | tf_op jit(solution)/shard_map/pallas_call | solution.py:217
  31.3 1.6 %collective-permute-start.8 = (bf16[256,512]{1,0:T(8,128)(2,1)S(1)}, bf16[256,512]{1,0:T(8,128)(2,1)S(1)}, u32[]{:S(2)}, u32[]{:S(2)}) collective-permute-start(bf16[256,512]{1,0:T(8,128)(2,1)S(1)} %get-tuple-element.58), channel_id=1, source_target_pairs={{0,16},{8,24},{16,0},{24,8},{1,17},{9,25},{17,1},{25,9},{2,18},{10... | collective-permute-start | bytes 786440 | tf_op jit(solution)/shard_map/ppermute | solution.py:26
  33.4 6.5 %collective-permute-done.8.got = bf16[256,512]{1,0:T(8,128)(2,1)S(1)} collective-permute-done((bf16[256,512]{1,0:T(8,128)(2,1)S(1)}, bf16[256,512]{1,0:T(8,128)(2,1)S(1)}, u32[]{:S(2)}, u32[]{:S(2)}) %collective-permute-start.8) | collective-permute-done | bytes 262176 | tf_op jit(solution)/shard_map/ppermute | solution.py:26
  39.9 1.7 %collective-permute-start.9 = (bf16[128,256]{1,0:T(8,128)(2,1)S(1)}, bf16[128,256]{1,0:T(8,128)(2,1)S(1)}, u32[]{:S(2)}, u32[]{:S(2)}) collective-permute-start(bf16[128,256]{1,0:T(8,128)(2,1)S(1)} %get-tuple-element.59), channel_id=1, source_target_pairs={{0,2},{1,3},{2,0},{3,1},{4,6},{5,7},{6,4},{7,5},{8,10},{9,11},{10,... | collective-permute-start | bytes 196616 | tf_op jit(solution)/shard_map/ppermute | solution.py:30
  42.0 1.4 %collective-permute-start.12 = (bf16[128,256]{1,0:T(8,128)(2,1)S(1)}, bf16[128,256]{1,0:T(8,128)(2,1)S(1)}, u32[]{:S(2)}, u32[]{:S(2)}) collective-permute-start(bf16[128,256]{1,0:T(8,128)(2,1)S(1)} %get-tuple-element.67), channel_id=1, source_target_pairs={{0,3},{1,2},{2,1},{3,0},{4,7},{5,6},{6,5},{7,4},{8,11},{9,10},{10,... | collective-permute-start | bytes 196616 | tf_op jit(solution)/shard_map/ppermute | solution.py:30
  44.3 2.2 %collective-permute-start.17 = (bf16[128,512]{1,0:T(8,128)(2,1)S(1)}, bf16[128,512]{1,0:T(8,128)(2,1)S(1)}, u32[]{:S(2)}, u32[]{:S(2)}) collective-permute-start(bf16[128,512]{1,0:T(8,128)(2,1)S(1)} %get-tuple-element.70), channel_id=1, source_target_pairs={{0,2},{1,3},{2,0},{3,1},{4,6},{5,7},{6,4},{7,5},{8,10},{9,11},{10,... | collective-permute-start | bytes 393224 | tf_op jit(solution)/shard_map/ppermute | solution.py:30
  47.3 2.7 %collective-permute-start.13 = (bf16[128,256]{1,0:T(8,128)(2,1)S(1)}, bf16[128,256]{1,0:T(8,128)(2,1)S(1)}, u32[]{:S(2)}, u32[]{:S(2)}) collective-permute-start(bf16[128,256]{1,0:T(8,128)(2,1)S(1)} %shard_map.127.keep), channel_id=1, source_target_pairs={{0,4},{1,5},{2,6},{3,7},{4,0},{5,1},{6,2},{7,3},{8,12},{9,13},{10,... | collective-permute-start | bytes 196616 | tf_op jit(solution)/shard_map/ppermute | solution.py:30
  50.0 3.2 %collective-permute-done.13.refs_0_ = bf16[128,256]{1,0:T(8,128)(2,1)S(1)} collective-permute-done((bf16[128,256]{1,0:T(8,128)(2,1)S(1)}, bf16[128,256]{1,0:T(8,128)(2,1)S(1)}, u32[]{:S(2)}, u32[]{:S(2)}) %collective-permute-start.13) | collective-permute-done | bytes 65568 | tf_op jit(solution)/shard_map/ppermute | solution.py:30
  53.7 1.6 %collective-permute-start.15 = (bf16[128,256]{1,0:T(8,128)(2,1)S(1)}, bf16[128,256]{1,0:T(8,128)(2,1)S(1)}, u32[]{:S(2)}, u32[]{:S(2)}) collective-permute-start(bf16[128,256]{1,0:T(8,128)(2,1)S(1)} %shard_map.128.refs_0_), channel_id=1, source_target_pairs={{0,1},{1,0},{2,3},{3,2},{4,5},{5,4},{6,7},{7,6},{8,9},{9,8},{10,11... | collective-permute-start | bytes 196616 | tf_op jit(solution)/shard_map/ppermute | solution.py:30
  55.3 1.5 %collective-permute-start.16 = (bf16[128,256]{1,0:T(8,128)(2,1)S(1)}, bf16[128,256]{1,0:T(8,128)(2,1)S(1)}, u32[]{:S(2)}, u32[]{:S(2)}) collective-permute-start(bf16[128,256]{1,0:T(8,128)(2,1)S(1)} %shard_map.128.refs_0_), channel_id=1, source_target_pairs={{0,3},{1,2},{2,1},{3,0},{4,7},{5,6},{6,5},{7,4},{8,11},{9,10},{10,... | collective-permute-start | bytes 196616 | tf_op jit(solution)/shard_map/ppermute | solution.py:30
  56.8 2.3 %collective-permute-start.18 = (bf16[64,512]{1,0:T(8,128)(2,1)S(1)}, bf16[64,512]{1,0:T(8,128)(2,1)S(1)}, u32[]{:S(2)}, u32[]{:S(2)}) collective-permute-start(bf16[64,512]{1,0:T(8,128)(2,1)S(1)} %get-tuple-element.72), channel_id=1, source_target_pairs={{0,4},{1,5},{2,6},{3,7},{4,0},{5,1},{6,2},{7,3},{8,12},{9,13},{10,... | collective-permute-start | bytes 196616 | tf_op jit(solution)/shard_map/ppermute | solution.py:30
  59.3 1.0 %shard_map.132 = bf16[128,512]{1,0:T(8,128)(2,1)} custom-call(bf16[128,1536]{1,0:T(8,128)(2,1)S(1)} %get-tuple-element.73.mt, bf16[1536,512]{1,0:T(8,128)(2,1)S(1)} %get-tuple-element.74.weighted), custom_call_target="tpu_custom_call" | custom-call | flops 201326592 | bytes 1572864 | tf_op jit(solution)/shard_map/pallas_call | solution.py:203
  60.5 1.2 %shard_map.129 = f32[256,512]{1,0:T(8,128)} custom-call(f32[256,64]{1,0:T(8,128)S(1)} %copy.13.kinv, bf16[128,256]{1,0:T(8,128)(2,1)S(1)} %shard_map.128.refs_0_, bf16[128,256]{1,0:T(8,128)(2,1)S(1)} %collective-permute-done.14.refs_1_, bf16[128,256]{1,0:T(8,128)(2,1)S(1)} %collective-permute-done.15.refs_2_, ...), custom_call_target="tpu_custom_call" | custom-call | flops 100663296 | bytes 1048576 | tf_op jit(solution)/shard_map/pallas_call | solution.py:306
  61.7 1.1 %collective-permute-done.18.got = bf16[64,512]{1,0:T(8,128)(2,1)S(1)} collective-permute-done((bf16[64,512]{1,0:T(8,128)(2,1)S(1)}, bf16[64,512]{1,0:T(8,128)(2,1)S(1)}, u32[]{:S(2)}, u32[]{:S(2)}) %collective-permute-start.18) | collective-permute-done | bytes 65568 | tf_op jit(solution)/shard_map/ppermute | solution.py:30
  62.8 0.9 %shard_map.131 = f32[64,512]{1,0:T(8,128)} custom-call(f32[64,512]{1,0:T(8,128)S(1)} %get-tuple-element.71.keep, bf16[64,512]{1,0:T(8,128)(2,1)S(1)} %collective-permute-done.18.got, f32[64,64]{1,0:T(8,128)S(1)} %copy-done), custom_call_target="tpu_custom_call" | custom-call | flops 25165824 | bytes 262144 | tf_op jit(solution)/shard_map/pallas_call | solution.py:273
  (43 shorter events, 4.9 us)
Async XLA Ops:
  0.6 21.1 %copy-start.2 = (bf16[256,512]{1,0:T(8,128)(2,1)S(1)}, bf16[256,512]{1,0:T(8,128)(2,1)}, u32[]{:S(2)}) copy-start(bf16[256,512]{1,0:T(8,128)(2,1)} %refs_0_.1) | copy-start | bytes 786436
  0.7 21.0 %copy-start.4 = (s32[1,8]{1,0:T(1,128)S(1)}, s32[1,8]{1,0:T(1,128)}, u32[]{:S(2)}) copy-start(s32[1,8]{1,0:T(1,128)} %anc_top.1) | copy-start | bytes 100
  0.7 21.0 %copy-start.1 = (s32[1,8]{1,0:T(1,128)S(1)}, s32[1,8]{1,0:T(1,128)}, u32[]{:S(2)}) copy-start(s32[1,8]{1,0:T(1,128)} %anc_low.3) | copy-start | bytes 100
  0.7 9.5 %collective-permute-start.1 = (bf16[256,512]{1,0:T(8,128)(2,1)}, bf16[256,512]{1,0:T(8,128)(2,1)S(1)}, u32[]{:S(2)}, u32[]{:S(2)}) collective-permute-start(bf16[256,512]{1,0:T(8,128)(2,1)} %refs_0_.1), channel_id=1, source_target_pairs={{0,16},{8,24},{16,0},{24,8},{1,17},{9,25},{17,1},{25,9},{2,18},{10... | collective-permute-start | bytes 786440 | tf_op jit(solution)/shard_map/ppermute | solution.py:26
  3.7 6.0 %collective-permute-start = (bf16[64,512]{1,0:T(8,128)(2,1)}, bf16[64,512]{1,0:T(8,128)(2,1)S(1)}, u32[]{:S(2)}, u32[]{:S(2)}) collective-permute-start(bf16[64,512]{1,0:T(8,128)(2,1)} %param.11), channel_id=1, source_target_pairs={{0,4},{1,5},{2,6},{3,7},{4,0},{5,1},{6,2},{7,3},{8,12},{9,13},{10,... | collective-permute-start | bytes 196616 | tf_op jit(solution)/shard_map/ppermute | solution.py:30
  6.3 7.7 %collective-permute-start.2 = (bf16[256,512]{1,0:T(8,128)(2,1)}, bf16[256,512]{1,0:T(8,128)(2,1)S(1)}, u32[]{:S(2)}, u32[]{:S(2)}) collective-permute-start(bf16[256,512]{1,0:T(8,128)(2,1)} %refs_0_.1), channel_id=1, source_target_pairs={{0,8},{8,0},{16,24},{24,16},{1,9},{9,1},{17,25},{25,17},{2,10},{10... | collective-permute-start | bytes 786440 | tf_op jit(solution)/shard_map/ppermute | solution.py:26
  10.2 11.5 %collective-permute-start.3 = (bf16[256,512]{1,0:T(8,128)(2,1)S(1)}, bf16[256,512]{1,0:T(8,128)(2,1)S(1)}, u32[]{:S(2)}, u32[]{:S(2)}) collective-permute-start(bf16[256,512]{1,0:T(8,128)(2,1)S(1)} %collective-permute-done.1.refs_2_), channel_id=1, source_target_pairs={{0,8},{8,0},{16,24},{24,16},{1,9},{9,1},{17,25},{25,17},{2,10},{10... | collective-permute-start | bytes 786440 | tf_op jit(solution)/shard_map/ppermute | solution.py:26
  10.3 6.3 %collective-permute-start.4 = (bf16[128,512]{1,0:T(8,128)(2,1)S(1)}, bf16[128,512]{1,0:T(8,128)(2,1)S(1)}, u32[]{:S(2)}, u32[]{:S(2)}) collective-permute-start(bf16[128,512]{1,0:T(8,128)(2,1)S(1)} %constant_dynamic-update-slice_fusion.refs_4_), channel_id=1, source_target_pairs={{0,2},{1,3},{2,0},{3,1},{4,6},{5,7},{6,4},{7,5},{8,10},{9,11},{10,... | collective-permute-start | bytes 393224 | tf_op jit(solution)/shard_map/ppermute | solution.py:30
  12.1 8.2 %collective-permute-start.5 = (bf16[128,512]{1,0:T(8,128)(2,1)S(1)}, bf16[128,512]{1,0:T(8,128)(2,1)S(1)}, u32[]{:S(2)}, u32[]{:S(2)}) collective-permute-start(bf16[128,512]{1,0:T(8,128)(2,1)S(1)} %constant_dynamic-update-slice_fusion.refs_4_), channel_id=1, source_target_pairs={{0,3},{1,2},{2,1},{3,0},{4,7},{5,6},{6,5},{7,4},{8,11},{9,10},{10,... | collective-permute-start | bytes 393224 | tf_op jit(solution)/shard_map/ppermute | solution.py:30
  13.5 8.2 %collective-permute-start.6 = (bf16[128,512]{1,0:T(8,128)(2,1)S(1)}, bf16[128,512]{1,0:T(8,128)(2,1)S(1)}, u32[]{:S(2)}, u32[]{:S(2)}) collective-permute-start(bf16[128,512]{1,0:T(8,128)(2,1)S(1)} %constant_dynamic-update-slice_fusion.refs_4_), channel_id=1, source_target_pairs={{0,1},{1,0},{2,3},{3,2},{4,5},{5,4},{6,7},{7,6},{8,9},{9,8},{10,11... | collective-permute-start | bytes 393224 | tf_op jit(solution)/shard_map/ppermute | solution.py:30
  29.2 2.0 %collective-permute-start.7 = (bf16[512,512]{1,0:T(8,128)(2,1)S(1)}, bf16[512,512]{1,0:T(8,128)(2,1)S(1)}, u32[]{:S(2)}, u32[]{:S(2)}) collective-permute-start(bf16[512,512]{1,0:T(8,128)(2,1)S(1)} %get-tuple-element.53), channel_id=1, source_target_pairs={{0,8},{8,0},{16,24},{24,16},{1,9},{9,1},{17,25},{25,17},{2,10},{10... | collective-permute-start | bytes 1572872 | tf_op jit(solution)/shard_map/ppermute | solution.py:26
  30.9 28.3 %copy-start.5 = (f32[256,64]{0,1:T(8,128)S(1)}, f32[256,64]{0,1:T(8,128)}, u32[]{:S(2)}) copy-start(f32[256,64]{0,1:T(8,128)} %param.18) | copy-start | bytes 196612
  31.3 31.5 %copy-start = (f32[64,64]{1,0:T(8,128)S(1)}, f32[64,64]{1,0:T(8,128)}, u32[]{:S(2)}) copy-start(f32[64,64]{1,0:T(8,128)} %kinv.2) | copy-start | bytes 49156
  31.3 8.6 %collective-permute-start.8 = (bf16[256,512]{1,0:T(8,128)(2,1)S(1)}, bf16[256,512]{1,0:T(8,128)(2,1)S(1)}, u32[]{:S(2)}, u32[]{:S(2)}) collective-permute-start(bf16[256,512]{1,0:T(8,128)(2,1)S(1)} %get-tuple-element.58), channel_id=1, source_target_pairs={{0,16},{8,24},{16,0},{24,8},{1,17},{9,25},{17,1},{25,9},{2,18},{10... | collective-permute-start | bytes 786440 | tf_op jit(solution)/shard_map/ppermute | solution.py:26
  32.8 11.4 %collective-permute-start.10 = (bf16[256,512]{1,0:T(8,128)(2,1)S(1)}, bf16[256,512]{1,0:T(8,128)(2,1)S(1)}, u32[]{:S(2)}, u32[]{:S(2)}) collective-permute-start(bf16[256,512]{1,0:T(8,128)(2,1)S(1)} %get-tuple-element.61), channel_id=1, source_target_pairs={{0,1},{1,0},{2,3},{3,2},{4,5},{5,4},{6,7},{7,6},{8,9},{9,8},{10,11... | collective-permute-start | bytes 786440 | tf_op jit(solution)/shard_map/ppermute | solution.py:30
  39.9 4.3 %collective-permute-start.9 = (bf16[128,256]{1,0:T(8,128)(2,1)S(1)}, bf16[128,256]{1,0:T(8,128)(2,1)S(1)}, u32[]{:S(2)}, u32[]{:S(2)}) collective-permute-start(bf16[128,256]{1,0:T(8,128)(2,1)S(1)} %get-tuple-element.59), channel_id=1, source_target_pairs={{0,2},{1,3},{2,0},{3,1},{4,6},{5,7},{6,4},{7,5},{8,10},{9,11},{10,... | collective-permute-start | bytes 196616 | tf_op jit(solution)/shard_map/ppermute | solution.py:30
  41.5 4.9 %collective-permute-start.11 = (bf16[128,256]{1,0:T(8,128)(2,1)S(1)}, bf16[128,256]{1,0:T(8,128)(2,1)S(1)}, u32[]{:S(2)}, u32[]{:S(2)}) collective-permute-start(bf16[128,256]{1,0:T(8,128)(2,1)S(1)} %get-tuple-element.65), channel_id=1, source_target_pairs={{0,1},{1,0},{2,3},{3,2},{4,5},{5,4},{6,7},{7,6},{8,9},{9,8},{10,11... | collective-permute-start | bytes 196616 | tf_op jit(solution)/shard_map/ppermute | solution.py:30
  42.0 5.2 %collective-permute-start.12 = (bf16[128,256]{1,0:T(8,128)(2,1)S(1)}, bf16[128,256]{1,0:T(8,128)(2,1)S(1)}, u32[]{:S(2)}, u32[]{:S(2)}) collective-permute-start(bf16[128,256]{1,0:T(8,128)(2,1)S(1)} %get-tuple-element.67), channel_id=1, source_target_pairs={{0,3},{1,2},{2,1},{3,0},{4,7},{5,6},{6,5},{7,4},{8,11},{9,10},{10,... | collective-permute-start | bytes 196616 | tf_op jit(solution)/shard_map/ppermute | solution.py:30
  44.3 12.5 %collective-permute-start.17 = (bf16[128,512]{1,0:T(8,128)(2,1)S(1)}, bf16[128,512]{1,0:T(8,128)(2,1)S(1)}, u32[]{:S(2)}, u32[]{:S(2)}) collective-permute-start(bf16[128,512]{1,0:T(8,128)(2,1)S(1)} %get-tuple-element.70), channel_id=1, source_target_pairs={{0,2},{1,3},{2,0},{3,1},{4,6},{5,7},{6,4},{7,5},{8,10},{9,11},{10,... | collective-permute-start | bytes 393224 | tf_op jit(solution)/shard_map/ppermute | solution.py:30
  47.3 5.9 %collective-permute-start.13 = (bf16[128,256]{1,0:T(8,128)(2,1)S(1)}, bf16[128,256]{1,0:T(8,128)(2,1)S(1)}, u32[]{:S(2)}, u32[]{:S(2)}) collective-permute-start(bf16[128,256]{1,0:T(8,128)(2,1)S(1)} %shard_map.127.keep), channel_id=1, source_target_pairs={{0,4},{1,5},{2,6},{3,7},{4,0},{5,1},{6,2},{7,3},{8,12},{9,13},{10,... | collective-permute-start | bytes 196616 | tf_op jit(solution)/shard_map/ppermute | solution.py:30
  53.3 7.1 %collective-permute-start.14 = (bf16[128,256]{1,0:T(8,128)(2,1)S(1)}, bf16[128,256]{1,0:T(8,128)(2,1)S(1)}, u32[]{:S(2)}, u32[]{:S(2)}) collective-permute-start(bf16[128,256]{1,0:T(8,128)(2,1)S(1)} %shard_map.128.refs_0_), channel_id=1, source_target_pairs={{0,2},{1,3},{2,0},{3,1},{4,6},{5,7},{6,4},{7,5},{8,10},{9,11},{10,... | collective-permute-start | bytes 196616 | tf_op jit(solution)/shard_map/ppermute | solution.py:30
  53.7 6.6 %collective-permute-start.15 = (bf16[128,256]{1,0:T(8,128)(2,1)S(1)}, bf16[128,256]{1,0:T(8,128)(2,1)S(1)}, u32[]{:S(2)}, u32[]{:S(2)}) collective-permute-start(bf16[128,256]{1,0:T(8,128)(2,1)S(1)} %shard_map.128.refs_0_), channel_id=1, source_target_pairs={{0,1},{1,0},{2,3},{3,2},{4,5},{5,4},{6,7},{7,6},{8,9},{9,8},{10,11... | collective-permute-start | bytes 196616 | tf_op jit(solution)/shard_map/ppermute | solution.py:30
  55.3 5.2 %collective-permute-start.16 = (bf16[128,256]{1,0:T(8,128)(2,1)S(1)}, bf16[128,256]{1,0:T(8,128)(2,1)S(1)}, u32[]{:S(2)}, u32[]{:S(2)}) collective-permute-start(bf16[128,256]{1,0:T(8,128)(2,1)S(1)} %shard_map.128.refs_0_), channel_id=1, source_target_pairs={{0,3},{1,2},{2,1},{3,0},{4,7},{5,6},{6,5},{7,4},{8,11},{9,10},{10,... | collective-permute-start | bytes 196616 | tf_op jit(solution)/shard_map/ppermute | solution.py:30
  56.8 5.9 %collective-permute-start.18 = (bf16[64,512]{1,0:T(8,128)(2,1)S(1)}, bf16[64,512]{1,0:T(8,128)(2,1)S(1)}, u32[]{:S(2)}, u32[]{:S(2)}) collective-permute-start(bf16[64,512]{1,0:T(8,128)(2,1)S(1)} %get-tuple-element.72), channel_id=1, source_target_pairs={{0,4},{1,5},{2,6},{3,7},{4,0},{5,1},{6,2},{7,3},{8,12},{9,13},{10,... | collective-permute-start | bytes 196616 | tf_op jit(solution)/shard_map/ppermute | solution.py:30
  (2 other events, 30.7 us)

commit v3 on v2

v3 whole, which is shorter than its diff:
```python
import functools

import jax
import jax.numpy as jnp
from jax import lax
from jax.experimental import pallas as pl
from jax.experimental.pallas import tpu as pltpu
from jax.sharding import PartitionSpec as P

BF16, F32 = jnp.bfloat16, jnp.float32
VMEM = pl.BlockSpec(memory_space=pltpu.VMEM)
SMEM = pl.BlockSpec(memory_space=pltpu.SMEM)
HBM = pl.BlockSpec(memory_space=pltpu.HBM)
FILL = 20_000_000_000


def params(mib):
    return pltpu.CompilerParams(vmem_limit_bytes=mib * 2**20)


def cost(flops, moved):
    return pl.CostEstimate(flops=flops, bytes_accessed=moved, transcendentals=0)


def send_group(x, k):
    return lax.ppermute(x, "group", [(i, i ^ k) for i in range(lax.axis_size("group"))])


def send_leaf(x, k):
    return lax.ppermute(x, "leaf", [(i, i ^ k) for i in range(lax.axis_size("leaf"))])


def send_by_core(x, even, odd):
    groups, leaves = lax.axis_size("group"), lax.axis_size("leaf")
    pairs = []
    for g in range(groups):
        far, near = odd if g & 1 else even
        pairs += [(g * leaves + l, (g ^ far) * leaves + (l ^ near)) for l in range(leaves)]
    return lax.ppermute(x, ("group", "leaf"), pairs)


def gather_leaf(x, got):
    rels = [0]
    for bit in range(lax.axis_size("leaf").bit_length() - 2, 1, -1):
        if len(rels) > 1:
            got = send_leaf(x, 1 << bit)
        x = jnp.concatenate([x, got], axis=0)
        rels = rels + [r ^ (1 << bit) for r in rels]
    return [(x, rels)] + [(send_leaf(x, k), [r ^ k for r in rels]) for k in (2, 3, 1)]


def load_kernel(turned, *refs):
    n = len(turned)
    sources, copies, turns, sem = refs[:n], refs[n : 2 * n], list(refs[2 * n : -1]), refs[-1]
    moves = [pltpu.make_async_copy(s, d, sem.at[i]) for i, (s, d) in enumerate(zip(sources, copies))]
    for move in moves:
        move.start()
    for move, copy, turn in zip(moves, copies, turned):
        move.wait()
        if turn:
            out = turns.pop(0)
            step = 512
            for i in range(copy.shape[0] // step):
                at = slice(i * step, (i + 1) * step)
                out[:, at] = copy[at, :].T


def load_call(arrays, turned):
    shapes = [a.shape for a in arrays] + [a.shape[::-1] for a, t in zip(arrays, turned) if t]
    return pl.pallas_call(
        functools.partial(load_kernel, turned),
        in_specs=[HBM] * len(arrays),
        out_specs=[VMEM] * len(shapes),
        out_shape=[pltpu.VMEM(s, BF16) for s in shapes],
        scratch_shapes=[pltpu.SemaphoreType.DMA((len(arrays),))],
        compiler_params=params(8),
        cost_estimate=cost(FILL, 2 * sum(a.size for a in arrays)),
    )(*[pltpu.with_memory_space_constraint(a, pltpu.HBM) for a in arrays])


def main_kernel(n_top, low_rels, anc_top, anc_low, *refs):
    n_low = len(low_rels)
    tops, lows = refs[:n_top], refs[n_top : n_top + n_low]
    coupling, mass, modes, coef, ct = refs[n_top + n_low : n_top + n_low + 5]
    send, keep, weighted = refs[n_top + n_low + 5 : n_top + n_low + 8]
    slot_top, slot_low, stacked, shapes, loads = refs[n_top + n_low + 8 :]
    group, leaf = lax.axis_index("group"), lax.axis_index("leaf")
    top_slots, low_slots = anc_top.shape[1], anc_low.shape[1]
    slots = top_slots + low_slots
    sr = stacked.shape[0] // (slots + 1)
    per_group = tops[0].shape[0] // sr
    rows = mass.shape[0]
    step = 512

    for b in range(slot_top.shape[0]):
        slot_top[b] = slots
    for b in range(slot_low.shape[0]):
        slot_low[b] = slots
    for j in range(top_slots):
        slot_top[anc_top[0, j]] = j
    for j in range(low_slots):
        slot_low[anc_low[0, j]] = top_slots + j
    for r, piece in enumerate(tops):
        for p in range(per_group):
            at = pl.multiple_of(slot_top[(group ^ r) * per_group + p] * sr, sr)
            stacked[pl.ds(at, sr), :] = piece[p * sr : (p + 1) * sr, :]
    for piece, rels in zip(lows, low_rels):
        for p, r in enumerate(rels):
            at = pl.multiple_of(slot_low[leaf ^ r] * sr, sr)
            stacked[pl.ds(at, sr), :] = piece[p * sr : (p + 1) * sr, :]
    for i in range(rows // step):
        at = slice(i * step, (i + 1) * step)
        shapes[at, :] = (
            jnp.dot(modes[at, :], coef[...], preferred_element_type=F32)
            - jnp.dot(coupling[at, :], stacked[: slots * sr, :], preferred_element_type=F32)
        ).astype(BF16)
    for i in range(rows // step):
        at = slice(i * step, (i + 1) * step)
        weighted[at, :] = jnp.dot(mass[at, :], shapes[...], preferred_element_type=F32).astype(BF16)
    width = weighted.shape[1] // 2
    core, near, high = group & 1, leaf & 1, (leaf >> 1) & 1
    top_rows = top_slots * sr
    for q in range(2):
        loads[q, :top_rows, :] = jnp.dot(
            ct[:top_rows, :], weighted[:, q * width : (q + 1) * width], preferred_element_type=F32
        )
        loads[q, top_rows:, :] = jnp.zeros((sr, width), F32)
    for out, owner in ((keep, core), (send, 1 - core)):
        for first in range(2):
            for second in range(2):
                far = jnp.where(owner == 0, first, second) ^ (group >> 1)
                q = jnp.where(owner == 0, second, first) ^ near
                for p in range(per_group):
                    block = (2 * far + owner) * per_group + (p ^ (high * (per_group // 2)))
                    slot = jnp.minimum(slot_top[block], top_slots)
                    at = pl.ds(pl.multiple_of(slot * sr, sr), sr)
                    to = ((2 * first + second) * per_group + p) * sr
                    out[to : to + sr, :] = loads[q, at, :].astype(out.dtype)


def main_call(anc_top, anc_low, tops, lows, low_rels, coupling, mass, modes, coef, ct, sr, leaves):
    rows, sw = coupling.shape
    m = coef.shape[1]
    half_rows = len(tops) * tops[0].shape[0] // 2
    top_rows = anc_top.shape[1] * sr
    flops = 2 * m * rows * (sw + rows + modes.shape[1] + top_rows)
    return pl.pallas_call(
        functools.partial(main_kernel, len(tops), low_rels),
        in_specs=[SMEM, SMEM] + [VMEM] * (len(tops) + len(lows) + 5),
        out_specs=[VMEM, VMEM, VMEM],
        out_shape=[
            jax.ShapeDtypeStruct((2 * half_rows, m // 2), BF16),
            jax.ShapeDtypeStruct((2 * half_rows, m // 2), F32),
            jax.ShapeDtypeStruct((rows, m), BF16),
        ],
        scratch_shapes=[
            pltpu.SMEM((len(tops) * tops[0].shape[0] // sr,), jnp.int32),
            pltpu.SMEM((leaves,), jnp.int32),
            pltpu.VMEM((sw + sr, m), BF16),
            pltpu.VMEM((rows, m), BF16),
            pltpu.VMEM((2, top_rows + sr, m // 2), F32),
        ],
        compiler_params=params(12),
        cost_estimate=cost(flops, 2 * rows * (sw + rows)),
    )(anc_top, anc_low, *tops, *lows, coupling, mass, modes, coef, ct)


def low_kernel(leaves, anc_low, ct, weighted, keep, send, slot_low, loads):
    slots = anc_low.shape[1]
    sr = keep.shape[0] * 2 // leaves
    start = ct.shape[0] - slots * sr
    bits = leaves.bit_length() - 1
    leaf = lax.axis_index("leaf")
    even = (lax.axis_index("group") & 1) == 0
    for k in range(leaves):
        slot_low[k] = slots
    for j in range(slots):
        slot_low[anc_low[0, j]] = j
    loads[: slots * sr, :] = jnp.dot(ct[start:, :], weighted[...], preferred_element_type=F32)
    loads[slots * sr :, :] = jnp.zeros((sr, loads.shape[1]), F32)
    for first, out in enumerate((keep, send)):
        for row in range(leaves // 2):
            second = row >> (bits - 2)
            turn = jnp.where(even, 2 * first + second, 2 * second + first)
            for i in range(2, bits):
                turn += ((row >> (bits - 1 - i)) & 1) << i
            at = pl.ds(pl.multiple_of(slot_low[leaf ^ turn] * sr, sr), sr)
            out[row * sr : (row + 1) * sr, :] = loads[at, :].astype(out.dtype)


def proj_kernel(mt, weighted, proj):
    proj[...] = jnp.dot(mt[...], weighted[...], preferred_element_type=F32).astype(BF16)


def proj_call(mt, weighted):
    (modes, rows), m = mt.shape, weighted.shape[1]
    return pl.pallas_call(
        proj_kernel,
        in_specs=[VMEM] * 2,
        out_specs=VMEM,
        out_shape=jax.ShapeDtypeStruct((modes, m), BF16),
        compiler_params=params(4),
        cost_estimate=cost(FILL, 2 * rows * m),
    )(mt, weighted)


def low_call(anc_low, ct, weighted, sr, leaves):
    rows, m = weighted.shape
    kept = leaves // 2 * sr
    low_rows = anc_low.shape[1] * sr
    return pl.pallas_call(
        functools.partial(low_kernel, leaves),
        in_specs=[SMEM, VMEM, VMEM],
        out_specs=[VMEM] * 2,
        out_shape=[jax.ShapeDtypeStruct((kept, m), F32), jax.ShapeDtypeStruct((kept, m), BF16)],
        scratch_shapes=[pltpu.SMEM((leaves,), jnp.int32), pltpu.VMEM((low_rows + sr, m), F32)],
        compiler_params=params(12),
        cost_estimate=cost(2 * m * rows * low_rows, 2 * rows * (low_rows + m)),
    )(anc_low, ct, weighted)


def part_kernel(n_got, keep, *refs):
    got, outs = refs[:n_got], refs[n_got:]
    height, width = outs[0].shape
    n = 0
    for r in range(keep.shape[0] // height):
        for c in range(keep.shape[1] // width):
            at = (slice(r * height, (r + 1) * height), slice(c * width, (c + 1) * width))
            total = keep[at]
            for g in got:
                total += g[at].astype(F32)
            outs[n][...] = total.astype(outs[n].dtype)
            n += 1


def part_call(keep, got, high, wide):
    piece = (keep.shape[0] // high, keep.shape[1] // wide)
    return pl.pallas_call(
        functools.partial(part_kernel, len(got)),
        in_specs=[VMEM] * (1 + len(got)),
        out_specs=[VMEM] * (high * wide),
        out_shape=[jax.ShapeDtypeStruct(piece, F32)] + [jax.ShapeDtypeStruct(piece, BF16)] * (high * wide - 1),
        compiler_params=params(4),
        cost_estimate=cost(keep.size, 8 * keep.size),
    )(keep, *got)


def sum_kernel(keep, *refs):
    total = keep[...].astype(F32)
    for got in refs[:-1]:
        total += got[...].astype(F32)
    refs[-1][...] = total.astype(BF16)


def sum_call(keep, got):
    return pl.pallas_call(
        sum_kernel,
        in_specs=[VMEM] * (1 + len(got)),
        out_specs=VMEM,
        out_shape=jax.ShapeDtypeStruct(keep.shape, BF16),
        compiler_params=params(4),
        cost_estimate=cost(keep.size, 8 * keep.size),
    )(keep, *got)


def solve(kinv, loads):
    def parts(x):
        coarse = x.astype(BF16)
        fine = (x - coarse.astype(F32)).astype(BF16)
        return coarse, fine, (x - coarse.astype(F32) - fine.astype(F32)).astype(BF16)

    n = kinv.shape[0]
    total = None
    for i, part in enumerate(parts(loads) if loads.dtype == F32 else (loads,)):
        left = jnp.concatenate(parts(kinv)[: 3 - i], axis=0)
        product = jnp.dot(left, part, preferred_element_type=F32)
        for k in range(3 - i):
            term = product[k * n : (k + 1) * n]
            total = term if total is None else total + term
    return total


def low_end_kernel(kinv, keep, got, out):
    out[...] = solve(kinv[...], keep[...] + got[...].astype(F32))


def low_end_call(kinv, keep, got):
    return pl.pallas_call(
        low_end_kernel,
        in_specs=[VMEM] * 3,
        out_specs=VMEM,
        out_shape=jax.ShapeDtypeStruct(keep.shape, F32),
        compiler_params=params(4),
        cost_estimate=cost(12 * keep.size * 64, 8 * keep.size),
    )(kinv, keep, got)


def top_end_kernel(rels, kinv, *refs):
    parts, out, loads = refs[:-2], refs[-2], refs[-1]
    leaf = lax.axis_index("leaf")
    even = (lax.axis_index("group") & 1) == 0
    sr = kinv.shape[1]
    for part, (r_even, r_odd) in zip(parts, rels):
        height, width = part.shape
        there = leaf ^ jnp.where(even, r_even, r_odd)
        row = pl.multiple_of(((there >> 1) & 1) * height, height)
        col = pl.multiple_of((there & 1) * width, 128)
        loads[pl.ds(row, height), pl.ds(col, width)] = part[...]
    for b in range(out.shape[0] // sr):
        at = slice(b * sr, (b + 1) * sr)
        out[at, :] = solve(kinv[at, :], loads[at, :])


def top_end_call(parts, rels, kinv, m):
    rows = kinv.shape[0]
    return pl.pallas_call(
        functools.partial(top_end_kernel, rels),
        in_specs=[VMEM] * (1 + len(parts)),
        out_specs=VMEM,
        out_shape=jax.ShapeDtypeStruct((rows, m), F32),
        scratch_shapes=[pltpu.VMEM((rows, m), BF16)],
        compiler_params=params(8),
        cost_estimate=cost(12 * rows * m * 64, 8 * rows * m),
    )(kinv, *parts)


def per_device(
    top_modes, low_modes, anc_top, anc_low, coupling, leaf_mass, leaf_modes, leaf_coef, kinv_top, kinv_low
):
    sr = kinv_low.shape[1]
    m = low_modes.shape[1]
    leaves = lax.axis_size("leaf")
    near_top = send_group(top_modes, 1)
    far_low = send_leaf(low_modes, leaves // 2)
    near_top, to_send = lax.optimization_barrier((near_top, top_modes))
    far_top = send_group(to_send, 2)
    leaf_modes, mt = load_call((leaf_modes,), (True,))
    far_low, mt = lax.optimization_barrier((far_low, mt))
    held = gather_leaf(low_modes, far_low)
    coupling, leaf_mass, ct = load_call((coupling, leaf_mass), (True, False))
    tops = [top_modes, near_top, far_top, send_group(far_top, 1)]
    send, keep, weighted = main_call(
        anc_top,
        anc_low,
        tops,
        [a for a, _ in held],
        [r for _, r in held],
        coupling,
        leaf_mass,
        leaf_modes,
        leaf_coef,
        ct,
        sr,
        leaves,
    )
    got = send_group(send, 1)
    low_keep, low_send = low_call(anc_low, ct, weighted, sr, leaves)
    low_keep, low_send, got = lax.optimization_barrier((low_keep, low_send, got))
    low_got = send_by_core(low_send, (0, 2), (0, 1))
    keep, send = part_call(keep, [got], 2, 1)
    send, weighted = lax.optimization_barrier((send, weighted))
    got = send_by_core(send, (2, 0), (0, 1))
    leaf_proj = proj_call(mt, weighted)
    got, leaf_proj = lax.optimization_barrier((got, leaf_proj))
    keep, *sends = part_call(keep, [got], 4, 1)
    got = [
        send_by_core(x, *there)
        for x, there in zip(sends, (((0, 2), (0, 2)), ((0, 1), (2, 0)), ((0, 3), (2, 2))))
    ]
    low_keep, got[1] = lax.optimization_barrier((low_keep, got[1]))
    low_keep, low_send = part_call(low_keep, [low_got], 2, 1)
    low_got = send_by_core(low_send, (0, 1), (0, 2))
    total = sum_call(keep, got)
    low_keep, total = lax.optimization_barrier((low_keep, total))
    for bit in range(2, leaves.bit_length() - 1):
        low_keep, low_send = part_call(low_keep, [low_got], 2, 1)
        low_got = send_leaf(low_send, 1 << bit)
        total = sum_call(total, [send_leaf(total, 1 << bit)])
    rels = ((0, 0), (1, 2), (2, 1), (3, 3))
    parts = [total] + [send_by_core(total, (0, even), (0, odd)) for even, odd in rels[1:]]
    new_low = low_end_call(kinv_low, low_keep, low_got)
    new_top = top_end_call(parts, rels, kinv_top, m)
    return (new_top, new_low, leaf_proj)


def solution(mesh):
    both = P(("group", "leaf"), None)
    return jax.shard_map(
        per_device,
        mesh=mesh,
        in_specs=(P("group", None), both, both, both, both, both, both, both, P("group", None), both),
        out_specs=(P("group", None), both, both),
        check_vma=False,
    )
```

time: 63.9 us -> 57.7 us (0.903)
  waiting for transfers between devices: 21 us -> 13.8 us
  starting transfers between devices: 25.8 us -> 27.2 us
    ppermute x0 -> x9, starting transfers between devices: none -> 11.4 us  [send_by_core(): return lax.ppermute(x, ('group', 'leaf'), pairs)]
    ppermute x14 -> x6, starting transfers between devices: 21 us -> 13.7 us  [send_leaf(): lax.ppermute(x, 'leaf', [(i, i ^ k) for i in range(lax.axis_size('leaf'))])]
    ppermute x14 -> x6, waiting for transfers between devices: 13.8 us -> 6.56 us  [send_leaf(): lax.ppermute(x, 'leaf', [(i, i ^ k) for i in range(lax.axis_size('leaf'))])]
    ppermute x0 -> x9, waiting for transfers between devices: none -> 6.23 us  [send_by_core(): return lax.ppermute(x, ('group', 'leaf'), pairs)]
    ppermute x5 -> x4, waiting for transfers between devices: 7.18 us -> 1.01 us  [send_group(): lax.ppermute(x, 'group', [(i, i ^ k) for i in range(lax.axis_size('group'...]
    ppermute x5 -> x4, starting transfers between devices: 4.75 us -> 2.08 us  [send_group(): lax.ppermute(x, 'group', [(i, i ^ k) for i in range(lax.axis_size('group'...]
    pallas_call x1, Pallas kernels: 7.45 us -> 6.2 us  [main_call(): pl.pallas_call(functools.partial(main_kernel, len(tops), low_rels), in_sp...]
    pallas_call x5 -> x6, Pallas kernels: 3.69 us -> 4.72 us  [the longest x2 4.47 us: load_call(): pl.pallas_call(functools.partial(load_kernel, turned), in_specs=[HBM] * l...]
  transfers between devices with their start and end apart: 19 -> 19, of which waited for: 11 -> 12; matrix products, arithmetic and copies ran while one was open for 0% -> 0% of each run, Pallas kernels for 12% -> 15%
where the time goes in v3:
time: 57.7 us; the launch traced here: 57.6 us
  starting transfers between devices  27.2 us (47%)
  Pallas kernels  15.6 us (27%)
  waiting for transfers between devices  13.8 us (24%)
  between operations  0.82 us (1%)
    ppermute x6, starting transfers between devices, send_leaf(): lax.ppermute(x, 'leaf', [(i, i ^ k) for i in range(lax.axis_size('leaf'))])  13.7 us
    ppermute x9, starting transfers between devices, send_by_core(): return lax.ppermute(x, ('group', 'leaf'), pairs)  11.4 us
    ppermute x6, waiting for transfers between devices, send_leaf(): lax.ppermute(x, 'leaf', [(i, i ^ k) for i in range(lax.axis_size('leaf'))])  6.56 us
    ppermute x9, waiting for transfers between devices, send_by_core(): return lax.ppermute(x, ('group', 'leaf'), pairs)  6.23 us
    pallas_call x1, Pallas kernels, main_call(): pl.pallas_call(functools.partial(main_kernel, len(tops), low_rels), in_sp...  6.2 us
    pallas_call x2, Pallas kernels, load_call(): pl.pallas_call(functools.partial(load_kernel, turned), in_specs=[HBM] * l...  4.47 us
    ppermute x4, starting transfers between devices, send_group(): lax.ppermute(x, 'group', [(i, i ^ k) for i in range(lax.axis_size('group'...  2.08 us
    pallas_call x1, Pallas kernels, low_call(): pl.pallas_call(functools.partial(low_kernel, leaves), in_specs=[SMEM, VME...  1.58 us
  transfers between devices with their start and end apart: 19, of which 12 were waited for; matrix products, arithmetic and copies ran while one was open for 0% of the time, Pallas kernels for 15%

profile of v3, /device:TPU:0, one launch (start us, length us, event | category | flops | bytes accessed | tf_op | source)
XLA Modules:
  0.0 57.6 jit_solution(16718298503114406938)
XLA Ops:
  1.2 3.7 %collective-permute-start.3 = (bf16[64,512]{1,0:T(8,128)(2,1)}, bf16[64,512]{1,0:T(8,128)(2,1)S(1)}, u32[]{:S(2)}, u32[]{:S(2)}) collective-permute-start(bf16[64,512]{1,0:T(8,128)(2,1)} %param.11), channel_id=1, source_target_pairs={{0,4},{1,5},{2,6},{3,7},{4,0},{5,1},{6,2},{7,3},{8,12},{9,13},{10,... | collective-permute-start | bytes 196616 | tf_op jit(solution)/shard_map/ppermute | solution.py:30
  4.8 1.5 %collective-permute-start.1 = (bf16[256,512]{1,0:T(8,128)(2,1)}, bf16[256,512]{1,0:T(8,128)(2,1)S(1)}, u32[]{:S(2)}, u32[]{:S(2)}) collective-permute-start(bf16[256,512]{1,0:T(8,128)(2,1)} %refs_0_.5), channel_id=1, source_target_pairs={{0,16},{8,24},{16,0},{24,8},{1,17},{9,25},{17,1},{25,9},{2,18},{10... | collective-permute-start | bytes 786440 | tf_op jit(solution)/shard_map/ppermute | solution.py:26
  6.3 1.2 %shard_map.122 = (bf16[1536,128]{1,0:T(8,128)(2,1)S(1)}, bf16[128,1536]{1,0:T(8,128)(2,1)S(1)}) custom-call(bf16[1536,128]{1,0:T(8,128)(2,1)} %refs_0_.4), custom_call_target="tpu_custom_call" | custom-call | flops 20000000000 | bytes 393216 | tf_op jit(solution)/shard_map/pallas_call | solution.py:70
  7.5 1.6 %collective-permute-done.3 = bf16[64,512]{1,0:T(8,128)(2,1)S(1)} collective-permute-done((bf16[64,512]{1,0:T(8,128)(2,1)}, bf16[64,512]{1,0:T(8,128)(2,1)S(1)}, u32[]{:S(2)}, u32[]{:S(2)}) %collective-permute-start.3) | collective-permute-done | bytes 65568 | tf_op jit(solution)/shard_map/ppermute | solution.py:30
  10.1 2.2 %collective-permute-start.5 = (bf16[128,512]{1,0:T(8,128)(2,1)S(1)}, bf16[128,512]{1,0:T(8,128)(2,1)S(1)}, u32[]{:S(2)}, u32[]{:S(2)}) collective-permute-start(bf16[128,512]{1,0:T(8,128)(2,1)S(1)} %constant_dynamic-update-slice_fusion.refs_4_), channel_id=1, source_target_pairs={{0,3},{1,2},{2,1},{3,0},{4,7},{5,6},{6,5},{7,4},{8,11},{9,10},{10,... | collective-permute-start | bytes 393224 | tf_op jit(solution)/shard_map/ppermute | solution.py:30
  13.4 3.3 %shard_map.121 = (bf16[1536,1024]{1,0:T(8,128)(2,1)S(1)}, bf16[1536,1536]{1,0:T(8,128)(2,1)S(1)}, bf16[1024,1536]{1,0:T(8,128)(2,1)S(1)}) custom-call(bf16[1536,1024]{1,0:T(8,128)(2,1)} %refs_0_.3, bf16[1536,1536]{1,0:T(8,128)(2,1)} %refs_1_.1), custom_call_target="tpu_custom_call" | custom-call | flops 20000000000 | bytes 7864320 | tf_op jit(solution)/shard_map/pallas_call | solution.py:70
  16.7 0.9 %collective-permute-done.5.refs_6_ = bf16[128,512]{1,0:T(8,128)(2,1)S(1)} collective-permute-done((bf16[128,512]{1,0:T(8,128)(2,1)S(1)}, bf16[128,512]{1,0:T(8,128)(2,1)S(1)}, u32[]{:S(2)}, u32[]{:S(2)}) %collective-permute-start.5) | collective-permute-done | bytes 131104 | tf_op jit(solution)/shard_map/ppermute | solution.py:30
  17.7 1.3 %collective-permute-done.6.refs_7_ = bf16[128,512]{1,0:T(8,128)(2,1)S(1)} collective-permute-done((bf16[128,512]{1,0:T(8,128)(2,1)S(1)}, bf16[128,512]{1,0:T(8,128)(2,1)S(1)}, u32[]{:S(2)}, u32[]{:S(2)}) %collective-permute-start.6) | collective-permute-done | bytes 131104 | tf_op jit(solution)/shard_map/ppermute | solution.py:30
  19.0 6.2 %shard_map.123 = (bf16[1024,256]{1,0:T(8,128)(2,1)S(1)}, f32[1024,256]{1,0:T(8,128)S(1)}, bf16[1536,512]{1,0:T(8,128)(2,1)S(1)}) custom-call(s32[1,8]{1,0:T(1,128)S(1)} %copy-done.4, s32[1,8]{1,0:T(1,128)S(1)} %copy-done.1, bf16[256,512]{1,0:T(8,128)(2,1)S(1)} %copy-done.2, bf16[256,512]{1,0:T(8,128)(2,1)S(1)} %collective-permute-done.refs_1_, ...), custom_call_target="tpu_custom_call" | custom-call | flops 5033164800 | bytes 7864320 | tf_op jit(solution)/shard_map/pallas_call | solution.py:147
  25.3 1.6 %shard_map.124 = (f32[256,512]{1,0:T(8,128)S(1)}, bf16[256,512]{1,0:T(8,128)(2,1)S(1)}) custom-call(s32[1,8]{1,0:T(1,128)S(1)} %copy-done.1, bf16[1024,1536]{1,0:T(8,128)(2,1)S(1)} %get-tuple-element.38.refs_12_.ct, bf16[1536,512]{1,0:T(8,128)(2,1)S(1)} %get-tuple-element.57.weighted), custom_call_target="tpu_custom_call" | custom-call | flops 805306368 | bytes 3145728 | tf_op jit(solution)/shard_map/pallas_call | solution.py:211
  27.3 1.6 %collective-permute-start.8 = (bf16[512,256]{1,0:T(8,128)(2,1)S(1)}, bf16[512,256]{1,0:T(8,128)(2,1)S(1)}, u32[]{:S(2)}, u32[]{:S(2)}) collective-permute-start(bf16[512,256]{1,0:T(8,128)(2,1)S(1)} %get-tuple-element.55), channel_id=1, source_target_pairs={{0,16},{1,17},{2,18},{3,19},{4,20},{5,21},{6,22},{7,23},{8,9},{9,8... | collective-permute-start | bytes 786440 | tf_op jit(solution)/shard_map/ppermute | solution.py:39
  28.9 1.8 %collective-permute-start.10 = (bf16[256,512]{1,0:T(8,128)(2,1)S(1)}, bf16[256,512]{1,0:T(8,128)(2,1)S(1)}, u32[]{:S(2)}, u32[]{:S(2)}) collective-permute-start(bf16[256,512]{1,0:T(8,128)(2,1)S(1)} %get-tuple-element.61), channel_id=1, source_target_pairs={{0,2},{1,3},{2,0},{3,1},{4,6},{5,7},{6,4},{7,5},{8,9},{9,8},{10,11... | collective-permute-start | bytes 786440 | tf_op jit(solution)/shard_map/ppermute | solution.py:39
  30.7 1.0 %shard_map.126 = bf16[128,512]{1,0:T(8,128)(2,1)} custom-call(bf16[128,1536]{1,0:T(8,128)(2,1)S(1)} %get-tuple-element.56.mt, bf16[1536,512]{1,0:T(8,128)(2,1)S(1)} %get-tuple-element.57.weighted), custom_call_target="tpu_custom_call" | custom-call | flops 20000000000 | bytes 1572864 | tf_op jit(solution)/shard_map/pallas_call | solution.py:197
  31.7 2.0 %collective-permute-done.8.refs_0_ = bf16[512,256]{1,0:T(8,128)(2,1)S(1)} collective-permute-done((bf16[512,256]{1,0:T(8,128)(2,1)S(1)}, bf16[512,256]{1,0:T(8,128)(2,1)S(1)}, u32[]{:S(2)}, u32[]{:S(2)}) %collective-permute-start.8) | collective-permute-done | bytes 262176 | tf_op jit(solution)/shard_map/ppermute | solution.py:39
  34.7 1.5 %collective-permute-start.11 = (bf16[128,256]{1,0:T(8,128)(2,1)S(1)}, bf16[128,256]{1,0:T(8,128)(2,1)S(1)}, u32[]{:S(2)}, u32[]{:S(2)}) collective-permute-start(bf16[128,256]{1,0:T(8,128)(2,1)S(1)} %get-tuple-element.64), channel_id=1, source_target_pairs={{0,2},{1,3},{2,0},{3,1},{4,6},{5,7},{6,4},{7,5},{8,10},{9,11},{10,... | collective-permute-start | bytes 196616 | tf_op jit(solution)/shard_map/ppermute | solution.py:39
  36.2 1.2 %collective-permute-start.12 = (bf16[128,256]{1,0:T(8,128)(2,1)S(1)}, bf16[128,256]{1,0:T(8,128)(2,1)S(1)}, u32[]{:S(2)}, u32[]{:S(2)}) collective-permute-start(bf16[128,256]{1,0:T(8,128)(2,1)S(1)} %get-tuple-element.66), channel_id=1, source_target_pairs={{0,3},{1,2},{2,1},{3,0},{4,7},{5,6},{6,5},{7,4},{8,26},{9,27},{10,... | collective-permute-start | bytes 196616 | tf_op jit(solution)/shard_map/ppermute | solution.py:39
  39.4 2.6 %collective-permute-done.12.refs_2_ = bf16[128,256]{1,0:T(8,128)(2,1)S(1)} collective-permute-done((bf16[128,256]{1,0:T(8,128)(2,1)S(1)}, bf16[128,256]{1,0:T(8,128)(2,1)S(1)}, u32[]{:S(2)}, u32[]{:S(2)}) %collective-permute-start.12) | collective-permute-done | bytes 65568 | tf_op jit(solution)/shard_map/ppermute | solution.py:39
  42.0 3.5 %collective-permute-start.13 = (bf16[128,256]{1,0:T(8,128)(2,1)S(1)}, bf16[128,256]{1,0:T(8,128)(2,1)S(1)}, u32[]{:S(2)}, u32[]{:S(2)}) collective-permute-start(bf16[128,256]{1,0:T(8,128)(2,1)S(1)} %shard_map.129.keep), channel_id=1, source_target_pairs={{0,4},{1,5},{2,6},{3,7},{4,0},{5,1},{6,2},{7,3},{8,12},{9,13},{10,... | collective-permute-start | bytes 196616 | tf_op jit(solution)/shard_map/ppermute | solution.py:30
  45.5 2.2 %collective-permute-done.13.refs_0_ = bf16[128,256]{1,0:T(8,128)(2,1)S(1)} collective-permute-done((bf16[128,256]{1,0:T(8,128)(2,1)S(1)}, bf16[128,256]{1,0:T(8,128)(2,1)S(1)}, u32[]{:S(2)}, u32[]{:S(2)}) %collective-permute-start.13) | collective-permute-done | bytes 65568 | tf_op jit(solution)/shard_map/ppermute | solution.py:30
  47.8 2.1 %collective-permute-start.14 = (bf16[128,256]{1,0:T(8,128)(2,1)S(1)}, bf16[128,256]{1,0:T(8,128)(2,1)S(1)}, u32[]{:S(2)}, u32[]{:S(2)}) collective-permute-start(bf16[128,256]{1,0:T(8,128)(2,1)S(1)} %shard_map.130.refs_0_), channel_id=1, source_target_pairs={{0,1},{1,0},{2,3},{3,2},{4,5},{5,4},{6,7},{7,6},{8,10},{9,11},{10,... | collective-permute-start | bytes 196616 | tf_op jit(solution)/shard_map/ppermute | solution.py:39
  49.9 1.5 %collective-permute-start.16 = (bf16[128,256]{1,0:T(8,128)(2,1)S(1)}, bf16[128,256]{1,0:T(8,128)(2,1)S(1)}, u32[]{:S(2)}, u32[]{:S(2)}) collective-permute-start(bf16[128,256]{1,0:T(8,128)(2,1)S(1)} %shard_map.130.refs_0_), channel_id=1, source_target_pairs={{0,3},{1,2},{2,1},{3,0},{4,7},{5,6},{6,5},{7,4},{8,11},{9,10},{10,... | collective-permute-start | bytes 196616 | tf_op jit(solution)/shard_map/ppermute | solution.py:39
  51.5 3.0 %collective-permute-start.18 = (bf16[64,512]{1,0:T(8,128)(2,1)S(1)}, bf16[64,512]{1,0:T(8,128)(2,1)S(1)}, u32[]{:S(2)}, u32[]{:S(2)}) collective-permute-start(bf16[64,512]{1,0:T(8,128)(2,1)S(1)} %get-tuple-element.71), channel_id=1, source_target_pairs={{0,4},{1,5},{2,6},{3,7},{4,0},{5,1},{6,2},{7,3},{8,12},{9,13},{10,... | collective-permute-start | bytes 196616 | tf_op jit(solution)/shard_map/ppermute | solution.py:30
  55.0 1.2 %shard_map.131 = f32[256,512]{1,0:T(8,128)} custom-call(f32[256,64]{1,0:T(8,128)S(1)} %copy.13.kinv, bf16[128,256]{1,0:T(8,128)(2,1)S(1)} %shard_map.130.refs_0_, bf16[128,256]{1,0:T(8,128)(2,1)S(1)} %collective-permute-done.14.refs_1_, bf16[128,256]{1,0:T(8,128)(2,1)S(1)} %collective-permute-done.15.refs_2_, ...), custom_call_target="tpu_custom_call" | custom-call | flops 100663296 | bytes 1048576 | tf_op jit(solution)/shard_map/pallas_call | solution.py:316
  56.7 0.9 %shard_map.133 = f32[64,512]{1,0:T(8,128)} custom-call(f32[64,64]{1,0:T(8,128)S(1)} %copy-done, f32[64,512]{1,0:T(8,128)S(1)} %get-tuple-element.70.keep, bf16[64,512]{1,0:T(8,128)(2,1)S(1)} %collective-permute-done.18.got), custom_call_target="tpu_custom_call" | custom-call | flops 25165824 | bytes 262144 | tf_op jit(solution)/shard_map/pallas_call | solution.py:288
  (44 shorter events, 7.2 us)
Async XLA Ops:
  0.6 4.2 %collective-permute-start = (bf16[256,512]{1,0:T(8,128)(2,1)}, bf16[256,512]{1,0:T(8,128)(2,1)S(1)}, u32[]{:S(2)}, u32[]{:S(2)}) collective-permute-start(bf16[256,512]{1,0:T(8,128)(2,1)} %refs_0_.5), channel_id=1, source_target_pairs={{0,8},{8,0},{16,24},{24,16},{1,9},{9,1},{17,25},{25,17},{2,10},{10... | collective-permute-start | bytes 786440 | tf_op jit(solution)/shard_map/ppermute | solution.py:26
  1.2 8.0 %collective-permute-start.3 = (bf16[64,512]{1,0:T(8,128)(2,1)}, bf16[64,512]{1,0:T(8,128)(2,1)S(1)}, u32[]{:S(2)}, u32[]{:S(2)}) collective-permute-start(bf16[64,512]{1,0:T(8,128)(2,1)} %param.11), channel_id=1, source_target_pairs={{0,4},{1,5},{2,6},{3,7},{4,0},{5,1},{6,2},{7,3},{8,12},{9,13},{10,... | collective-permute-start | bytes 196616 | tf_op jit(solution)/shard_map/ppermute | solution.py:30
  4.8 8.6 %collective-permute-start.1 = (bf16[256,512]{1,0:T(8,128)(2,1)}, bf16[256,512]{1,0:T(8,128)(2,1)S(1)}, u32[]{:S(2)}, u32[]{:S(2)}) collective-permute-start(bf16[256,512]{1,0:T(8,128)(2,1)} %refs_0_.5), channel_id=1, source_target_pairs={{0,16},{8,24},{16,0},{24,8},{1,17},{9,25},{17,1},{25,9},{2,18},{10... | collective-permute-start | bytes 786440 | tf_op jit(solution)/shard_map/ppermute | solution.py:26
  9.1 9.8 %copy-start.1 = (s32[1,8]{1,0:T(1,128)S(1)}, s32[1,8]{1,0:T(1,128)}, u32[]{:S(2)}) copy-start(s32[1,8]{1,0:T(1,128)} %anc_low.3) | copy-start | bytes 100
  9.1 9.8 %copy-start.2 = (bf16[256,512]{1,0:T(8,128)(2,1)S(1)}, bf16[256,512]{1,0:T(8,128)(2,1)}, u32[]{:S(2)}) copy-start(bf16[256,512]{1,0:T(8,128)(2,1)} %refs_0_.5) | copy-start | bytes 786436
  9.1 9.8 %copy-start.3 = (bf16[128,512]{1,0:T(8,128)(2,1)S(1)}, bf16[128,512]{1,0:T(8,128)(2,1)}, u32[]{:S(2)}) copy-start(bf16[128,512]{1,0:T(8,128)(2,1)} %refs_11_.1) | copy-start | bytes 393220
  9.2 7.6 %collective-permute-start.4 = (bf16[128,512]{1,0:T(8,128)(2,1)S(1)}, bf16[128,512]{1,0:T(8,128)(2,1)S(1)}, u32[]{:S(2)}, u32[]{:S(2)}) collective-permute-start(bf16[128,512]{1,0:T(8,128)(2,1)S(1)} %constant_dynamic-update-slice_fusion.refs_4_), channel_id=1, source_target_pairs={{0,2},{1,3},{2,0},{3,1},{4,6},{5,7},{6,4},{7,5},{8,10},{9,11},{10,... | collective-permute-start | bytes 393224 | tf_op jit(solution)/shard_map/ppermute | solution.py:30
  10.1 7.6 %collective-permute-start.5 = (bf16[128,512]{1,0:T(8,128)(2,1)S(1)}, bf16[128,512]{1,0:T(8,128)(2,1)S(1)}, u32[]{:S(2)}, u32[]{:S(2)}) collective-permute-start(bf16[128,512]{1,0:T(8,128)(2,1)S(1)} %constant_dynamic-update-slice_fusion.refs_4_), channel_id=1, source_target_pairs={{0,3},{1,2},{2,1},{3,0},{4,7},{5,6},{6,5},{7,4},{8,11},{9,10},{10,... | collective-permute-start | bytes 393224 | tf_op jit(solution)/shard_map/ppermute | solution.py:30
  12.3 6.7 %collective-permute-start.6 = (bf16[128,512]{1,0:T(8,128)(2,1)S(1)}, bf16[128,512]{1,0:T(8,128)(2,1)S(1)}, u32[]{:S(2)}, u32[]{:S(2)}) collective-permute-start(bf16[128,512]{1,0:T(8,128)(2,1)S(1)} %constant_dynamic-update-slice_fusion.refs_4_), channel_id=1, source_target_pairs={{0,1},{1,0},{2,3},{3,2},{4,5},{5,4},{6,7},{7,6},{8,9},{9,8},{10,11... | collective-permute-start | bytes 393224 | tf_op jit(solution)/shard_map/ppermute | solution.py:30
  13.4 5.6 %collective-permute-start.2 = (bf16[256,512]{1,0:T(8,128)(2,1)S(1)}, bf16[256,512]{1,0:T(8,128)(2,1)S(1)}, u32[]{:S(2)}, u32[]{:S(2)}) collective-permute-start(bf16[256,512]{1,0:T(8,128)(2,1)S(1)} %collective-permute-done.1.refs_2_), channel_id=1, source_target_pairs={{0,8},{8,0},{16,24},{24,16},{1,9},{9,1},{17,25},{25,17},{2,10},{10... | collective-permute-start | bytes 786440 | tf_op jit(solution)/shard_map/ppermute | solution.py:26
  25.2 2.0 %collective-permute-start.7 = (bf16[1024,256]{1,0:T(8,128)(2,1)S(1)}, bf16[1024,256]{1,0:T(8,128)(2,1)S(1)}, u32[]{:S(2)}, u32[]{:S(2)}) collective-permute-start(bf16[1024,256]{1,0:T(8,128)(2,1)S(1)} %get-tuple-element.49), channel_id=1, source_target_pairs={{0,8},{8,0},{16,24},{24,16},{1,9},{9,1},{17,25},{25,17},{2,10},{10... | collective-permute-start | bytes 1572872 | tf_op jit(solution)/shard_map/ppermute | solution.py:26
  27.3 27.1 %copy-start.5 = (f32[256,64]{0,1:T(8,128)S(1)}, f32[256,64]{0,1:T(8,128)}, u32[]{:S(2)}) copy-start(f32[256,64]{0,1:T(8,128)} %param.18) | copy-start | bytes 196612
  27.3 6.4 %collective-permute-start.8 = (bf16[512,256]{1,0:T(8,128)(2,1)S(1)}, bf16[512,256]{1,0:T(8,128)(2,1)S(1)}, u32[]{:S(2)}, u32[]{:S(2)}) collective-permute-start(bf16[512,256]{1,0:T(8,128)(2,1)S(1)} %get-tuple-element.55), channel_id=1, source_target_pairs={{0,16},{1,17},{2,18},{3,19},{4,20},{5,21},{6,22},{7,23},{8,9},{9,8... | collective-permute-start | bytes 786440 | tf_op jit(solution)/shard_map/ppermute | solution.py:39
  28.9 9.3 %collective-permute-start.10 = (bf16[256,512]{1,0:T(8,128)(2,1)S(1)}, bf16[256,512]{1,0:T(8,128)(2,1)S(1)}, u32[]{:S(2)}, u32[]{:S(2)}) collective-permute-start(bf16[256,512]{1,0:T(8,128)(2,1)S(1)} %get-tuple-element.61), channel_id=1, source_target_pairs={{0,2},{1,3},{2,0},{3,1},{4,6},{5,7},{6,4},{7,5},{8,9},{9,8},{10,11... | collective-permute-start | bytes 786440 | tf_op jit(solution)/shard_map/ppermute | solution.py:39
  31.7 25.0 %copy-start = (f32[64,64]{1,0:T(8,128)S(1)}, f32[64,64]{1,0:T(8,128)}, u32[]{:S(2)}) copy-start(f32[64,64]{1,0:T(8,128)} %kinv.2) | copy-start | bytes 49156
  33.8 4.3 %collective-permute-start.9 = (bf16[128,256]{1,0:T(8,128)(2,1)S(1)}, bf16[128,256]{1,0:T(8,128)(2,1)S(1)}, u32[]{:S(2)}, u32[]{:S(2)}) collective-permute-start(bf16[128,256]{1,0:T(8,128)(2,1)S(1)} %get-tuple-element.59), channel_id=1, source_target_pairs={{0,1},{1,0},{2,3},{3,2},{4,5},{5,4},{6,7},{7,6},{8,24},{9,25},{10,... | collective-permute-start | bytes 196616 | tf_op jit(solution)/shard_map/ppermute | solution.py:39
  34.7 4.7 %collective-permute-start.11 = (bf16[128,256]{1,0:T(8,128)(2,1)S(1)}, bf16[128,256]{1,0:T(8,128)(2,1)S(1)}, u32[]{:S(2)}, u32[]{:S(2)}) collective-permute-start(bf16[128,256]{1,0:T(8,128)(2,1)S(1)} %get-tuple-element.64), channel_id=1, source_target_pairs={{0,2},{1,3},{2,0},{3,1},{4,6},{5,7},{6,4},{7,5},{8,10},{9,11},{10,... | collective-permute-start | bytes 196616 | tf_op jit(solution)/shard_map/ppermute | solution.py:39
  36.2 5.8 %collective-permute-start.12 = (bf16[128,256]{1,0:T(8,128)(2,1)S(1)}, bf16[128,256]{1,0:T(8,128)(2,1)S(1)}, u32[]{:S(2)}, u32[]{:S(2)}) collective-permute-start(bf16[128,256]{1,0:T(8,128)(2,1)S(1)} %get-tuple-element.66), channel_id=1, source_target_pairs={{0,3},{1,2},{2,1},{3,0},{4,7},{5,6},{6,5},{7,4},{8,26},{9,27},{10,... | collective-permute-start | bytes 196616 | tf_op jit(solution)/shard_map/ppermute | solution.py:39
  38.2 13.2 %collective-permute-start.17 = (bf16[128,512]{1,0:T(8,128)(2,1)S(1)}, bf16[128,512]{1,0:T(8,128)(2,1)S(1)}, u32[]{:S(2)}, u32[]{:S(2)}) collective-permute-start(bf16[128,512]{1,0:T(8,128)(2,1)S(1)} %get-tuple-element.69), channel_id=1, source_target_pairs={{0,1},{1,0},{2,3},{3,2},{4,5},{5,4},{6,7},{7,6},{8,10},{9,11},{10,... | collective-permute-start | bytes 393224 | tf_op jit(solution)/shard_map/ppermute | solution.py:39
  42.0 5.7 %collective-permute-start.13 = (bf16[128,256]{1,0:T(8,128)(2,1)S(1)}, bf16[128,256]{1,0:T(8,128)(2,1)S(1)}, u32[]{:S(2)}, u32[]{:S(2)}) collective-permute-start(bf16[128,256]{1,0:T(8,128)(2,1)S(1)} %shard_map.129.keep), channel_id=1, source_target_pairs={{0,4},{1,5},{2,6},{3,7},{4,0},{5,1},{6,2},{7,3},{8,12},{9,13},{10,... | collective-permute-start | bytes 196616 | tf_op jit(solution)/shard_map/ppermute | solution.py:30
  47.8 6.8 %collective-permute-start.14 = (bf16[128,256]{1,0:T(8,128)(2,1)S(1)}, bf16[128,256]{1,0:T(8,128)(2,1)S(1)}, u32[]{:S(2)}, u32[]{:S(2)}) collective-permute-start(bf16[128,256]{1,0:T(8,128)(2,1)S(1)} %shard_map.130.refs_0_), channel_id=1, source_target_pairs={{0,1},{1,0},{2,3},{3,2},{4,5},{5,4},{6,7},{7,6},{8,10},{9,11},{10,... | collective-permute-start | bytes 196616 | tf_op jit(solution)/shard_map/ppermute | solution.py:39
  49.9 4.7 %collective-permute-start.15 = (bf16[128,256]{1,0:T(8,128)(2,1)S(1)}, bf16[128,256]{1,0:T(8,128)(2,1)S(1)}, u32[]{:S(2)}, u32[]{:S(2)}) collective-permute-start(bf16[128,256]{1,0:T(8,128)(2,1)S(1)} %shard_map.130.refs_0_), channel_id=1, source_target_pairs={{0,2},{1,3},{2,0},{3,1},{4,6},{5,7},{6,4},{7,5},{8,9},{9,8},{10,11... | collective-permute-start | bytes 196616 | tf_op jit(solution)/shard_map/ppermute | solution.py:39
  49.9 5.2 %collective-permute-start.16 = (bf16[128,256]{1,0:T(8,128)(2,1)S(1)}, bf16[128,256]{1,0:T(8,128)(2,1)S(1)}, u32[]{:S(2)}, u32[]{:S(2)}) collective-permute-start(bf16[128,256]{1,0:T(8,128)(2,1)S(1)} %shard_map.130.refs_0_), channel_id=1, source_target_pairs={{0,3},{1,2},{2,1},{3,0},{4,7},{5,6},{6,5},{7,4},{8,11},{9,10},{10,... | collective-permute-start | bytes 196616 | tf_op jit(solution)/shard_map/ppermute | solution.py:39
  51.5 5.2 %collective-permute-start.18 = (bf16[64,512]{1,0:T(8,128)(2,1)S(1)}, bf16[64,512]{1,0:T(8,128)(2,1)S(1)}, u32[]{:S(2)}, u32[]{:S(2)}) collective-permute-start(bf16[64,512]{1,0:T(8,128)(2,1)S(1)} %get-tuple-element.71), channel_id=1, source_target_pairs={{0,4},{1,5},{2,6},{3,7},{4,0},{5,1},{6,2},{7,3},{8,12},{9,13},{10,... | collective-permute-start | bytes 196616 | tf_op jit(solution)/shard_map/ppermute | solution.py:30
  (2 other events, 16.7 us)

commit v4 on v3

--- a/solution.py
+++ b/solution.py
@@ -46,80 +46,114 @@
             got = send_leaf(x, 1 << bit)
         x = jnp.concatenate([x, got], axis=0)
         rels = rels + [r ^ (1 << bit) for r in rels]
-    return [(x, rels)] + [(send_leaf(x, k), [r ^ k for r in rels]) for k in (2, 3, 1)]
-
-
-def load_kernel(turned, *refs):
+    return [(x, rels, rels)] + [(send_by_core(x, (0, a), (0, b)), [r ^ a for r in rels], [r ^ b for r in rels]) for a, b in ((3, 3), (2, 1), (1, 2))]
+
+
+def load_kernel(turned, step, *refs):
     n = len(turned)
     sources, copies, turns, sem = refs[:n], refs[n : 2 * n], list(refs[2 * n : -1]), refs[-1]
-    moves = [pltpu.make_async_copy(s, d, sem.at[i]) for i, (s, d) in enumerate(zip(sources, copies))]
-    for move in moves:
-        move.start()
-    for move, copy, turn in zip(moves, copies, turned):
+    pieces = []
+    for source, copy, turn in zip(sources, copies, turned):
+        out = turns.pop(0) if turn else None
+        for i in range(source.shape[0] // step):
+            at = slice(i * step, (i + 1) * step)
+            move = pltpu.make_async_copy(source.at[at, :], copy.at[at, :], sem.at[len(pieces)])
+            move.start()
+            pieces.append((move, copy, at, out))
+    for move, copy, at, out in pieces:
         move.wait()
-        if turn:
-            out = turns.pop(0)
-            step = 512
-            for i in range(copy.shape[0] // step):
-                at = slice(i * step, (i + 1) * step)
-                out[:, at] = copy[at, :].T
+        if out is not None:
+            out[:, at] = copy[at, :].T
 
 
 def load_call(arrays, turned):
     shapes = [a.shape for a in arrays] + [a.shape[::-1] for a, t in zip(arrays, turned) if t]
-    return pl.pallas_call(
-        functools.partial(load_kernel, turned),
+    step = 512
+    return pl.pallas_call(
+        functools.partial(load_kernel, turned, step),
         in_specs=[HBM] * len(arrays),
         out_specs=[VMEM] * len(shapes),
         out_shape=[pltpu.VMEM(s, BF16) for s in shapes],
-        scratch_shapes=[pltpu.SemaphoreType.DMA((len(arrays),))],
+        scratch_shapes=[pltpu.SemaphoreType.DMA((sum(a.shape[0] // step for a in arrays),))],
         compiler_params=params(8),
         cost_estimate=cost(FILL, 2 * sum(a.size for a in arrays)),
     )(*[pltpu.with_memory_space_constraint(a, pltpu.HBM) for a in arrays])
 
 
-def main_kernel(n_top, low_rels, anc_top, anc_low, *refs):
-    n_low = len(low_rels)
-    tops, lows = refs[:n_top], refs[n_top : n_top + n_low]
-    coupling, mass, modes, coef, ct = refs[n_top + n_low : n_top + n_low + 5]
-    send, keep, weighted = refs[n_top + n_low + 5 : n_top + n_low + 8]
-    slot_top, slot_low, stacked, shapes, loads = refs[n_top + n_low + 8 :]
-    group, leaf = lax.axis_index("group"), lax.axis_index("leaf")
-    top_slots, low_slots = anc_top.shape[1], anc_low.shape[1]
-    slots = top_slots + low_slots
+def fill_slots(slot_of, anc):
+    for b in range(slot_of.shape[0]):
+        slot_of[b] = anc.shape[1]
+    for j in range(anc.shape[1]):
+        slot_of[anc[0, j]] = j
+
+
+def first_kernel(n_top, anc_top, *refs):
+    tops = refs[:n_top]
+    coupling, modes, coef, part, slot_top, stacked = refs[n_top:]
+    group = lax.axis_index("group")
+    slots = anc_top.shape[1]
     sr = stacked.shape[0] // (slots + 1)
     per_group = tops[0].shape[0] // sr
-    rows = mass.shape[0]
-    step = 512
-
-    for b in range(slot_top.shape[0]):
-        slot_top[b] = slots
-    for b in range(slot_low.shape[0]):
-        slot_low[b] = slots
-    for j in range(top_slots):
-        slot_top[anc_top[0, j]] = j
-    for j in range(low_slots):
-        slot_low[anc_low[0, j]] = top_slots + j
+    fill_slots(slot_top, anc_top)
     for r, piece in enumerate(tops):
         for p in range(per_group):
             at = pl.multiple_of(slot_top[(group ^ r) * per_group + p] * sr, sr)
             stacked[pl.ds(at, sr), :] = piece[p * sr : (p + 1) * sr, :]
+    step = 512
+    for i in range(part.shape[0] // step):
+        at = slice(i * step, (i + 1) * step)
+        part[at, :] = jnp.dot(modes[at, :], coef[...], preferred_element_type=F32) - jnp.dot(
+            coupling[at, : slots * sr], stacked[: slots * sr, :], preferred_element_type=F32
+        )
+
+
+def first_call(anc_top, tops, coupling, modes, coef, sr):
+    rows, m = coupling.shape[0], coef.shape[1]
+    top_rows = anc_top.shape[1] * sr
+    return pl.pallas_call(
+        functools.partial(first_kernel, len(tops)),
+        in_specs=[SMEM] + [VMEM] * (len(tops) + 3),
+        out_specs=VMEM,
+        out_shape=jax.ShapeDtypeStruct((rows, m), F32),
+        scratch_shapes=[
+            pltpu.SMEM((len(tops) * tops[0].shape[0] // sr,), jnp.int32),
+            pltpu.VMEM((top_rows + sr, m), BF16),
+        ],
+        compiler_params=params(8),
+        cost_estimate=cost(0, 0),
+    )(anc_top, *tops, coupling, modes, coef)
+
+
+def main_kernel(per_group, low_rels, anc_top, anc_low, *refs):
+    n_low = len(low_rels)
+    lows = refs[:n_low]
+    part, coupling, mass, ct, send, keep, weighted = refs[n_low : n_low + 7]
+    slot_top, slot_low, stacked, shapes, loads = refs[n_low + 7 :]
+    group, leaf = lax.axis_index("group"), lax.axis_index("leaf")
+    top_slots, low_slots = anc_top.shape[1], anc_low.shape[1]
+    sr = stacked.shape[0] // (low_slots + 1)
+    top_rows = top_slots * sr
+    rows = mass.shape[0]
+    step = 512
+
+    fill_slots(slot_top, anc_top)
+    fill_slots(slot_low, anc_low)
+    even = (group & 1) == 0
     for piece, rels in zip(lows, low_rels):
-        for p, r in enumerate(rels):
-            at = pl.multiple_of(slot_low[leaf ^ r] * sr, sr)
+        for p, (r_even, r_odd) in enumerate(zip(*rels)):
+            at = pl.multiple_of(slot_low[leaf ^ jnp.where(even, r_even, r_odd)] * sr, sr)
             stacked[pl.ds(at, sr), :] = piece[p * sr : (p + 1) * sr, :]
     for i in range(rows // step):
         at = slice(i * step, (i + 1) * step)
         shapes[at, :] = (
-            jnp.dot(modes[at, :], coef[...], preferred_element_type=F32)
-            - jnp.dot(coupling[at, :], stacked[: slots * sr, :], preferred_element_type=F32)
+            part[at, :]
+            - jnp.dot(coupling[at, top_rows:], stacked[: low_slots * sr, :], preferred_element_type=F32)
         ).astype(BF16)
     for i in range(rows // step):
         at = slice(i * step, (i + 1) * step)
         weighted[at, :] = jnp.dot(mass[at, :], shapes[...], preferred_element_type=F32).astype(BF16)
     width = weighted.shape[1] // 2
     core, near, high = group & 1, leaf & 1, (leaf >> 1) & 1
-    top_rows = top_slots * sr
     for q in range(2):
         loads[q, :top_rows, :] = jnp.dot(
             ct[:top_rows, :], weighted[:, q * width : (q + 1) * width], preferred_element_type=F32
@@ -132,21 +166,19 @@
                 q = jnp.where(owner == 0, second, first) ^ near
                 for p in range(per_group):
                     block = (2 * far + owner) * per_group + (p ^ (high * (per_group // 2)))
-                    slot = jnp.minimum(slot_top[block], top_slots)
-                    at = pl.ds(pl.multiple_of(slot * sr, sr), sr)
+                    at = pl.ds(pl.multiple_of(slot_top[block] * sr, sr), sr)
                     to = ((2 * first + second) * per_group + p) * sr
                     out[to : to + sr, :] = loads[q, at, :].astype(out.dtype)
 
 
-def main_call(anc_top, anc_low, tops, lows, low_rels, coupling, mass, modes, coef, ct, sr, leaves):
-    rows, sw = coupling.shape
-    m = coef.shape[1]
-    half_rows = len(tops) * tops[0].shape[0] // 2
-    top_rows = anc_top.shape[1] * sr
-    flops = 2 * m * rows * (sw + rows + modes.shape[1] + top_rows)
-    return pl.pallas_call(
-        functools.partial(main_kernel, len(tops), low_rels),
-        in_specs=[SMEM, SMEM] + [VMEM] * (len(tops) + len(lows) + 5),
+def main_call(anc_top, anc_low, part, lows, low_rels, coupling, mass, ct, sr, leaves, groups, per_group):
+    rows, m = part.shape
+    half_rows = groups * per_group * sr // 2
+    top_rows, low_rows = anc_top.shape[1] * sr, anc_low.shape[1] * sr
+    flops = 2 * m * rows * (low_rows + rows + top_rows)
+    return pl.pallas_call(
+        functools.partial(main_kernel, per_group, low_rels),
+        in_specs=[SMEM, SMEM] + [VMEM] * (len(lows) + 4),
         out_specs=[VMEM, VMEM, VMEM],
         out_shape=[
             jax.ShapeDtypeStruct((2 * half_rows, m // 2), BF16),
@@ -154,15 +186,15 @@
             jax.ShapeDtypeStruct((rows, m), BF16),
         ],
         scratch_shapes=[
-            pltpu.SMEM((len(tops) * tops[0].shape[0] // sr,), jnp.int32),
+            pltpu.SMEM((groups * per_group,), jnp.int32),
             pltpu.SMEM((leaves,), jnp.int32),
-            pltpu.VMEM((sw + sr, m), BF16),
+            pltpu.VMEM((low_rows + sr, m), BF16),
             pltpu.VMEM((rows, m), BF16),
             pltpu.VMEM((2, top_rows + sr, m // 2), F32),
         ],
         compiler_params=params(12),
-        cost_estimate=cost(flops, 2 * rows * (sw + rows)),
-    )(anc_top, anc_low, *tops, *lows, coupling, mass, modes, coef, ct)
+        cost_estimate=cost(flops, 2 * rows * (low_rows + rows)),
+    )(anc_top, anc_low, *lows, part, coupling, mass, ct)
 
 
 def low_kernel(leaves, anc_low, ct, weighted, keep, send, slot_low, loads):
@@ -172,10 +204,7 @@
     bits = leaves.bit_length() - 1
     leaf = lax.axis_index("leaf")
     even = (lax.axis_index("group") & 1) == 0
-    for k in range(leaves):
-        slot_low[k] = slots
-    for j in range(slots):
-        slot_low[anc_low[0, j]] = j
+    fill_slots(slot_low, anc_low)
     loads[: slots * sr, :] = jnp.dot(ct[start:, :], weighted[...], preferred_element_type=F32)
     loads[slots * sr :, :] = jnp.zeros((sr, loads.shape[1]), F32)
     for first, out in enumerate((keep, send)):
@@ -334,24 +363,25 @@
     far_low = send_leaf(low_modes, leaves // 2)
     near_top, to_send = lax.optimization_barrier((near_top, top_modes))
     far_top = send_group(to_send, 2)
-    leaf_modes, mt = load_call((leaf_modes,), (True,))
-    far_low, mt = lax.optimization_barrier((far_low, mt))
+    coupling, leaf_modes, ct, mt = load_call((coupling, leaf_modes), (True, True))
+    far_low, ct = lax.optimization_barrier((far_low, ct))
     held = gather_leaf(low_modes, far_low)
-    coupling, leaf_mass, ct = load_call((coupling, leaf_mass), (True, False))
+    (leaf_mass,) = load_call((leaf_mass,), (False,))
     tops = [top_modes, near_top, far_top, send_group(far_top, 1)]
+    part = first_call(anc_top, tops, coupling, leaf_modes, leaf_coef, sr)
     send, keep, weighted = main_call(
         anc_top,
         anc_low,
-        tops,
-        [a for a, _ in held],
-        [r for _, r in held],
+        part,
+        [h[0] for h in held],
+        [h[1:] for h in held],
         coupling,
         leaf_mass,
-        leaf_modes,
-        leaf_coef,
         ct,
         sr,
         leaves,
+        len(tops),
+        top_modes.shape[0] // sr,
     )
     got = send_group(send, 1)
     low_keep, low_send = low_call(anc_low, ct, weighted, sr, leaves)
@@ -365,7 +395,7 @@
     keep, *sends = part_call(keep, [got], 4, 1)
     got = [
         send_by_core(x, *there)
-        for x, there in zip(sends, (((0, 2), (0, 2)), ((0, 1), (2, 0)), ((0, 3), (2, 2))))
+        for x, there in zip(sends[::-1], (((0, 3), (2, 2)), ((0, 1), (2, 0)), ((0, 2), (0, 2))))
     ]
     low_keep, got[1] = lax.optimization_barrier((low_keep, got[1]))
     low_keep, low_send = part_call(low_keep, [low_got], 2, 1)

time: 57.7 us -> 55.4 us (0.960)
  waiting for transfers between devices: 13.8 us -> 9.86 us
  Pallas kernels: 15.6 us -> 16.9 us
    ppermute x6 -> x3, waiting for transfers between devices: 6.56 us -> 2.55 us  [send_leaf(): lax.ppermute(x, 'leaf', [(i, i ^ k) for i in range(lax.axis_size('leaf'))])]
    ppermute x9 -> x12, starting transfers between devices: 11.4 us -> 15.4 us  [send_by_core(): return lax.ppermute(x, ('group', 'leaf'), pairs)]
    ppermute x6 -> x3, starting transfers between devices: 13.7 us -> 9.69 us  [send_leaf(): lax.ppermute(x, 'leaf', [(i, i ^ k) for i in range(lax.axis_size('leaf'))])]
    pallas_call x3 -> x4, Pallas kernels: 10.7 us -> 11.9 us  [the longest x1 5.01 us: main_call(): pl.pallas_call(functools.partial(main_kernel, per_group, low_rels), in_sp...]
    ppermute x9 -> x12, waiting for transfers between devices: 6.23 us -> 6.6 us  [send_by_core(): return lax.ppermute(x, ('group', 'leaf'), pairs)]
  transfers between devices with their start and end apart: 19 -> 19, of which waited for: 12 -> 9; matrix products, arithmetic and copies ran while one was open for 0% -> 0% of each run, Pallas kernels for 15% -> 20%
where the time goes in v4:
time: 55.4 us; the launch traced here: 55.2 us
  starting transfers between devices  27.6 us (50%)
  Pallas kernels  16.9 us (31%)
  waiting for transfers between devices  9.86 us (18%)
  between operations  0.84 us (2%)
    ppermute x12, starting transfers between devices, send_by_core(): return lax.ppermute(x, ('group', 'leaf'), pairs)  15.4 us
    ppermute x3, starting transfers between devices, send_leaf(): lax.ppermute(x, 'leaf', [(i, i ^ k) for i in range(lax.axis_size('leaf'))])  9.69 us
    ppermute x12, waiting for transfers between devices, send_by_core(): return lax.ppermute(x, ('group', 'leaf'), pairs)  6.6 us
    pallas_call x1, Pallas kernels, main_call(): pl.pallas_call(functools.partial(main_kernel, per_group, low_rels), in_sp...  5.01 us
    pallas_call x2, Pallas kernels, load_call(): pl.pallas_call(functools.partial(load_kernel, turned, step), in_specs=[HB...  4.9 us
    ppermute x3, waiting for transfers between devices, send_leaf(): lax.ppermute(x, 'leaf', [(i, i ^ k) for i in range(lax.axis_size('leaf'))])  2.55 us
    ppermute x4, starting transfers between devices, send_group(): lax.ppermute(x, 'group', [(i, i ^ k) for i in range(lax.axis_size('group'...  2.42 us
    pallas_call x1, Pallas kernels, first_call(): pl.pallas_call(functools.partial(first_kernel, len(tops)), in_specs=[SMEM...  1.98 us
  transfers between devices with their start and end apart: 19, of which 9 were waited for; matrix products, arithmetic and copies ran while one was open for 0% of the time, Pallas kernels for 20%

profile of v4, /device:TPU:0, one launch (start us, length us, event | category | flops | bytes accessed | tf_op | source)
XLA Modules:
  0.0 55.2 jit_solution(3347682528353148623)
XLA Ops:
  1.2 3.7 %collective-permute-start = (bf16[64,512]{1,0:T(8,128)(2,1)}, bf16[64,512]{1,0:T(8,128)(2,1)S(1)}, u32[]{:S(2)}, u32[]{:S(2)}) collective-permute-start(bf16[64,512]{1,0:T(8,128)(2,1)} %param.11), channel_id=1, source_target_pairs={{0,4},{1,5},{2,6},{3,7},{4,0},{5,1},{6,2},{7,3},{8,12},{9,13},{10,... | collective-permute-start | bytes 196616 | tf_op jit(solution)/shard_map/ppermute | solution.py:30
  4.8 1.5 %collective-permute-start.5 = (bf16[256,512]{1,0:T(8,128)(2,1)}, bf16[256,512]{1,0:T(8,128)(2,1)S(1)}, u32[]{:S(2)}, u32[]{:S(2)}) collective-permute-start(bf16[256,512]{1,0:T(8,128)(2,1)} %refs_0_.4), channel_id=1, source_target_pairs={{0,16},{8,24},{16,0},{24,8},{1,17},{9,25},{17,1},{25,9},{2,18},{10... | collective-permute-start | bytes 786440 | tf_op jit(solution)/shard_map/ppermute | solution.py:26
  6.3 2.5 %shard_map.121 = (bf16[1536,1024]{1,0:T(8,128)(2,1)S(1)}, bf16[1536,128]{1,0:T(8,128)(2,1)S(1)}, bf16[1024,1536]{1,0:T(8,128)(2,1)S(1)}, bf16[128,1536]{1,0:T(8,128)(2,1)S(1)}) custom-call(bf16[1536,1024]{1,0:T(8,128)(2,1)} %refs_0_.3, bf16[1536,128]{1,0:T(8,128)(2,1)} %refs_1_.1), custom_call_target="tpu_custom_call" | custom-call | flops 20000000000 | bytes 3538944 | tf_op jit(solution)/shard_map/pallas_call | solution.py:72
  9.2 2.4 %collective-permute-start.1 = (bf16[128,512]{1,0:T(8,128)(2,1)S(1)}, bf16[128,512]{1,0:T(8,128)(2,1)S(1)}, u32[]{:S(2)}, u32[]{:S(2)}) collective-permute-start(bf16[128,512]{1,0:T(8,128)(2,1)S(1)} %constant_dynamic-update-slice_fusion.refs_0_), channel_id=1, source_target_pairs={{0,3},{1,2},{2,1},{3,0},{4,7},{5,6},{6,5},{7,4},{8,11},{9,10},{10,... | collective-permute-start | bytes 393224 | tf_op jit(solution)/shard_map/ppermute | solution.py:39
  13.4 2.4 %shard_map.123.refs_6_ = bf16[1536,1536]{1,0:T(8,128)(2,1)S(1)} custom-call(bf16[1536,1536]{1,0:T(8,128)(2,1)} %refs_0_.5), custom_call_target="tpu_custom_call" | custom-call | flops 20000000000 | bytes 4718592 | tf_op jit(solution)/shard_map/pallas_call | solution.py:72
  15.9 2.0 %shard_map.122.refs_4_ = f32[1536,512]{1,0:T(8,128)S(1)} custom-call(s32[1,8]{1,0:T(1,128)S(1)} %copy-done.3, bf16[256,512]{1,0:T(8,128)(2,1)S(1)} %copy-done, bf16[256,512]{1,0:T(8,128)(2,1)S(1)} %collective-permute-done.4.refs_1_, bf16[256,512]{1,0:T(8,128)(2,1)S(1)} %collective-permute-done.5.refs_2_, ...), custom_call_target="tpu_custom_call" | custom-call | tf_op jit(solution)/shard_map/pallas_call | solution.py:113
  18.1 5.0 %shard_map.124 = (bf16[1024,256]{1,0:T(8,128)(2,1)S(1)}, f32[1024,256]{1,0:T(8,128)S(1)}, bf16[1536,512]{1,0:T(8,128)(2,1)S(1)}) custom-call(s32[1,8]{1,0:T(1,128)S(1)} %copy-done.3, s32[1,8]{1,0:T(1,128)S(1)} %copy-done.4, bf16[128,512]{1,0:T(8,128)(2,1)S(1)} %constant_dynamic-update-slice_fusion.refs_0_, ...), custom_call_target="tpu_custom_call" | custom-call | flops 4026531840 | bytes 6291456 | tf_op jit(solution)/shard_map/pallas_call | solution.py:179
  23.5 1.6 %shard_map.125 = (f32[256,512]{1,0:T(8,128)S(1)}, bf16[256,512]{1,0:T(8,128)(2,1)S(1)}) custom-call(s32[1,8]{1,0:T(1,128)S(1)} %copy-done.4, bf16[1024,1536]{1,0:T(8,128)(2,1)S(1)} %get-tuple-element.38.refs_7_.ct, bf16[1536,512]{1,0:T(8,128)(2,1)S(1)} %get-tuple-element.55.weighted), custom_call_target="tpu_custom_call" | custom-call | flops 805306368 | bytes 3145728 | tf_op jit(solution)/shard_map/pallas_call | solution.py:240
  25.2 1.6 %collective-permute-start.8 = (bf16[512,256]{1,0:T(8,128)(2,1)S(1)}, bf16[512,256]{1,0:T(8,128)(2,1)S(1)}, u32[]{:S(2)}, u32[]{:S(2)}) collective-permute-start(bf16[512,256]{1,0:T(8,128)(2,1)S(1)} %get-tuple-element.53), channel_id=1, source_target_pairs={{0,16},{1,17},{2,18},{3,19},{4,20},{5,21},{6,22},{7,23},{8,9},{9,8... | collective-permute-start | bytes 786440 | tf_op jit(solution)/shard_map/ppermute | solution.py:39
  26.7 1.6 %collective-permute-start.10 = (bf16[256,512]{1,0:T(8,128)(2,1)S(1)}, bf16[256,512]{1,0:T(8,128)(2,1)S(1)}, u32[]{:S(2)}, u32[]{:S(2)}) collective-permute-start(bf16[256,512]{1,0:T(8,128)(2,1)S(1)} %get-tuple-element.59), channel_id=1, source_target_pairs={{0,2},{1,3},{2,0},{3,1},{4,6},{5,7},{6,4},{7,5},{8,9},{9,8},{10,11... | collective-permute-start | bytes 786440 | tf_op jit(solution)/shard_map/ppermute | solution.py:39
  28.3 1.0 %shard_map.127 = bf16[128,512]{1,0:T(8,128)(2,1)} custom-call(bf16[128,1536]{1,0:T(8,128)(2,1)S(1)} %get-tuple-element.54.mt, bf16[1536,512]{1,0:T(8,128)(2,1)S(1)} %get-tuple-element.55.weighted), custom_call_target="tpu_custom_call" | custom-call | flops 20000000000 | bytes 1572864 | tf_op jit(solution)/shard_map/pallas_call | solution.py:226
  29.4 2.3 %collective-permute-done.8.refs_0_ = bf16[512,256]{1,0:T(8,128)(2,1)S(1)} collective-permute-done((bf16[512,256]{1,0:T(8,128)(2,1)S(1)}, bf16[512,256]{1,0:T(8,128)(2,1)S(1)}, u32[]{:S(2)}, u32[]{:S(2)}) %collective-permute-start.8) | collective-permute-done | bytes 262176 | tf_op jit(solution)/shard_map/ppermute | solution.py:39
  31.7 1.6 %collective-permute-start.9 = (bf16[128,256]{1,0:T(8,128)(2,1)S(1)}, bf16[128,256]{1,0:T(8,128)(2,1)S(1)}, u32[]{:S(2)}, u32[]{:S(2)}) collective-permute-start(bf16[128,256]{1,0:T(8,128)(2,1)S(1)} %get-tuple-element.57), channel_id=1, source_target_pairs={{0,1},{1,0},{2,3},{3,2},{4,5},{5,4},{6,7},{7,6},{8,24},{9,25},{10,... | collective-permute-start | bytes 196616 | tf_op jit(solution)/shard_map/ppermute | solution.py:39
  33.3 1.5 %collective-permute-start.11 = (bf16[128,256]{1,0:T(8,128)(2,1)S(1)}, bf16[128,256]{1,0:T(8,128)(2,1)S(1)}, u32[]{:S(2)}, u32[]{:S(2)}) collective-permute-start(bf16[128,256]{1,0:T(8,128)(2,1)S(1)} %get-tuple-element.62), channel_id=1, source_target_pairs={{0,3},{1,2},{2,1},{3,0},{4,7},{5,6},{6,5},{7,4},{8,26},{9,27},{10,... | collective-permute-start | bytes 196616 | tf_op jit(solution)/shard_map/ppermute | solution.py:39
  36.1 1.6 %collective-permute-start.17 = (bf16[128,512]{1,0:T(8,128)(2,1)S(1)}, bf16[128,512]{1,0:T(8,128)(2,1)S(1)}, u32[]{:S(2)}, u32[]{:S(2)}) collective-permute-start(bf16[128,512]{1,0:T(8,128)(2,1)S(1)} %get-tuple-element.67), channel_id=1, source_target_pairs={{0,1},{1,0},{2,3},{3,2},{4,5},{5,4},{6,7},{7,6},{8,10},{9,11},{10,... | collective-permute-start | bytes 393224 | tf_op jit(solution)/shard_map/ppermute | solution.py:39
  37.7 1.4 %collective-permute-done.11.refs_0_ = bf16[128,256]{1,0:T(8,128)(2,1)S(1)} collective-permute-done((bf16[128,256]{1,0:T(8,128)(2,1)S(1)}, bf16[128,256]{1,0:T(8,128)(2,1)S(1)}, u32[]{:S(2)}, u32[]{:S(2)}) %collective-permute-start.11) | collective-permute-done | bytes 65568 | tf_op jit(solution)/shard_map/ppermute | solution.py:39
  39.8 3.1 %collective-permute-start.13 = (bf16[128,256]{1,0:T(8,128)(2,1)S(1)}, bf16[128,256]{1,0:T(8,128)(2,1)S(1)}, u32[]{:S(2)}, u32[]{:S(2)}) collective-permute-start(bf16[128,256]{1,0:T(8,128)(2,1)S(1)} %shard_map.130.keep), channel_id=1, source_target_pairs={{0,4},{1,5},{2,6},{3,7},{4,0},{5,1},{6,2},{7,3},{8,12},{9,13},{10,... | collective-permute-start | bytes 196616 | tf_op jit(solution)/shard_map/ppermute | solution.py:30
  42.9 2.3 %collective-permute-done.13.refs_0_ = bf16[128,256]{1,0:T(8,128)(2,1)S(1)} collective-permute-done((bf16[128,256]{1,0:T(8,128)(2,1)S(1)}, bf16[128,256]{1,0:T(8,128)(2,1)S(1)}, u32[]{:S(2)}, u32[]{:S(2)}) %collective-permute-start.13) | collective-permute-done | bytes 65568 | tf_op jit(solution)/shard_map/ppermute | solution.py:30
  45.2 2.1 %collective-permute-start.14 = (bf16[128,256]{1,0:T(8,128)(2,1)S(1)}, bf16[128,256]{1,0:T(8,128)(2,1)S(1)}, u32[]{:S(2)}, u32[]{:S(2)}) collective-permute-start(bf16[128,256]{1,0:T(8,128)(2,1)S(1)} %shard_map.131.refs_0_), channel_id=1, source_target_pairs={{0,1},{1,0},{2,3},{3,2},{4,5},{5,4},{6,7},{7,6},{8,10},{9,11},{10,... | collective-permute-start | bytes 196616 | tf_op jit(solution)/shard_map/ppermute | solution.py:39
  48.0 0.8 %collective-permute-start.16 = (bf16[128,256]{1,0:T(8,128)(2,1)S(1)}, bf16[128,256]{1,0:T(8,128)(2,1)S(1)}, u32[]{:S(2)}, u32[]{:S(2)}) collective-permute-start(bf16[128,256]{1,0:T(8,128)(2,1)S(1)} %shard_map.131.refs_0_), channel_id=1, source_target_pairs={{0,3},{1,2},{2,1},{3,0},{4,7},{5,6},{6,5},{7,4},{8,11},{9,10},{10,... | collective-permute-start | bytes 196616 | tf_op jit(solution)/shard_map/ppermute | solution.py:39
  48.8 3.0 %collective-permute-start.18 = (bf16[64,512]{1,0:T(8,128)(2,1)S(1)}, bf16[64,512]{1,0:T(8,128)(2,1)S(1)}, u32[]{:S(2)}, u32[]{:S(2)}) collective-permute-start(bf16[64,512]{1,0:T(8,128)(2,1)S(1)} %get-tuple-element.69), channel_id=1, source_target_pairs={{0,4},{1,5},{2,6},{3,7},{4,0},{5,1},{6,2},{7,3},{8,12},{9,13},{10,... | collective-permute-start | bytes 196616 | tf_op jit(solution)/shard_map/ppermute | solution.py:30
  51.9 1.2 %collective-permute-done.16.refs_3_ = bf16[128,256]{1,0:T(8,128)(2,1)S(1)} collective-permute-done((bf16[128,256]{1,0:T(8,128)(2,1)S(1)}, bf16[128,256]{1,0:T(8,128)(2,1)S(1)}, u32[]{:S(2)}, u32[]{:S(2)}) %collective-permute-start.16) | collective-permute-done | bytes 65568 | tf_op jit(solution)/shard_map/ppermute | solution.py:39
  53.2 1.2 %shard_map.132 = f32[256,512]{1,0:T(8,128)} custom-call(f32[256,64]{1,0:T(8,128)S(1)} %copy.13.kinv, bf16[128,256]{1,0:T(8,128)(2,1)S(1)} %shard_map.131.refs_0_, bf16[128,256]{1,0:T(8,128)(2,1)S(1)} %collective-permute-done.14.refs_1_, bf16[128,256]{1,0:T(8,128)(2,1)S(1)} %collective-permute-done.15.refs_2_, ...), custom_call_target="tpu_custom_call" | custom-call | flops 100663296 | bytes 1048576 | tf_op jit(solution)/shard_map/pallas_call | solution.py:345
  54.3 0.9 %shard_map.134 = f32[64,512]{1,0:T(8,128)} custom-call(f32[64,64]{1,0:T(8,128)S(1)} %copy-done.2, f32[64,512]{1,0:T(8,128)S(1)} %get-tuple-element.68.keep, bf16[64,512]{1,0:T(8,128)(2,1)S(1)} %collective-permute-done.18.got), custom_call_target="tpu_custom_call" | custom-call | flops 25165824 | bytes 262144 | tf_op jit(solution)/shard_map/pallas_call | solution.py:317
  (45 shorter events, 6.4 us)
Async XLA Ops:
  0.6 8.2 %copy-start.6 = (bf16[64,512]{1,0:T(8,128)(2,1)S(1)}, bf16[64,512]{1,0:T(8,128)(2,1)}, u32[]{:S(2)}) copy-start(bf16[64,512]{1,0:T(8,128)(2,1)} %param.11) | copy-start | bytes 196612
  0.6 4.2 %collective-permute-start.4 = (bf16[256,512]{1,0:T(8,128)(2,1)}, bf16[256,512]{1,0:T(8,128)(2,1)S(1)}, u32[]{:S(2)}, u32[]{:S(2)}) collective-permute-start(bf16[256,512]{1,0:T(8,128)(2,1)} %refs_0_.4), channel_id=1, source_target_pairs={{0,8},{8,0},{16,24},{24,16},{1,9},{9,1},{17,25},{25,17},{2,10},{10... | collective-permute-start | bytes 786440 | tf_op jit(solution)/shard_map/ppermute | solution.py:26
  1.2 8.0 %collective-permute-start = (bf16[64,512]{1,0:T(8,128)(2,1)}, bf16[64,512]{1,0:T(8,128)(2,1)S(1)}, u32[]{:S(2)}, u32[]{:S(2)}) collective-permute-start(bf16[64,512]{1,0:T(8,128)(2,1)} %param.11), channel_id=1, source_target_pairs={{0,4},{1,5},{2,6},{3,7},{4,0},{5,1},{6,2},{7,3},{8,12},{9,13},{10,... | collective-permute-start | bytes 196616 | tf_op jit(solution)/shard_map/ppermute | solution.py:30
  4.8 8.6 %collective-permute-start.5 = (bf16[256,512]{1,0:T(8,128)(2,1)}, bf16[256,512]{1,0:T(8,128)(2,1)S(1)}, u32[]{:S(2)}, u32[]{:S(2)}) collective-permute-start(bf16[256,512]{1,0:T(8,128)(2,1)} %refs_0_.4), channel_id=1, source_target_pairs={{0,16},{8,24},{16,0},{24,8},{1,17},{9,25},{17,1},{25,9},{2,18},{10... | collective-permute-start | bytes 786440 | tf_op jit(solution)/shard_map/ppermute | solution.py:26
  9.1 6.7 %copy-start.1 = (bf16[128,512]{1,0:T(8,128)(2,1)S(1)}, bf16[128,512]{1,0:T(8,128)(2,1)}, u32[]{:S(2)}) copy-start(bf16[128,512]{1,0:T(8,128)(2,1)} %refs_6_.1) | copy-start | bytes 393220
  9.1 6.7 %copy-start.3 = (s32[1,8]{1,0:T(1,128)S(1)}, s32[1,8]{1,0:T(1,128)}, u32[]{:S(2)}) copy-start(s32[1,8]{1,0:T(1,128)} %anc_top.3) | copy-start | bytes 100
  9.2 8.7 %collective-permute-start.1 = (bf16[128,512]{1,0:T(8,128)(2,1)S(1)}, bf16[128,512]{1,0:T(8,128)(2,1)S(1)}, u32[]{:S(2)}, u32[]{:S(2)}) collective-permute-start(bf16[128,512]{1,0:T(8,128)(2,1)S(1)} %constant_dynamic-update-slice_fusion.refs_0_), channel_id=1, source_target_pairs={{0,3},{1,2},{2,1},{3,0},{4,7},{5,6},{6,5},{7,4},{8,11},{9,10},{10,... | collective-permute-start | bytes 393224 | tf_op jit(solution)/shard_map/ppermute | solution.py:39
  11.5 6.5 %collective-permute-start.2 = (bf16[128,512]{1,0:T(8,128)(2,1)S(1)}, bf16[128,512]{1,0:T(8,128)(2,1)S(1)}, u32[]{:S(2)}, u32[]{:S(2)}) collective-permute-start(bf16[128,512]{1,0:T(8,128)(2,1)S(1)} %constant_dynamic-update-slice_fusion.refs_0_), channel_id=1, source_target_pairs={{0,2},{1,3},{2,0},{3,1},{4,6},{5,7},{6,4},{7,5},{8,9},{9,8},{10,11... | collective-permute-start | bytes 393224 | tf_op jit(solution)/shard_map/ppermute | solution.py:39
  12.3 5.8 %collective-permute-start.3 = (bf16[128,512]{1,0:T(8,128)(2,1)S(1)}, bf16[128,512]{1,0:T(8,128)(2,1)S(1)}, u32[]{:S(2)}, u32[]{:S(2)}) collective-permute-start(bf16[128,512]{1,0:T(8,128)(2,1)S(1)} %constant_dynamic-update-slice_fusion.refs_0_), channel_id=1, source_target_pairs={{0,1},{1,0},{2,3},{3,2},{4,5},{5,4},{6,7},{7,6},{8,10},{9,11},{10,... | collective-permute-start | bytes 393224 | tf_op jit(solution)/shard_map/ppermute | solution.py:39
  13.4 2.4 %collective-permute-start.6 = (bf16[256,512]{1,0:T(8,128)(2,1)S(1)}, bf16[256,512]{1,0:T(8,128)(2,1)S(1)}, u32[]{:S(2)}, u32[]{:S(2)}) collective-permute-start(bf16[256,512]{1,0:T(8,128)(2,1)S(1)} %collective-permute-done.5.refs_2_), channel_id=1, source_target_pairs={{0,8},{8,0},{16,24},{24,16},{1,9},{9,1},{17,25},{25,17},{2,10},{10... | collective-permute-start | bytes 786440 | tf_op jit(solution)/shard_map/ppermute | solution.py:26
  23.1 2.0 %collective-permute-start.7 = (bf16[1024,256]{1,0:T(8,128)(2,1)S(1)}, bf16[1024,256]{1,0:T(8,128)(2,1)S(1)}, u32[]{:S(2)}, u32[]{:S(2)}) collective-permute-start(bf16[1024,256]{1,0:T(8,128)(2,1)S(1)} %get-tuple-element.47), channel_id=1, source_target_pairs={{0,8},{8,0},{16,24},{24,16},{1,9},{9,1},{17,25},{25,17},{2,10},{10... | collective-permute-start | bytes 1572872 | tf_op jit(solution)/shard_map/ppermute | solution.py:26
  25.2 6.4 %collective-permute-start.8 = (bf16[512,256]{1,0:T(8,128)(2,1)S(1)}, bf16[512,256]{1,0:T(8,128)(2,1)S(1)}, u32[]{:S(2)}, u32[]{:S(2)}) collective-permute-start(bf16[512,256]{1,0:T(8,128)(2,1)S(1)} %get-tuple-element.53), channel_id=1, source_target_pairs={{0,16},{1,17},{2,18},{3,19},{4,20},{5,21},{6,22},{7,23},{8,9},{9,8... | collective-permute-start | bytes 786440 | tf_op jit(solution)/shard_map/ppermute | solution.py:39
  26.7 9.3 %collective-permute-start.10 = (bf16[256,512]{1,0:T(8,128)(2,1)S(1)}, bf16[256,512]{1,0:T(8,128)(2,1)S(1)}, u32[]{:S(2)}, u32[]{:S(2)}) collective-permute-start(bf16[256,512]{1,0:T(8,128)(2,1)S(1)} %get-tuple-element.59), channel_id=1, source_target_pairs={{0,2},{1,3},{2,0},{3,1},{4,6},{5,7},{6,4},{7,5},{8,9},{9,8},{10,11... | collective-permute-start | bytes 786440 | tf_op jit(solution)/shard_map/ppermute | solution.py:39
  28.3 23.5 %copy-start.5 = (f32[256,64]{0,1:T(8,128)S(1)}, f32[256,64]{0,1:T(8,128)}, u32[]{:S(2)}) copy-start(f32[256,64]{0,1:T(8,128)} %param.18) | copy-start | bytes 196612
  29.4 25.0 %copy-start.2 = (f32[64,64]{1,0:T(8,128)S(1)}, f32[64,64]{1,0:T(8,128)}, u32[]{:S(2)}) copy-start(f32[64,64]{1,0:T(8,128)} %kinv.2) | copy-start | bytes 49156
  31.7 4.3 %collective-permute-start.9 = (bf16[128,256]{1,0:T(8,128)(2,1)S(1)}, bf16[128,256]{1,0:T(8,128)(2,1)S(1)}, u32[]{:S(2)}, u32[]{:S(2)}) collective-permute-start(bf16[128,256]{1,0:T(8,128)(2,1)S(1)} %get-tuple-element.57), channel_id=1, source_target_pairs={{0,1},{1,0},{2,3},{3,2},{4,5},{5,4},{6,7},{7,6},{8,24},{9,25},{10,... | collective-permute-start | bytes 196616 | tf_op jit(solution)/shard_map/ppermute | solution.py:39
  33.3 5.8 %collective-permute-start.11 = (bf16[128,256]{1,0:T(8,128)(2,1)S(1)}, bf16[128,256]{1,0:T(8,128)(2,1)S(1)}, u32[]{:S(2)}, u32[]{:S(2)}) collective-permute-start(bf16[128,256]{1,0:T(8,128)(2,1)S(1)} %get-tuple-element.62), channel_id=1, source_target_pairs={{0,3},{1,2},{2,1},{3,0},{4,7},{5,6},{6,5},{7,4},{8,26},{9,27},{10,... | collective-permute-start | bytes 196616 | tf_op jit(solution)/shard_map/ppermute | solution.py:39
  34.8 5.0 %collective-permute-start.12 = (bf16[128,256]{1,0:T(8,128)(2,1)S(1)}, bf16[128,256]{1,0:T(8,128)(2,1)S(1)}, u32[]{:S(2)}, u32[]{:S(2)}) collective-permute-start(bf16[128,256]{1,0:T(8,128)(2,1)S(1)} %get-tuple-element.64), channel_id=1, source_target_pairs={{0,2},{1,3},{2,0},{3,1},{4,6},{5,7},{6,4},{7,5},{8,10},{9,11},{10,... | collective-permute-start | bytes 196616 | tf_op jit(solution)/shard_map/ppermute | solution.py:39
  36.1 12.7 %collective-permute-start.17 = (bf16[128,512]{1,0:T(8,128)(2,1)S(1)}, bf16[128,512]{1,0:T(8,128)(2,1)S(1)}, u32[]{:S(2)}, u32[]{:S(2)}) collective-permute-start(bf16[128,512]{1,0:T(8,128)(2,1)S(1)} %get-tuple-element.67), channel_id=1, source_target_pairs={{0,1},{1,0},{2,3},{3,2},{4,5},{5,4},{6,7},{7,6},{8,10},{9,11},{10,... | collective-permute-start | bytes 393224 | tf_op jit(solution)/shard_map/ppermute | solution.py:39
  39.8 5.4 %collective-permute-start.13 = (bf16[128,256]{1,0:T(8,128)(2,1)S(1)}, bf16[128,256]{1,0:T(8,128)(2,1)S(1)}, u32[]{:S(2)}, u32[]{:S(2)}) collective-permute-start(bf16[128,256]{1,0:T(8,128)(2,1)S(1)} %shard_map.130.keep), channel_id=1, source_target_pairs={{0,4},{1,5},{2,6},{3,7},{4,0},{5,1},{6,2},{7,3},{8,12},{9,13},{10,... | collective-permute-start | bytes 196616 | tf_op jit(solution)/shard_map/ppermute | solution.py:30
  45.2 6.7 %collective-permute-start.14 = (bf16[128,256]{1,0:T(8,128)(2,1)S(1)}, bf16[128,256]{1,0:T(8,128)(2,1)S(1)}, u32[]{:S(2)}, u32[]{:S(2)}) collective-permute-start(bf16[128,256]{1,0:T(8,128)(2,1)S(1)} %shard_map.131.refs_0_), channel_id=1, source_target_pairs={{0,1},{1,0},{2,3},{3,2},{4,5},{5,4},{6,7},{7,6},{8,10},{9,11},{10,... | collective-permute-start | bytes 196616 | tf_op jit(solution)/shard_map/ppermute | solution.py:39
  47.3 4.7 %collective-permute-start.15 = (bf16[128,256]{1,0:T(8,128)(2,1)S(1)}, bf16[128,256]{1,0:T(8,128)(2,1)S(1)}, u32[]{:S(2)}, u32[]{:S(2)}) collective-permute-start(bf16[128,256]{1,0:T(8,128)(2,1)S(1)} %shard_map.131.refs_0_), channel_id=1, source_target_pairs={{0,2},{1,3},{2,0},{3,1},{4,6},{5,7},{6,4},{7,5},{8,9},{9,8},{10,11... | collective-permute-start | bytes 196616 | tf_op jit(solution)/shard_map/ppermute | solution.py:39
  48.0 5.2 %collective-permute-start.16 = (bf16[128,256]{1,0:T(8,128)(2,1)S(1)}, bf16[128,256]{1,0:T(8,128)(2,1)S(1)}, u32[]{:S(2)}, u32[]{:S(2)}) collective-permute-start(bf16[128,256]{1,0:T(8,128)(2,1)S(1)} %shard_map.131.refs_0_), channel_id=1, source_target_pairs={{0,3},{1,2},{2,1},{3,0},{4,7},{5,6},{6,5},{7,4},{8,11},{9,10},{10,... | collective-permute-start | bytes 196616 | tf_op jit(solution)/shard_map/ppermute | solution.py:39
  48.8 5.5 %collective-permute-start.18 = (bf16[64,512]{1,0:T(8,128)(2,1)S(1)}, bf16[64,512]{1,0:T(8,128)(2,1)S(1)}, u32[]{:S(2)}, u32[]{:S(2)}) collective-permute-start(bf16[64,512]{1,0:T(8,128)(2,1)S(1)} %get-tuple-element.69), channel_id=1, source_target_pairs={{0,4},{1,5},{2,6},{3,7},{4,0},{5,1},{6,2},{7,3},{8,12},{9,13},{10,... | collective-permute-start | bytes 196616 | tf_op jit(solution)/shard_map/ppermute | solution.py:30
  (2 other events, 8.9 us)

commit v5 on v4

--- a/solution.py
+++ b/solution.py
@@ -274,6 +274,31 @@
     )(keep, *got)
 
 
+def quarter_kernel(keep, got, own, near, other, across):
+    even = (lax.axis_index("group") & 1) == 0
+    n = own.shape[0]
+    for out, at in (
+        (own, 0),
+        (near, jnp.where(even, 2 * n, n)),
+        (other, jnp.where(even, n, 2 * n)),
+        (across, 3 * n),
+    ):
+        at = pl.ds(pl.multiple_of(at, n), n)
+        out[...] = (keep[at, :] + got[at, :].astype(F32)).astype(out.dtype)
+
+
+def quarter_call(keep, got):
+    piece = (keep.shape[0] // 4, keep.shape[1])
+    return pl.pallas_call(
+        quarter_kernel,
+        in_specs=[VMEM] * 2,
+        out_specs=[VMEM] * 4,
+        out_shape=[jax.ShapeDtypeStruct(piece, F32)] + [jax.ShapeDtypeStruct(piece, BF16)] * 3,
+        compiler_params=params(4),
+        cost_estimate=cost(keep.size, 8 * keep.size),
+    )(keep, got)
+
+
 def sum_kernel(keep, *refs):
     total = keep[...].astype(F32)
     for got in refs[:-1]:
@@ -363,10 +388,10 @@
     far_low = send_leaf(low_modes, leaves // 2)
     near_top, to_send = lax.optimization_barrier((near_top, top_modes))
     far_top = send_group(to_send, 2)
-    coupling, leaf_modes, ct, mt = load_call((coupling, leaf_modes), (True, True))
-    far_low, ct = lax.optimization_barrier((far_low, ct))
+    leaf_modes, mt = load_call((leaf_modes,), (True,))
+    far_low, mt = lax.optimization_barrier((far_low, mt))
     held = gather_leaf(low_modes, far_low)
-    (leaf_mass,) = load_call((leaf_mass,), (False,))
+    coupling, ct = load_call((coupling,), (True,))
     tops = [top_modes, near_top, far_top, send_group(far_top, 1)]
     part = first_call(anc_top, tops, coupling, leaf_modes, leaf_coef, sr)
     send, keep, weighted = main_call(
@@ -392,11 +417,8 @@
     got = send_by_core(send, (2, 0), (0, 1))
     leaf_proj = proj_call(mt, weighted)
     got, leaf_proj = lax.optimization_barrier((got, leaf_proj))
-    keep, *sends = part_call(keep, [got], 4, 1)
-    got = [
-        send_by_core(x, *there)
-        for x, there in zip(sends[::-1], (((0, 3), (2, 2)), ((0, 1), (2, 0)), ((0, 2), (0, 2))))
-    ]
+    keep, near, other, across = quarter_call(keep, got)
+    got = [send_by_core(x, *there) for x, *there in ((across, (0, 3), (2, 2)), (other, (0, 2), (2, 0)), (near, (0, 1), (0, 2)))]
     low_keep, got[1] = lax.optimization_barrier((low_keep, got[1]))
     low_keep, low_send = part_call(low_keep, [low_got], 2, 1)
     low_got = send_by_core(low_send, (0, 1), (0, 2))

time: 55.4 us -> 54.5 us (0.984)
  Pallas kernels: 16.9 us -> 15.5 us
  waiting for transfers between devices: 9.86 us -> 10.5 us
    ppermute x3, waiting for transfers between devices: 2.55 us -> 4.07 us  [send_leaf(): lax.ppermute(x, 'leaf', [(i, i ^ k) for i in range(lax.axis_size('leaf'))])]
    pallas_call x2, Pallas kernels: 4.9 us -> 3.58 us  [load_call(): pl.pallas_call(functools.partial(load_kernel, turned, step), in_specs=[HB...]
    ppermute x12, waiting for transfers between devices: 6.6 us -> 5.76 us  [send_by_core(): return lax.ppermute(x, ('group', 'leaf'), pairs)]
  transfers between devices with their start and end apart: 19 -> 19, of which waited for: 9 -> 10; matrix products, arithmetic and copies ran while one was open for 0% -> 0% of each run, Pallas kernels for 20% -> 18%
where the time goes in v5:
time: 54.5 us; the launch traced here: 54.4 us
  starting transfers between devices  27.3 us (50%)
  Pallas kernels  15.5 us (28%)
  waiting for transfers between devices  10.5 us (19%)
  between operations  0.87 us (2%)
    ppermute x12, starting transfers between devices, send_by_core(): return lax.ppermute(x, ('group', 'leaf'), pairs)  15.5 us
    ppermute x3, starting transfers between devices, send_leaf(): lax.ppermute(x, 'leaf', [(i, i ^ k) for i in range(lax.axis_size('leaf'))])  9.38 us
    ppermute x12, waiting for transfers between devices, send_by_core(): return lax.ppermute(x, ('group', 'leaf'), pairs)  5.76 us
    pallas_call x1, Pallas kernels, main_call(): pl.pallas_call(functools.partial(main_kernel, per_group, low_rels), in_sp...  5 us
    ppermute x3, waiting for transfers between devices, send_leaf(): lax.ppermute(x, 'leaf', [(i, i ^ k) for i in range(lax.axis_size('leaf'))])  4.07 us
    pallas_call x2, Pallas kernels, load_call(): pl.pallas_call(functools.partial(load_kernel, turned, step), in_specs=[HB...  3.58 us
    ppermute x4, starting transfers between devices, send_group(): lax.ppermute(x, 'group', [(i, i ^ k) for i in range(lax.axis_size('group'...  2.48 us
    pallas_call x1, Pallas kernels, first_call(): pl.pallas_call(functools.partial(first_kernel, len(tops)), in_specs=[SMEM...  1.99 us
  transfers between devices with their start and end apart: 19, of which 10 were waited for; matrix products, arithmetic and copies ran while one was open for 0% of the time, Pallas kernels for 18%

profile of v5, /device:TPU:0, one launch (start us, length us, event | category | flops | bytes accessed | tf_op | source)
XLA Modules:
  0.0 54.4 jit_solution(245559986083022995)
XLA Ops:
  1.2 3.7 %collective-permute-start = (bf16[64,512]{1,0:T(8,128)(2,1)}, bf16[64,512]{1,0:T(8,128)(2,1)S(1)}, u32[]{:S(2)}, u32[]{:S(2)}) collective-permute-start(bf16[64,512]{1,0:T(8,128)(2,1)} %param.11), channel_id=1, source_target_pairs={{0,4},{1,5},{2,6},{3,7},{4,0},{5,1},{6,2},{7,3},{8,12},{9,13},{10,... | collective-permute-start | bytes 196616 | tf_op jit(solution)/shard_map/ppermute | solution.py:30
  4.8 1.5 %collective-permute-start.5 = (bf16[256,512]{1,0:T(8,128)(2,1)}, bf16[256,512]{1,0:T(8,128)(2,1)S(1)}, u32[]{:S(2)}, u32[]{:S(2)}) collective-permute-start(bf16[256,512]{1,0:T(8,128)(2,1)} %refs_0_.5), channel_id=1, source_target_pairs={{0,16},{8,24},{16,0},{24,8},{1,17},{9,25},{17,1},{25,9},{2,18},{10... | collective-permute-start | bytes 786440 | tf_op jit(solution)/shard_map/ppermute | solution.py:26
  6.3 1.3 %shard_map.122 = (bf16[1536,128]{1,0:T(8,128)(2,1)S(1)}, bf16[128,1536]{1,0:T(8,128)(2,1)S(1)}) custom-call(bf16[1536,128]{1,0:T(8,128)(2,1)} %refs_0_.4), custom_call_target="tpu_custom_call" | custom-call | flops 20000000000 | bytes 393216 | tf_op jit(solution)/shard_map/pallas_call | solution.py:72
  7.7 1.4 %collective-permute-done = bf16[64,512]{1,0:T(8,128)(2,1)S(1)} collective-permute-done((bf16[64,512]{1,0:T(8,128)(2,1)}, bf16[64,512]{1,0:T(8,128)(2,1)S(1)}, u32[]{:S(2)}, u32[]{:S(2)}) %collective-permute-start) | collective-permute-done | bytes 65568 | tf_op jit(solution)/shard_map/ppermute | solution.py:30
  9.2 1.9 %collective-permute-start.1 = (bf16[128,512]{1,0:T(8,128)(2,1)S(1)}, bf16[128,512]{1,0:T(8,128)(2,1)S(1)}, u32[]{:S(2)}, u32[]{:S(2)}) collective-permute-start(bf16[128,512]{1,0:T(8,128)(2,1)S(1)} %constant_dynamic-update-slice_fusion.refs_0_), channel_id=1, source_target_pairs={{0,3},{1,2},{2,1},{3,0},{4,7},{5,6},{6,5},{7,4},{8,11},{9,10},{10,... | collective-permute-start | bytes 393224 | tf_op jit(solution)/shard_map/ppermute | solution.py:39
  11.0 1.3 %collective-permute-start.2 = (bf16[128,512]{1,0:T(8,128)(2,1)S(1)}, bf16[128,512]{1,0:T(8,128)(2,1)S(1)}, u32[]{:S(2)}, u32[]{:S(2)}) collective-permute-start(bf16[128,512]{1,0:T(8,128)(2,1)S(1)} %constant_dynamic-update-slice_fusion.refs_0_), channel_id=1, source_target_pairs={{0,2},{1,3},{2,0},{3,1},{4,6},{5,7},{6,4},{7,5},{8,9},{9,8},{10,11... | collective-permute-start | bytes 393224 | tf_op jit(solution)/shard_map/ppermute | solution.py:39
  13.4 2.2 %shard_map.121 = (bf16[1536,1024]{1,0:T(8,128)(2,1)S(1)}, bf16[1024,1536]{1,0:T(8,128)(2,1)S(1)}) custom-call(bf16[1536,1024]{1,0:T(8,128)(2,1)} %refs_0_.3), custom_call_target="tpu_custom_call" | custom-call | flops 20000000000 | bytes 3145728 | tf_op jit(solution)/shard_map/pallas_call | solution.py:72
  15.7 2.0 %shard_map.123.refs_4_ = f32[1536,512]{1,0:T(8,128)S(1)} custom-call(s32[1,8]{1,0:T(1,128)S(1)} %copy-done.3, bf16[256,512]{1,0:T(8,128)(2,1)S(1)} %copy-done, bf16[256,512]{1,0:T(8,128)(2,1)S(1)} %collective-permute-done.4.refs_1_, bf16[256,512]{1,0:T(8,128)(2,1)S(1)} %collective-permute-done.5.refs_2_, ...), custom_call_target="tpu_custom_call" | custom-call | tf_op jit(solution)/shard_map/pallas_call | solution.py:113
  17.9 5.0 %shard_map.124 = (bf16[1024,256]{1,0:T(8,128)(2,1)S(1)}, f32[1024,256]{1,0:T(8,128)S(1)}, bf16[1536,512]{1,0:T(8,128)(2,1)S(1)}) custom-call(s32[1,8]{1,0:T(1,128)S(1)} %copy-done.3, s32[1,8]{1,0:T(1,128)S(1)} %copy-done.4, bf16[128,512]{1,0:T(8,128)(2,1)S(1)} %constant_dynamic-update-slice_fusion.refs_0_, ...), custom_call_target="tpu_custom_call" | custom-call | flops 4026531840 | bytes 6291456 | tf_op jit(solution)/shard_map/pallas_call | solution.py:179
  23.4 1.6 %shard_map.125 = (f32[256,512]{1,0:T(8,128)S(1)}, bf16[256,512]{1,0:T(8,128)(2,1)S(1)}) custom-call(s32[1,8]{1,0:T(1,128)S(1)} %copy-done.4, bf16[1024,1536]{1,0:T(8,128)(2,1)S(1)} %get-tuple-element.37.refs_7_.ct, bf16[1536,512]{1,0:T(8,128)(2,1)S(1)} %get-tuple-element.55.weighted), custom_call_target="tpu_custom_call" | custom-call | flops 805306368 | bytes 3145728 | tf_op jit(solution)/shard_map/pallas_call | solution.py:240
  25.1 1.6 %collective-permute-start.8 = (bf16[512,256]{1,0:T(8,128)(2,1)S(1)}, bf16[512,256]{1,0:T(8,128)(2,1)S(1)}, u32[]{:S(2)}, u32[]{:S(2)}) collective-permute-start(bf16[512,256]{1,0:T(8,128)(2,1)S(1)} %get-tuple-element.53), channel_id=1, source_target_pairs={{0,16},{1,17},{2,18},{3,19},{4,20},{5,21},{6,22},{7,23},{8,9},{9,8... | collective-permute-start | bytes 786440 | tf_op jit(solution)/shard_map/ppermute | solution.py:39
  26.6 1.6 %collective-permute-start.10 = (bf16[256,512]{1,0:T(8,128)(2,1)S(1)}, bf16[256,512]{1,0:T(8,128)(2,1)S(1)}, u32[]{:S(2)}, u32[]{:S(2)}) collective-permute-start(bf16[256,512]{1,0:T(8,128)(2,1)S(1)} %get-tuple-element.59), channel_id=1, source_target_pairs={{0,2},{1,3},{2,0},{3,1},{4,6},{5,7},{6,4},{7,5},{8,9},{9,8},{10,11... | collective-permute-start | bytes 786440 | tf_op jit(solution)/shard_map/ppermute | solution.py:39
  28.2 1.0 %shard_map.127 = bf16[128,512]{1,0:T(8,128)(2,1)} custom-call(bf16[128,1536]{1,0:T(8,128)(2,1)S(1)} %get-tuple-element.54.mt, bf16[1536,512]{1,0:T(8,128)(2,1)S(1)} %get-tuple-element.55.weighted), custom_call_target="tpu_custom_call" | custom-call | flops 20000000000 | bytes 1572864 | tf_op jit(solution)/shard_map/pallas_call | solution.py:226
  29.2 2.3 %collective-permute-done.8.got = bf16[512,256]{1,0:T(8,128)(2,1)S(1)} collective-permute-done((bf16[512,256]{1,0:T(8,128)(2,1)S(1)}, bf16[512,256]{1,0:T(8,128)(2,1)S(1)}, u32[]{:S(2)}, u32[]{:S(2)}) %collective-permute-start.8) | collective-permute-done | bytes 262176 | tf_op jit(solution)/shard_map/ppermute | solution.py:39
  31.5 1.6 %collective-permute-start.9 = (bf16[128,256]{1,0:T(8,128)(2,1)S(1)}, bf16[128,256]{1,0:T(8,128)(2,1)S(1)}, u32[]{:S(2)}, u32[]{:S(2)}) collective-permute-start(bf16[128,256]{1,0:T(8,128)(2,1)S(1)} %get-tuple-element.57), channel_id=1, source_target_pairs={{0,2},{1,3},{2,0},{3,1},{4,6},{5,7},{6,4},{7,5},{8,24},{9,25},{10,... | collective-permute-start | bytes 196616 | tf_op jit(solution)/shard_map/ppermute | solution.py:39
  33.2 1.4 %collective-permute-start.11 = (bf16[128,256]{1,0:T(8,128)(2,1)S(1)}, bf16[128,256]{1,0:T(8,128)(2,1)S(1)}, u32[]{:S(2)}, u32[]{:S(2)}) collective-permute-start(bf16[128,256]{1,0:T(8,128)(2,1)S(1)} %get-tuple-element.62), channel_id=1, source_target_pairs={{0,3},{1,2},{2,1},{3,0},{4,7},{5,6},{6,5},{7,4},{8,26},{9,27},{10,... | collective-permute-start | bytes 196616 | tf_op jit(solution)/shard_map/ppermute | solution.py:39
  35.1 1.2 %collective-permute-done.9.refs_1_ = bf16[128,256]{1,0:T(8,128)(2,1)S(1)} collective-permute-done((bf16[128,256]{1,0:T(8,128)(2,1)S(1)}, bf16[128,256]{1,0:T(8,128)(2,1)S(1)}, u32[]{:S(2)}, u32[]{:S(2)}) %collective-permute-start.9) | collective-permute-done | bytes 65568 | tf_op jit(solution)/shard_map/ppermute | solution.py:39
  36.4 1.6 %collective-permute-start.17 = (bf16[128,512]{1,0:T(8,128)(2,1)S(1)}, bf16[128,512]{1,0:T(8,128)(2,1)S(1)}, u32[]{:S(2)}, u32[]{:S(2)}) collective-permute-start(bf16[128,512]{1,0:T(8,128)(2,1)S(1)} %get-tuple-element.67), channel_id=1, source_target_pairs={{0,1},{1,0},{2,3},{3,2},{4,5},{5,4},{6,7},{7,6},{8,10},{9,11},{10,... | collective-permute-start | bytes 393224 | tf_op jit(solution)/shard_map/ppermute | solution.py:39
  39.3 2.8 %collective-permute-start.13 = (bf16[128,256]{1,0:T(8,128)(2,1)S(1)}, bf16[128,256]{1,0:T(8,128)(2,1)S(1)}, u32[]{:S(2)}, u32[]{:S(2)}) collective-permute-start(bf16[128,256]{1,0:T(8,128)(2,1)S(1)} %shard_map.130.keep), channel_id=1, source_target_pairs={{0,4},{1,5},{2,6},{3,7},{4,0},{5,1},{6,2},{7,3},{8,12},{9,13},{10,... | collective-permute-start | bytes 196616 | tf_op jit(solution)/shard_map/ppermute | solution.py:30
  42.1 2.5 %collective-permute-done.13.refs_0_ = bf16[128,256]{1,0:T(8,128)(2,1)S(1)} collective-permute-done((bf16[128,256]{1,0:T(8,128)(2,1)S(1)}, bf16[128,256]{1,0:T(8,128)(2,1)S(1)}, u32[]{:S(2)}, u32[]{:S(2)}) %collective-permute-start.13) | collective-permute-done | bytes 65568 | tf_op jit(solution)/shard_map/ppermute | solution.py:30
  44.6 2.1 %collective-permute-start.14 = (bf16[128,256]{1,0:T(8,128)(2,1)S(1)}, bf16[128,256]{1,0:T(8,128)(2,1)S(1)}, u32[]{:S(2)}, u32[]{:S(2)}) collective-permute-start(bf16[128,256]{1,0:T(8,128)(2,1)S(1)} %shard_map.131.refs_0_), channel_id=1, source_target_pairs={{0,1},{1,0},{2,3},{3,2},{4,5},{5,4},{6,7},{7,6},{8,10},{9,11},{10,... | collective-permute-start | bytes 196616 | tf_op jit(solution)/shard_map/ppermute | solution.py:39
  47.0 1.2 %collective-permute-start.16 = (bf16[128,256]{1,0:T(8,128)(2,1)S(1)}, bf16[128,256]{1,0:T(8,128)(2,1)S(1)}, u32[]{:S(2)}, u32[]{:S(2)}) collective-permute-start(bf16[128,256]{1,0:T(8,128)(2,1)S(1)} %shard_map.131.refs_0_), channel_id=1, source_target_pairs={{0,3},{1,2},{2,1},{3,0},{4,7},{5,6},{6,5},{7,4},{8,11},{9,10},{10,... | collective-permute-start | bytes 196616 | tf_op jit(solution)/shard_map/ppermute | solution.py:39
  48.3 2.9 %collective-permute-start.18 = (bf16[64,512]{1,0:T(8,128)(2,1)S(1)}, bf16[64,512]{1,0:T(8,128)(2,1)S(1)}, u32[]{:S(2)}, u32[]{:S(2)}) collective-permute-start(bf16[64,512]{1,0:T(8,128)(2,1)S(1)} %get-tuple-element.69), channel_id=1, source_target_pairs={{0,4},{1,5},{2,6},{3,7},{4,0},{5,1},{6,2},{7,3},{8,12},{9,13},{10,... | collective-permute-start | bytes 196616 | tf_op jit(solution)/shard_map/ppermute | solution.py:30
  52.1 1.2 %shard_map.132 = f32[256,512]{1,0:T(8,128)} custom-call(f32[256,64]{1,0:T(8,128)S(1)} %copy.13.kinv, bf16[128,256]{1,0:T(8,128)(2,1)S(1)} %shard_map.131.refs_0_, bf16[128,256]{1,0:T(8,128)(2,1)S(1)} %collective-permute-done.14.refs_1_, bf16[128,256]{1,0:T(8,128)(2,1)S(1)} %collective-permute-done.15.refs_2_, ...), custom_call_target="tpu_custom_call" | custom-call | flops 100663296 | bytes 1048576 | tf_op jit(solution)/shard_map/pallas_call | solution.py:370
  (50 shorter events, 6.7 us)
Async XLA Ops:
  0.6 7.0 %copy-start.6 = (bf16[64,512]{1,0:T(8,128)(2,1)S(1)}, bf16[64,512]{1,0:T(8,128)(2,1)}, u32[]{:S(2)}) copy-start(bf16[64,512]{1,0:T(8,128)(2,1)} %param.11) | copy-start | bytes 196612
  0.6 4.2 %collective-permute-start.4 = (bf16[256,512]{1,0:T(8,128)(2,1)}, bf16[256,512]{1,0:T(8,128)(2,1)S(1)}, u32[]{:S(2)}, u32[]{:S(2)}) collective-permute-start(bf16[256,512]{1,0:T(8,128)(2,1)} %refs_0_.5), channel_id=1, source_target_pairs={{0,8},{8,0},{16,24},{24,16},{1,9},{9,1},{17,25},{25,17},{2,10},{10... | collective-permute-start | bytes 786440 | tf_op jit(solution)/shard_map/ppermute | solution.py:26
  1.2 8.0 %collective-permute-start = (bf16[64,512]{1,0:T(8,128)(2,1)}, bf16[64,512]{1,0:T(8,128)(2,1)S(1)}, u32[]{:S(2)}, u32[]{:S(2)}) collective-permute-start(bf16[64,512]{1,0:T(8,128)(2,1)} %param.11), channel_id=1, source_target_pairs={{0,4},{1,5},{2,6},{3,7},{4,0},{5,1},{6,2},{7,3},{8,12},{9,13},{10,... | collective-permute-start | bytes 196616 | tf_op jit(solution)/shard_map/ppermute | solution.py:30
  4.8 8.6 %collective-permute-start.5 = (bf16[256,512]{1,0:T(8,128)(2,1)}, bf16[256,512]{1,0:T(8,128)(2,1)S(1)}, u32[]{:S(2)}, u32[]{:S(2)}) collective-permute-start(bf16[256,512]{1,0:T(8,128)(2,1)} %refs_0_.5), channel_id=1, source_target_pairs={{0,16},{8,24},{16,0},{24,8},{1,17},{9,25},{17,1},{25,9},{2,18},{10... | collective-permute-start | bytes 786440 | tf_op jit(solution)/shard_map/ppermute | solution.py:26
  6.3 11.5 %slice-start = ((s8[4718592]{0:T(1024)(128)(4,1)}), s8[4194304]{0:T(1024)(128)(4,1)S(1)}, s32[]{:S(2)}) async-start(s8[4718592]{0:T(1024)(128)(4,1)} %bitcast), calls=%async_computation | async-start | bytes 8388608
  9.2 8.7 %slice-start.1 = ((s8[4718592]{0:T(1024)(128)(4,1)}), s8[524288]{0:T(1024)(128)(4,1)S(1)}, s32[]{:S(2)}) async-start(s8[4718592]{0:T(1024)(128)(4,1)} %bitcast), calls=%async_computation.1 | async-start | bytes 1048576
  9.2 8.5 %collective-permute-start.1 = (bf16[128,512]{1,0:T(8,128)(2,1)S(1)}, bf16[128,512]{1,0:T(8,128)(2,1)S(1)}, u32[]{:S(2)}, u32[]{:S(2)}) collective-permute-start(bf16[128,512]{1,0:T(8,128)(2,1)S(1)} %constant_dynamic-update-slice_fusion.refs_0_), channel_id=1, source_target_pairs={{0,3},{1,2},{2,1},{3,0},{4,7},{5,6},{6,5},{7,4},{8,11},{9,10},{10,... | collective-permute-start | bytes 393224 | tf_op jit(solution)/shard_map/ppermute | solution.py:39
  11.0 6.8 %collective-permute-start.2 = (bf16[128,512]{1,0:T(8,128)(2,1)S(1)}, bf16[128,512]{1,0:T(8,128)(2,1)S(1)}, u32[]{:S(2)}, u32[]{:S(2)}) collective-permute-start(bf16[128,512]{1,0:T(8,128)(2,1)S(1)} %constant_dynamic-update-slice_fusion.refs_0_), channel_id=1, source_target_pairs={{0,2},{1,3},{2,0},{3,1},{4,6},{5,7},{6,4},{7,5},{8,9},{9,8},{10,11... | collective-permute-start | bytes 393224 | tf_op jit(solution)/shard_map/ppermute | solution.py:39
  12.3 5.6 %collective-permute-start.3 = (bf16[128,512]{1,0:T(8,128)(2,1)S(1)}, bf16[128,512]{1,0:T(8,128)(2,1)S(1)}, u32[]{:S(2)}, u32[]{:S(2)}) collective-permute-start(bf16[128,512]{1,0:T(8,128)(2,1)S(1)} %constant_dynamic-update-slice_fusion.refs_0_), channel_id=1, source_target_pairs={{0,1},{1,0},{2,3},{3,2},{4,5},{5,4},{6,7},{7,6},{8,10},{9,11},{10,... | collective-permute-start | bytes 393224 | tf_op jit(solution)/shard_map/ppermute | solution.py:39
  13.4 2.2 %collective-permute-start.6 = (bf16[256,512]{1,0:T(8,128)(2,1)S(1)}, bf16[256,512]{1,0:T(8,128)(2,1)S(1)}, u32[]{:S(2)}, u32[]{:S(2)}) collective-permute-start(bf16[256,512]{1,0:T(8,128)(2,1)S(1)} %collective-permute-done.5.refs_2_), channel_id=1, source_target_pairs={{0,8},{8,0},{16,24},{24,16},{1,9},{9,1},{17,25},{25,17},{2,10},{10... | collective-permute-start | bytes 786440 | tf_op jit(solution)/shard_map/ppermute | solution.py:26
  22.9 2.1 %collective-permute-start.7 = (bf16[1024,256]{1,0:T(8,128)(2,1)S(1)}, bf16[1024,256]{1,0:T(8,128)(2,1)S(1)}, u32[]{:S(2)}, u32[]{:S(2)}) collective-permute-start(bf16[1024,256]{1,0:T(8,128)(2,1)S(1)} %get-tuple-element.47), channel_id=1, source_target_pairs={{0,8},{8,0},{16,24},{24,16},{1,9},{9,1},{17,25},{25,17},{2,10},{10... | collective-permute-start | bytes 1572872 | tf_op jit(solution)/shard_map/ppermute | solution.py:26
  25.0 26.1 %copy-start.5 = (f32[256,64]{0,1:T(8,128)S(1)}, f32[256,64]{0,1:T(8,128)}, u32[]{:S(2)}) copy-start(f32[256,64]{0,1:T(8,128)} %param.18) | copy-start | bytes 196612
  25.1 6.4 %collective-permute-start.8 = (bf16[512,256]{1,0:T(8,128)(2,1)S(1)}, bf16[512,256]{1,0:T(8,128)(2,1)S(1)}, u32[]{:S(2)}, u32[]{:S(2)}) collective-permute-start(bf16[512,256]{1,0:T(8,128)(2,1)S(1)} %get-tuple-element.53), channel_id=1, source_target_pairs={{0,16},{1,17},{2,18},{3,19},{4,20},{5,21},{6,22},{7,23},{8,9},{9,8... | collective-permute-start | bytes 786440 | tf_op jit(solution)/shard_map/ppermute | solution.py:39
  26.6 9.7 %collective-permute-start.10 = (bf16[256,512]{1,0:T(8,128)(2,1)S(1)}, bf16[256,512]{1,0:T(8,128)(2,1)S(1)}, u32[]{:S(2)}, u32[]{:S(2)}) collective-permute-start(bf16[256,512]{1,0:T(8,128)(2,1)S(1)} %get-tuple-element.59), channel_id=1, source_target_pairs={{0,2},{1,3},{2,0},{3,1},{4,6},{5,7},{6,4},{7,5},{8,9},{9,8},{10,11... | collective-permute-start | bytes 786440 | tf_op jit(solution)/shard_map/ppermute | solution.py:39
  29.2 24.2 %copy-start.2 = (f32[64,64]{1,0:T(8,128)S(1)}, f32[64,64]{1,0:T(8,128)}, u32[]{:S(2)}) copy-start(f32[64,64]{1,0:T(8,128)} %kinv.2) | copy-start | bytes 49156
  31.5 4.8 %collective-permute-start.9 = (bf16[128,256]{1,0:T(8,128)(2,1)S(1)}, bf16[128,256]{1,0:T(8,128)(2,1)S(1)}, u32[]{:S(2)}, u32[]{:S(2)}) collective-permute-start(bf16[128,256]{1,0:T(8,128)(2,1)S(1)} %get-tuple-element.57), channel_id=1, source_target_pairs={{0,2},{1,3},{2,0},{3,1},{4,6},{5,7},{6,4},{7,5},{8,24},{9,25},{10,... | collective-permute-start | bytes 196616 | tf_op jit(solution)/shard_map/ppermute | solution.py:39
  33.2 5.8 %collective-permute-start.11 = (bf16[128,256]{1,0:T(8,128)(2,1)S(1)}, bf16[128,256]{1,0:T(8,128)(2,1)S(1)}, u32[]{:S(2)}, u32[]{:S(2)}) collective-permute-start(bf16[128,256]{1,0:T(8,128)(2,1)S(1)} %get-tuple-element.62), channel_id=1, source_target_pairs={{0,3},{1,2},{2,1},{3,0},{4,7},{5,6},{6,5},{7,4},{8,26},{9,27},{10,... | collective-permute-start | bytes 196616 | tf_op jit(solution)/shard_map/ppermute | solution.py:39
  34.6 4.7 %collective-permute-start.12 = (bf16[128,256]{1,0:T(8,128)(2,1)S(1)}, bf16[128,256]{1,0:T(8,128)(2,1)S(1)}, u32[]{:S(2)}, u32[]{:S(2)}) collective-permute-start(bf16[128,256]{1,0:T(8,128)(2,1)S(1)} %get-tuple-element.64), channel_id=1, source_target_pairs={{0,1},{1,0},{2,3},{3,2},{4,5},{5,4},{6,7},{7,6},{8,10},{9,11},{10,... | collective-permute-start | bytes 196616 | tf_op jit(solution)/shard_map/ppermute | solution.py:39
  36.4 11.8 %collective-permute-start.17 = (bf16[128,512]{1,0:T(8,128)(2,1)S(1)}, bf16[128,512]{1,0:T(8,128)(2,1)S(1)}, u32[]{:S(2)}, u32[]{:S(2)}) collective-permute-start(bf16[128,512]{1,0:T(8,128)(2,1)S(1)} %get-tuple-element.67), channel_id=1, source_target_pairs={{0,1},{1,0},{2,3},{3,2},{4,5},{5,4},{6,7},{7,6},{8,10},{9,11},{10,... | collective-permute-start | bytes 393224 | tf_op jit(solution)/shard_map/ppermute | solution.py:39
  39.3 5.2 %collective-permute-start.13 = (bf16[128,256]{1,0:T(8,128)(2,1)S(1)}, bf16[128,256]{1,0:T(8,128)(2,1)S(1)}, u32[]{:S(2)}, u32[]{:S(2)}) collective-permute-start(bf16[128,256]{1,0:T(8,128)(2,1)S(1)} %shard_map.130.keep), channel_id=1, source_target_pairs={{0,4},{1,5},{2,6},{3,7},{4,0},{5,1},{6,2},{7,3},{8,12},{9,13},{10,... | collective-permute-start | bytes 196616 | tf_op jit(solution)/shard_map/ppermute | solution.py:30
  44.6 6.7 %collective-permute-start.14 = (bf16[128,256]{1,0:T(8,128)(2,1)S(1)}, bf16[128,256]{1,0:T(8,128)(2,1)S(1)}, u32[]{:S(2)}, u32[]{:S(2)}) collective-permute-start(bf16[128,256]{1,0:T(8,128)(2,1)S(1)} %shard_map.131.refs_0_), channel_id=1, source_target_pairs={{0,1},{1,0},{2,3},{3,2},{4,5},{5,4},{6,7},{7,6},{8,10},{9,11},{10,... | collective-permute-start | bytes 196616 | tf_op jit(solution)/shard_map/ppermute | solution.py:39
  46.7 4.6 %collective-permute-start.15 = (bf16[128,256]{1,0:T(8,128)(2,1)S(1)}, bf16[128,256]{1,0:T(8,128)(2,1)S(1)}, u32[]{:S(2)}, u32[]{:S(2)}) collective-permute-start(bf16[128,256]{1,0:T(8,128)(2,1)S(1)} %shard_map.131.refs_0_), channel_id=1, source_target_pairs={{0,2},{1,3},{2,0},{3,1},{4,6},{5,7},{6,4},{7,5},{8,9},{9,8},{10,11... | collective-permute-start | bytes 196616 | tf_op jit(solution)/shard_map/ppermute | solution.py:39
  47.0 5.2 %collective-permute-start.16 = (bf16[128,256]{1,0:T(8,128)(2,1)S(1)}, bf16[128,256]{1,0:T(8,128)(2,1)S(1)}, u32[]{:S(2)}, u32[]{:S(2)}) collective-permute-start(bf16[128,256]{1,0:T(8,128)(2,1)S(1)} %shard_map.131.refs_0_), channel_id=1, source_target_pairs={{0,3},{1,2},{2,1},{3,0},{4,7},{5,6},{6,5},{7,4},{8,11},{9,10},{10,... | collective-permute-start | bytes 196616 | tf_op jit(solution)/shard_map/ppermute | solution.py:39
  48.3 5.2 %collective-permute-start.18 = (bf16[64,512]{1,0:T(8,128)(2,1)S(1)}, bf16[64,512]{1,0:T(8,128)(2,1)S(1)}, u32[]{:S(2)}, u32[]{:S(2)}) collective-permute-start(bf16[64,512]{1,0:T(8,128)(2,1)S(1)} %get-tuple-element.69), channel_id=1, source_target_pairs={{0,4},{1,5},{2,6},{3,7},{4,0},{5,1},{6,2},{7,3},{8,12},{9,13},{10,... | collective-permute-start | bytes 196616 | tf_op jit(solution)/shard_map/ppermute | solution.py:30
  (4 other events, 21.8 us)

commit v6 on v5

--- a/solution.py
+++ b/solution.py
@@ -349,33 +349,47 @@
     )(kinv, keep, got)
 
 
-def top_end_kernel(rels, kinv, *refs):
-    parts, out, loads = refs[:-2], refs[-2], refs[-1]
+def solve_kernel(kinv, keep, got, out):
+    sr, height = kinv.shape[1], out.shape[0]
+    high = (lax.axis_index("leaf") >> 1) & 1
+    loads = (keep[...].astype(F32) + got[...].astype(F32)).astype(BF16)
+    for b in range(height // sr):
+        at = pl.ds(pl.multiple_of(high * height + b * sr, sr), sr)
+        out[b * sr : (b + 1) * sr, :] = solve(kinv[at, :], loads[b * sr : (b + 1) * sr]).astype(BF16)
+
+
+def solve_call(kinv, keep, got):
+    return pl.pallas_call(
+        solve_kernel,
+        in_specs=[VMEM] * 3,
+        out_specs=VMEM,
+        out_shape=jax.ShapeDtypeStruct(keep.shape, BF16),
+        compiler_params=params(4),
+        cost_estimate=cost(12 * keep.size * 64, 8 * keep.size),
+    )(kinv, keep, got)
+
+
+def top_end_kernel(rels, *refs):
+    parts, out = refs[:-1], refs[-1]
     leaf = lax.axis_index("leaf")
     even = (lax.axis_index("group") & 1) == 0
-    sr = kinv.shape[1]
     for part, (r_even, r_odd) in zip(parts, rels):
         height, width = part.shape
         there = leaf ^ jnp.where(even, r_even, r_odd)
         row = pl.multiple_of(((there >> 1) & 1) * height, height)
         col = pl.multiple_of((there & 1) * width, 128)
-        loads[pl.ds(row, height), pl.ds(col, width)] = part[...]
-    for b in range(out.shape[0] // sr):
-        at = slice(b * sr, (b + 1) * sr)
-        out[at, :] = solve(kinv[at, :], loads[at, :])
-
-
-def top_end_call(parts, rels, kinv, m):
-    rows = kinv.shape[0]
+        out[pl.ds(row, height), pl.ds(col, width)] = part[...].astype(F32)
+
+
+def top_end_call(parts, rels, rows, m):
     return pl.pallas_call(
         functools.partial(top_end_kernel, rels),
-        in_specs=[VMEM] * (1 + len(parts)),
+        in_specs=[VMEM] * len(parts),
         out_specs=VMEM,
         out_shape=jax.ShapeDtypeStruct((rows, m), F32),
-        scratch_shapes=[pltpu.VMEM((rows, m), BF16)],
         compiler_params=params(8),
-        cost_estimate=cost(12 * rows * m * 64, 8 * rows * m),
-    )(kinv, *parts)
+        cost_estimate=cost(rows * m, 6 * rows * m),
+    )(*parts)
 
 
 def per_device(
@@ -418,8 +432,8 @@
     leaf_proj = proj_call(mt, weighted)
     got, leaf_proj = lax.optimization_barrier((got, leaf_proj))
     keep, near, other, across = quarter_call(keep, got)
-    got = [send_by_core(x, *there) for x, *there in ((across, (0, 3), (2, 2)), (other, (0, 2), (2, 0)), (near, (0, 1), (0, 2)))]
-    low_keep, got[1] = lax.optimization_barrier((low_keep, got[1]))
+    got = [send_by_core(x, *there) for x, *there in ((other, (0, 2), (2, 0)), (across, (0, 3), (2, 2)), (near, (0, 1), (0, 2)))]
+    low_keep, got[0] = lax.optimization_barrier((low_keep, got[0]))
     low_keep, low_send = part_call(low_keep, [low_got], 2, 1)
     low_got = send_by_core(low_send, (0, 1), (0, 2))
     total = sum_call(keep, got)
@@ -427,11 +441,15 @@
     for bit in range(2, leaves.bit_length() - 1):
         low_keep, low_send = part_call(low_keep, [low_got], 2, 1)
         low_got = send_leaf(low_send, 1 << bit)
-        total = sum_call(total, [send_leaf(total, 1 << bit)])
-    rels = ((0, 0), (1, 2), (2, 1), (3, 3))
+        got = send_leaf(total, 1 << bit)
+        if bit == leaves.bit_length() - 2:
+            total = solve_call(kinv_top, total, got)
+        else:
+            total = sum_call(total, [got])
+    rels = ((0, 0), (3, 3), (2, 1), (1, 2))
     parts = [total] + [send_by_core(total, (0, even), (0, odd)) for even, odd in rels[1:]]
     new_low = low_end_call(kinv_low, low_keep, low_got)
-    new_top = top_end_call(parts, rels, kinv_top, m)
+    new_top = top_end_call(parts, rels, kinv_top.shape[0], m)
     return (new_top, new_low, leaf_proj)
 
 

time: 54.5 us -> 54.7 us (level)
  transfers between devices with their start and end apart: 19 -> 19, of which waited for: 10 -> 11; matrix products, arithmetic and copies ran while one was open for 0% -> 0% of each run, Pallas kernels for 18% -> 17%
where the time goes in v6:
time: 54.7 us; the launch traced here: 54.5 us
  starting transfers between devices  27.2 us (50%)
  Pallas kernels  15.4 us (28%)
  waiting for transfers between devices  11 us (20%)
  between operations  0.86 us (2%)
    ppermute x12, starting transfers between devices, send_by_core(): return lax.ppermute(x, ('group', 'leaf'), pairs)  15.4 us
    ppermute x3, starting transfers between devices, send_leaf(): lax.ppermute(x, 'leaf', [(i, i ^ k) for i in range(lax.axis_size('leaf'))])  9.28 us
    ppermute x12, waiting for transfers between devices, send_by_core(): return lax.ppermute(x, ('group', 'leaf'), pairs)  6.3 us
    pallas_call x1, Pallas kernels, main_call(): pl.pallas_call(functools.partial(main_kernel, per_group, low_rels), in_sp...  5 us
    ppermute x3, waiting for transfers between devices, send_leaf(): lax.ppermute(x, 'leaf', [(i, i ^ k) for i in range(lax.axis_size('leaf'))])  3.95 us
    pallas_call x2, Pallas kernels, load_call(): pl.pallas_call(functools.partial(load_kernel, turned, step), in_specs=[HB...  3.58 us
    ppermute x4, starting transfers between devices, send_group(): lax.ppermute(x, 'group', [(i, i ^ k) for i in range(lax.axis_size('group'...  2.48 us
    pallas_call x1, Pallas kernels, first_call(): pl.pallas_call(functools.partial(first_kernel, len(tops)), in_specs=[SMEM...  1.99 us
  transfers between devices with their start and end apart: 19, of which 11 were waited for; matrix products, arithmetic and copies ran while one was open for 0% of the time, Pallas kernels for 17%

profile of v6, /device:TPU:0, one launch (start us, length us, event | category | flops | bytes accessed | tf_op | source)
XLA Modules:
  0.0 54.5 jit_solution(4281206501882688184)
XLA Ops:
  1.2 3.7 %collective-permute-start = (bf16[64,512]{1,0:T(8,128)(2,1)}, bf16[64,512]{1,0:T(8,128)(2,1)S(1)}, u32[]{:S(2)}, u32[]{:S(2)}) collective-permute-start(bf16[64,512]{1,0:T(8,128)(2,1)} %param.11), channel_id=1, source_target_pairs={{0,4},{1,5},{2,6},{3,7},{4,0},{5,1},{6,2},{7,3},{8,12},{9,13},{10,... | collective-permute-start | bytes 196616 | tf_op jit(solution)/shard_map/ppermute | solution.py:30
  4.8 1.5 %collective-permute-start.5 = (bf16[256,512]{1,0:T(8,128)(2,1)}, bf16[256,512]{1,0:T(8,128)(2,1)S(1)}, u32[]{:S(2)}, u32[]{:S(2)}) collective-permute-start(bf16[256,512]{1,0:T(8,128)(2,1)} %refs_0_.5), channel_id=1, source_target_pairs={{0,16},{8,24},{16,0},{24,8},{1,17},{9,25},{17,1},{25,9},{2,18},{10... | collective-permute-start | bytes 786440 | tf_op jit(solution)/shard_map/ppermute | solution.py:26
  6.3 1.3 %shard_map.122 = (bf16[1536,128]{1,0:T(8,128)(2,1)S(1)}, bf16[128,1536]{1,0:T(8,128)(2,1)S(1)}) custom-call(bf16[1536,128]{1,0:T(8,128)(2,1)} %refs_0_.4), custom_call_target="tpu_custom_call" | custom-call | flops 20000000000 | bytes 393216 | tf_op jit(solution)/shard_map/pallas_call | solution.py:72
  7.7 1.4 %collective-permute-done = bf16[64,512]{1,0:T(8,128)(2,1)S(1)} collective-permute-done((bf16[64,512]{1,0:T(8,128)(2,1)}, bf16[64,512]{1,0:T(8,128)(2,1)S(1)}, u32[]{:S(2)}, u32[]{:S(2)}) %collective-permute-start) | collective-permute-done | bytes 65568 | tf_op jit(solution)/shard_map/ppermute | solution.py:30
  9.2 1.9 %collective-permute-start.1 = (bf16[128,512]{1,0:T(8,128)(2,1)S(1)}, bf16[128,512]{1,0:T(8,128)(2,1)S(1)}, u32[]{:S(2)}, u32[]{:S(2)}) collective-permute-start(bf16[128,512]{1,0:T(8,128)(2,1)S(1)} %constant_dynamic-update-slice_fusion.refs_0_), channel_id=1, source_target_pairs={{0,3},{1,2},{2,1},{3,0},{4,7},{5,6},{6,5},{7,4},{8,11},{9,10},{10,... | collective-permute-start | bytes 393224 | tf_op jit(solution)/shard_map/ppermute | solution.py:39
  11.0 1.3 %collective-permute-start.2 = (bf16[128,512]{1,0:T(8,128)(2,1)S(1)}, bf16[128,512]{1,0:T(8,128)(2,1)S(1)}, u32[]{:S(2)}, u32[]{:S(2)}) collective-permute-start(bf16[128,512]{1,0:T(8,128)(2,1)S(1)} %constant_dynamic-update-slice_fusion.refs_0_), channel_id=1, source_target_pairs={{0,2},{1,3},{2,0},{3,1},{4,6},{5,7},{6,4},{7,5},{8,9},{9,8},{10,11... | collective-permute-start | bytes 393224 | tf_op jit(solution)/shard_map/ppermute | solution.py:39
  13.4 2.2 %shard_map.121 = (bf16[1536,1024]{1,0:T(8,128)(2,1)S(1)}, bf16[1024,1536]{1,0:T(8,128)(2,1)S(1)}) custom-call(bf16[1536,1024]{1,0:T(8,128)(2,1)} %refs_0_.3), custom_call_target="tpu_custom_call" | custom-call | flops 20000000000 | bytes 3145728 | tf_op jit(solution)/shard_map/pallas_call | solution.py:72
  15.7 2.0 %shard_map.123.refs_4_ = f32[1536,512]{1,0:T(8,128)S(1)} custom-call(s32[1,8]{1,0:T(1,128)S(1)} %copy-done.3, bf16[256,512]{1,0:T(8,128)(2,1)S(1)} %copy-done, bf16[256,512]{1,0:T(8,128)(2,1)S(1)} %collective-permute-done.4.refs_1_, bf16[256,512]{1,0:T(8,128)(2,1)S(1)} %collective-permute-done.5.refs_2_, ...), custom_call_target="tpu_custom_call" | custom-call | tf_op jit(solution)/shard_map/pallas_call | solution.py:113
  17.9 5.0 %shard_map.124 = (bf16[1024,256]{1,0:T(8,128)(2,1)S(1)}, f32[1024,256]{1,0:T(8,128)S(1)}, bf16[1536,512]{1,0:T(8,128)(2,1)S(1)}) custom-call(s32[1,8]{1,0:T(1,128)S(1)} %copy-done.3, s32[1,8]{1,0:T(1,128)S(1)} %copy-done.4, bf16[128,512]{1,0:T(8,128)(2,1)S(1)} %constant_dynamic-update-slice_fusion.refs_0_, ...), custom_call_target="tpu_custom_call" | custom-call | flops 4026531840 | bytes 6291456 | tf_op jit(solution)/shard_map/pallas_call | solution.py:179
  23.4 1.6 %shard_map.125 = (f32[256,512]{1,0:T(8,128)S(1)}, bf16[256,512]{1,0:T(8,128)(2,1)S(1)}) custom-call(s32[1,8]{1,0:T(1,128)S(1)} %copy-done.4, bf16[1024,1536]{1,0:T(8,128)(2,1)S(1)} %get-tuple-element.37.refs_7_.ct, bf16[1536,512]{1,0:T(8,128)(2,1)S(1)} %get-tuple-element.55.weighted), custom_call_target="tpu_custom_call" | custom-call | flops 805306368 | bytes 3145728 | tf_op jit(solution)/shard_map/pallas_call | solution.py:240
  25.1 1.6 %collective-permute-start.8 = (bf16[512,256]{1,0:T(8,128)(2,1)S(1)}, bf16[512,256]{1,0:T(8,128)(2,1)S(1)}, u32[]{:S(2)}, u32[]{:S(2)}) collective-permute-start(bf16[512,256]{1,0:T(8,128)(2,1)S(1)} %get-tuple-element.53), channel_id=1, source_target_pairs={{0,16},{1,17},{2,18},{3,19},{4,20},{5,21},{6,22},{7,23},{8,9},{9,8... | collective-permute-start | bytes 786440 | tf_op jit(solution)/shard_map/ppermute | solution.py:39
  26.6 1.6 %collective-permute-start.10 = (bf16[256,512]{1,0:T(8,128)(2,1)S(1)}, bf16[256,512]{1,0:T(8,128)(2,1)S(1)}, u32[]{:S(2)}, u32[]{:S(2)}) collective-permute-start(bf16[256,512]{1,0:T(8,128)(2,1)S(1)} %get-tuple-element.59), channel_id=1, source_target_pairs={{0,2},{1,3},{2,0},{3,1},{4,6},{5,7},{6,4},{7,5},{8,9},{9,8},{10,11... | collective-permute-start | bytes 786440 | tf_op jit(solution)/shard_map/ppermute | solution.py:39
  28.2 1.0 %shard_map.127 = bf16[128,512]{1,0:T(8,128)(2,1)} custom-call(bf16[128,1536]{1,0:T(8,128)(2,1)S(1)} %get-tuple-element.54.mt, bf16[1536,512]{1,0:T(8,128)(2,1)S(1)} %get-tuple-element.55.weighted), custom_call_target="tpu_custom_call" | custom-call | flops 20000000000 | bytes 1572864 | tf_op jit(solution)/shard_map/pallas_call | solution.py:226
  29.2 2.3 %collective-permute-done.8.got = bf16[512,256]{1,0:T(8,128)(2,1)S(1)} collective-permute-done((bf16[512,256]{1,0:T(8,128)(2,1)S(1)}, bf16[512,256]{1,0:T(8,128)(2,1)S(1)}, u32[]{:S(2)}, u32[]{:S(2)}) %collective-permute-start.8) | collective-permute-done | bytes 262176 | tf_op jit(solution)/shard_map/ppermute | solution.py:39
  31.5 1.6 %collective-permute-start.9 = (bf16[128,256]{1,0:T(8,128)(2,1)S(1)}, bf16[128,256]{1,0:T(8,128)(2,1)S(1)}, u32[]{:S(2)}, u32[]{:S(2)}) collective-permute-start(bf16[128,256]{1,0:T(8,128)(2,1)S(1)} %get-tuple-element.57), channel_id=1, source_target_pairs={{0,2},{1,3},{2,0},{3,1},{4,6},{5,7},{6,4},{7,5},{8,24},{9,25},{10,... | collective-permute-start | bytes 196616 | tf_op jit(solution)/shard_map/ppermute | solution.py:39
  33.2 1.4 %collective-permute-start.11 = (bf16[128,256]{1,0:T(8,128)(2,1)S(1)}, bf16[128,256]{1,0:T(8,128)(2,1)S(1)}, u32[]{:S(2)}, u32[]{:S(2)}) collective-permute-start(bf16[128,256]{1,0:T(8,128)(2,1)S(1)} %get-tuple-element.63), channel_id=1, source_target_pairs={{0,3},{1,2},{2,1},{3,0},{4,7},{5,6},{6,5},{7,4},{8,26},{9,27},{10,... | collective-permute-start | bytes 196616 | tf_op jit(solution)/shard_map/ppermute | solution.py:39
  35.1 1.2 %collective-permute-done.9.refs_0_ = bf16[128,256]{1,0:T(8,128)(2,1)S(1)} collective-permute-done((bf16[128,256]{1,0:T(8,128)(2,1)S(1)}, bf16[128,256]{1,0:T(8,128)(2,1)S(1)}, u32[]{:S(2)}, u32[]{:S(2)}) %collective-permute-start.9) | collective-permute-done | bytes 65568 | tf_op jit(solution)/shard_map/ppermute | solution.py:39
  36.4 1.6 %collective-permute-start.17 = (bf16[128,512]{1,0:T(8,128)(2,1)S(1)}, bf16[128,512]{1,0:T(8,128)(2,1)S(1)}, u32[]{:S(2)}, u32[]{:S(2)}) collective-permute-start(bf16[128,512]{1,0:T(8,128)(2,1)S(1)} %get-tuple-element.67), channel_id=1, source_target_pairs={{0,1},{1,0},{2,3},{3,2},{4,5},{5,4},{6,7},{7,6},{8,10},{9,11},{10,... | collective-permute-start | bytes 393224 | tf_op jit(solution)/shard_map/ppermute | solution.py:39
  39.3 2.8 %collective-permute-start.13 = (bf16[128,256]{1,0:T(8,128)(2,1)S(1)}, bf16[128,256]{1,0:T(8,128)(2,1)S(1)}, u32[]{:S(2)}, u32[]{:S(2)}) collective-permute-start(bf16[128,256]{1,0:T(8,128)(2,1)S(1)} %shard_map.130.keep), channel_id=1, source_target_pairs={{0,4},{1,5},{2,6},{3,7},{4,0},{5,1},{6,2},{7,3},{8,12},{9,13},{10,... | collective-permute-start | bytes 196616 | tf_op jit(solution)/shard_map/ppermute | solution.py:30
  42.2 2.4 %collective-permute-done.13.got = bf16[128,256]{1,0:T(8,128)(2,1)S(1)} collective-permute-done((bf16[128,256]{1,0:T(8,128)(2,1)S(1)}, bf16[128,256]{1,0:T(8,128)(2,1)S(1)}, u32[]{:S(2)}, u32[]{:S(2)}) %collective-permute-start.13) | collective-permute-done | bytes 65568 | tf_op jit(solution)/shard_map/ppermute | solution.py:30
  44.7 1.8 %collective-permute-start.14 = (bf16[128,256]{1,0:T(8,128)(2,1)S(1)}, bf16[128,256]{1,0:T(8,128)(2,1)S(1)}, u32[]{:S(2)}, u32[]{:S(2)}) collective-permute-start(bf16[128,256]{1,0:T(8,128)(2,1)S(1)} %shard_map.131.refs_0_), channel_id=1, source_target_pairs={{0,3},{1,2},{2,1},{3,0},{4,7},{5,6},{6,5},{7,4},{8,11},{9,10},{10,... | collective-permute-start | bytes 196616 | tf_op jit(solution)/shard_map/ppermute | solution.py:39
  46.6 1.7 %collective-permute-start.15 = (bf16[128,256]{1,0:T(8,128)(2,1)S(1)}, bf16[128,256]{1,0:T(8,128)(2,1)S(1)}, u32[]{:S(2)}, u32[]{:S(2)}) collective-permute-start(bf16[128,256]{1,0:T(8,128)(2,1)S(1)} %shard_map.131.refs_0_), channel_id=1, source_target_pairs={{0,2},{1,3},{2,0},{3,1},{4,6},{5,7},{6,4},{7,5},{8,9},{9,8},{10,11... | collective-permute-start | bytes 196616 | tf_op jit(solution)/shard_map/ppermute | solution.py:39
  48.4 2.8 %collective-permute-start.18 = (bf16[64,512]{1,0:T(8,128)(2,1)S(1)}, bf16[64,512]{1,0:T(8,128)(2,1)S(1)}, u32[]{:S(2)}, u32[]{:S(2)}) collective-permute-start(bf16[64,512]{1,0:T(8,128)(2,1)S(1)} %get-tuple-element.69), channel_id=1, source_target_pairs={{0,4},{1,5},{2,6},{3,7},{4,0},{5,1},{6,2},{7,3},{8,12},{9,13},{10,... | collective-permute-start | bytes 196616 | tf_op jit(solution)/shard_map/ppermute | solution.py:30
  51.3 1.3 %collective-permute-done.16.refs_3_ = bf16[128,256]{1,0:T(8,128)(2,1)S(1)} collective-permute-done((bf16[128,256]{1,0:T(8,128)(2,1)S(1)}, bf16[128,256]{1,0:T(8,128)(2,1)S(1)}, u32[]{:S(2)}, u32[]{:S(2)}) %collective-permute-start.16) | collective-permute-done | bytes 65568 | tf_op jit(solution)/shard_map/ppermute | solution.py:39
  (50 shorter events, 6.6 us)
Async XLA Ops:
  0.6 7.0 %copy-start.6 = (bf16[64,512]{1,0:T(8,128)(2,1)S(1)}, bf16[64,512]{1,0:T(8,128)(2,1)}, u32[]{:S(2)}) copy-start(bf16[64,512]{1,0:T(8,128)(2,1)} %param.11) | copy-start | bytes 196612
  0.6 4.2 %collective-permute-start.4 = (bf16[256,512]{1,0:T(8,128)(2,1)}, bf16[256,512]{1,0:T(8,128)(2,1)S(1)}, u32[]{:S(2)}, u32[]{:S(2)}) collective-permute-start(bf16[256,512]{1,0:T(8,128)(2,1)} %refs_0_.5), channel_id=1, source_target_pairs={{0,8},{8,0},{16,24},{24,16},{1,9},{9,1},{17,25},{25,17},{2,10},{10... | collective-permute-start | bytes 786440 | tf_op jit(solution)/shard_map/ppermute | solution.py:26
  1.2 8.0 %collective-permute-start = (bf16[64,512]{1,0:T(8,128)(2,1)}, bf16[64,512]{1,0:T(8,128)(2,1)S(1)}, u32[]{:S(2)}, u32[]{:S(2)}) collective-permute-start(bf16[64,512]{1,0:T(8,128)(2,1)} %param.11), channel_id=1, source_target_pairs={{0,4},{1,5},{2,6},{3,7},{4,0},{5,1},{6,2},{7,3},{8,12},{9,13},{10,... | collective-permute-start | bytes 196616 | tf_op jit(solution)/shard_map/ppermute | solution.py:30
  4.8 8.6 %collective-permute-start.5 = (bf16[256,512]{1,0:T(8,128)(2,1)}, bf16[256,512]{1,0:T(8,128)(2,1)S(1)}, u32[]{:S(2)}, u32[]{:S(2)}) collective-permute-start(bf16[256,512]{1,0:T(8,128)(2,1)} %refs_0_.5), channel_id=1, source_target_pairs={{0,16},{8,24},{16,0},{24,8},{1,17},{9,25},{17,1},{25,9},{2,18},{10... | collective-permute-start | bytes 786440 | tf_op jit(solution)/shard_map/ppermute | solution.py:26
  6.3 11.5 %slice-start = ((s8[4718592]{0:T(1024)(128)(4,1)}), s8[4194304]{0:T(1024)(128)(4,1)S(1)}, s32[]{:S(2)}) async-start(s8[4718592]{0:T(1024)(128)(4,1)} %bitcast), calls=%async_computation | async-start | bytes 8388608
  9.2 8.7 %slice-start.1 = ((s8[4718592]{0:T(1024)(128)(4,1)}), s8[524288]{0:T(1024)(128)(4,1)S(1)}, s32[]{:S(2)}) async-start(s8[4718592]{0:T(1024)(128)(4,1)} %bitcast), calls=%async_computation.1 | async-start | bytes 1048576
  9.2 8.5 %collective-permute-start.1 = (bf16[128,512]{1,0:T(8,128)(2,1)S(1)}, bf16[128,512]{1,0:T(8,128)(2,1)S(1)}, u32[]{:S(2)}, u32[]{:S(2)}) collective-permute-start(bf16[128,512]{1,0:T(8,128)(2,1)S(1)} %constant_dynamic-update-slice_fusion.refs_0_), channel_id=1, source_target_pairs={{0,3},{1,2},{2,1},{3,0},{4,7},{5,6},{6,5},{7,4},{8,11},{9,10},{10,... | collective-permute-start | bytes 393224 | tf_op jit(solution)/shard_map/ppermute | solution.py:39
  11.0 6.8 %collective-permute-start.2 = (bf16[128,512]{1,0:T(8,128)(2,1)S(1)}, bf16[128,512]{1,0:T(8,128)(2,1)S(1)}, u32[]{:S(2)}, u32[]{:S(2)}) collective-permute-start(bf16[128,512]{1,0:T(8,128)(2,1)S(1)} %constant_dynamic-update-slice_fusion.refs_0_), channel_id=1, source_target_pairs={{0,2},{1,3},{2,0},{3,1},{4,6},{5,7},{6,4},{7,5},{8,9},{9,8},{10,11... | collective-permute-start | bytes 393224 | tf_op jit(solution)/shard_map/ppermute | solution.py:39
  12.3 5.6 %collective-permute-start.3 = (bf16[128,512]{1,0:T(8,128)(2,1)S(1)}, bf16[128,512]{1,0:T(8,128)(2,1)S(1)}, u32[]{:S(2)}, u32[]{:S(2)}) collective-permute-start(bf16[128,512]{1,0:T(8,128)(2,1)S(1)} %constant_dynamic-update-slice_fusion.refs_0_), channel_id=1, source_target_pairs={{0,1},{1,0},{2,3},{3,2},{4,5},{5,4},{6,7},{7,6},{8,10},{9,11},{10,... | collective-permute-start | bytes 393224 | tf_op jit(solution)/shard_map/ppermute | solution.py:39
  13.4 2.2 %collective-permute-start.6 = (bf16[256,512]{1,0:T(8,128)(2,1)S(1)}, bf16[256,512]{1,0:T(8,128)(2,1)S(1)}, u32[]{:S(2)}, u32[]{:S(2)}) collective-permute-start(bf16[256,512]{1,0:T(8,128)(2,1)S(1)} %collective-permute-done.5.refs_2_), channel_id=1, source_target_pairs={{0,8},{8,0},{16,24},{24,16},{1,9},{9,1},{17,25},{25,17},{2,10},{10... | collective-permute-start | bytes 786440 | tf_op jit(solution)/shard_map/ppermute | solution.py:26
  22.9 2.1 %collective-permute-start.7 = (bf16[1024,256]{1,0:T(8,128)(2,1)S(1)}, bf16[1024,256]{1,0:T(8,128)(2,1)S(1)}, u32[]{:S(2)}, u32[]{:S(2)}) collective-permute-start(bf16[1024,256]{1,0:T(8,128)(2,1)S(1)} %get-tuple-element.47), channel_id=1, source_target_pairs={{0,8},{8,0},{16,24},{24,16},{1,9},{9,1},{17,25},{25,17},{2,10},{10... | collective-permute-start | bytes 1572872 | tf_op jit(solution)/shard_map/ppermute | solution.py:26
  25.0 17.0 %copy-start.5 = (f32[256,64]{0,1:T(8,128)S(1)}, f32[256,64]{0,1:T(8,128)}, u32[]{:S(2)}) copy-start(f32[256,64]{0,1:T(8,128)} %param.18) | copy-start | bytes 196612
  25.1 6.4 %collective-permute-start.8 = (bf16[512,256]{1,0:T(8,128)(2,1)S(1)}, bf16[512,256]{1,0:T(8,128)(2,1)S(1)}, u32[]{:S(2)}, u32[]{:S(2)}) collective-permute-start(bf16[512,256]{1,0:T(8,128)(2,1)S(1)} %get-tuple-element.53), channel_id=1, source_target_pairs={{0,16},{1,17},{2,18},{3,19},{4,20},{5,21},{6,22},{7,23},{8,9},{9,8... | collective-permute-start | bytes 786440 | tf_op jit(solution)/shard_map/ppermute | solution.py:39
  26.6 9.7 %collective-permute-start.10 = (bf16[256,512]{1,0:T(8,128)(2,1)S(1)}, bf16[256,512]{1,0:T(8,128)(2,1)S(1)}, u32[]{:S(2)}, u32[]{:S(2)}) collective-permute-start(bf16[256,512]{1,0:T(8,128)(2,1)S(1)} %get-tuple-element.59), channel_id=1, source_target_pairs={{0,2},{1,3},{2,0},{3,1},{4,6},{5,7},{6,4},{7,5},{8,9},{9,8},{10,11... | collective-permute-start | bytes 786440 | tf_op jit(solution)/shard_map/ppermute | solution.py:39
  29.2 24.4 %copy-start.2 = (f32[64,64]{1,0:T(8,128)S(1)}, f32[64,64]{1,0:T(8,128)}, u32[]{:S(2)}) copy-start(f32[64,64]{1,0:T(8,128)} %kinv.2) | copy-start | bytes 49156
  31.5 4.8 %collective-permute-start.9 = (bf16[128,256]{1,0:T(8,128)(2,1)S(1)}, bf16[128,256]{1,0:T(8,128)(2,1)S(1)}, u32[]{:S(2)}, u32[]{:S(2)}) collective-permute-start(bf16[128,256]{1,0:T(8,128)(2,1)S(1)} %get-tuple-element.57), channel_id=1, source_target_pairs={{0,2},{1,3},{2,0},{3,1},{4,6},{5,7},{6,4},{7,5},{8,24},{9,25},{10,... | collective-permute-start | bytes 196616 | tf_op jit(solution)/shard_map/ppermute | solution.py:39
  33.2 5.8 %collective-permute-start.11 = (bf16[128,256]{1,0:T(8,128)(2,1)S(1)}, bf16[128,256]{1,0:T(8,128)(2,1)S(1)}, u32[]{:S(2)}, u32[]{:S(2)}) collective-permute-start(bf16[128,256]{1,0:T(8,128)(2,1)S(1)} %get-tuple-element.63), channel_id=1, source_target_pairs={{0,3},{1,2},{2,1},{3,0},{4,7},{5,6},{6,5},{7,4},{8,26},{9,27},{10,... | collective-permute-start | bytes 196616 | tf_op jit(solution)/shard_map/ppermute | solution.py:39
  34.6 4.7 %collective-permute-start.12 = (bf16[128,256]{1,0:T(8,128)(2,1)S(1)}, bf16[128,256]{1,0:T(8,128)(2,1)S(1)}, u32[]{:S(2)}, u32[]{:S(2)}) collective-permute-start(bf16[128,256]{1,0:T(8,128)(2,1)S(1)} %get-tuple-element.64), channel_id=1, source_target_pairs={{0,1},{1,0},{2,3},{3,2},{4,5},{5,4},{6,7},{7,6},{8,10},{9,11},{10,... | collective-permute-start | bytes 196616 | tf_op jit(solution)/shard_map/ppermute | solution.py:39
  36.4 11.9 %collective-permute-start.17 = (bf16[128,512]{1,0:T(8,128)(2,1)S(1)}, bf16[128,512]{1,0:T(8,128)(2,1)S(1)}, u32[]{:S(2)}, u32[]{:S(2)}) collective-permute-start(bf16[128,512]{1,0:T(8,128)(2,1)S(1)} %get-tuple-element.67), channel_id=1, source_target_pairs={{0,1},{1,0},{2,3},{3,2},{4,5},{5,4},{6,7},{7,6},{8,10},{9,11},{10,... | collective-permute-start | bytes 393224 | tf_op jit(solution)/shard_map/ppermute | solution.py:39
  39.3 5.2 %collective-permute-start.13 = (bf16[128,256]{1,0:T(8,128)(2,1)S(1)}, bf16[128,256]{1,0:T(8,128)(2,1)S(1)}, u32[]{:S(2)}, u32[]{:S(2)}) collective-permute-start(bf16[128,256]{1,0:T(8,128)(2,1)S(1)} %shard_map.130.keep), channel_id=1, source_target_pairs={{0,4},{1,5},{2,6},{3,7},{4,0},{5,1},{6,2},{7,3},{8,12},{9,13},{10,... | collective-permute-start | bytes 196616 | tf_op jit(solution)/shard_map/ppermute | solution.py:30
  44.7 6.5 %collective-permute-start.14 = (bf16[128,256]{1,0:T(8,128)(2,1)S(1)}, bf16[128,256]{1,0:T(8,128)(2,1)S(1)}, u32[]{:S(2)}, u32[]{:S(2)}) collective-permute-start(bf16[128,256]{1,0:T(8,128)(2,1)S(1)} %shard_map.131.refs_0_), channel_id=1, source_target_pairs={{0,3},{1,2},{2,1},{3,0},{4,7},{5,6},{6,5},{7,4},{8,11},{9,10},{10,... | collective-permute-start | bytes 196616 | tf_op jit(solution)/shard_map/ppermute | solution.py:39
  46.6 4.7 %collective-permute-start.15 = (bf16[128,256]{1,0:T(8,128)(2,1)S(1)}, bf16[128,256]{1,0:T(8,128)(2,1)S(1)}, u32[]{:S(2)}, u32[]{:S(2)}) collective-permute-start(bf16[128,256]{1,0:T(8,128)(2,1)S(1)} %shard_map.131.refs_0_), channel_id=1, source_target_pairs={{0,2},{1,3},{2,0},{3,1},{4,6},{5,7},{6,4},{7,5},{8,9},{9,8},{10,11... | collective-permute-start | bytes 196616 | tf_op jit(solution)/shard_map/ppermute | solution.py:39
  48.3 4.3 %collective-permute-start.16 = (bf16[128,256]{1,0:T(8,128)(2,1)S(1)}, bf16[128,256]{1,0:T(8,128)(2,1)S(1)}, u32[]{:S(2)}, u32[]{:S(2)}) collective-permute-start(bf16[128,256]{1,0:T(8,128)(2,1)S(1)} %shard_map.131.refs_0_), channel_id=1, source_target_pairs={{0,1},{1,0},{2,3},{3,2},{4,5},{5,4},{6,7},{7,6},{8,10},{9,11},{10,... | collective-permute-start | bytes 196616 | tf_op jit(solution)/shard_map/ppermute | solution.py:39
  48.4 5.2 %collective-permute-start.18 = (bf16[64,512]{1,0:T(8,128)(2,1)S(1)}, bf16[64,512]{1,0:T(8,128)(2,1)S(1)}, u32[]{:S(2)}, u32[]{:S(2)}) collective-permute-start(bf16[64,512]{1,0:T(8,128)(2,1)S(1)} %get-tuple-element.69), channel_id=1, source_target_pairs={{0,4},{1,5},{2,6},{3,7},{4,0},{5,1},{6,2},{7,3},{8,12},{9,13},{10,... | collective-permute-start | bytes 196616 | tf_op jit(solution)/shard_map/ppermute | solution.py:30
  (4 other events, 21.8 us)

commit v7 on v5

--- a/solution.py
+++ b/solution.py
@@ -418,8 +418,8 @@
     leaf_proj = proj_call(mt, weighted)
     got, leaf_proj = lax.optimization_barrier((got, leaf_proj))
     keep, near, other, across = quarter_call(keep, got)
-    got = [send_by_core(x, *there) for x, *there in ((across, (0, 3), (2, 2)), (other, (0, 2), (2, 0)), (near, (0, 1), (0, 2)))]
-    low_keep, got[1] = lax.optimization_barrier((low_keep, got[1]))
+    got = [send_by_core(x, *there) for x, *there in ((other, (0, 2), (2, 0)), (across, (0, 3), (2, 2)), (near, (0, 1), (0, 2)))]
+    low_keep, got[0] = lax.optimization_barrier((low_keep, got[0]))
     low_keep, low_send = part_call(low_keep, [low_got], 2, 1)
     low_got = send_by_core(low_send, (0, 1), (0, 2))
     total = sum_call(keep, got)
@@ -428,7 +428,7 @@
         low_keep, low_send = part_call(low_keep, [low_got], 2, 1)
         low_got = send_leaf(low_send, 1 << bit)
         total = sum_call(total, [send_leaf(total, 1 << bit)])
-    rels = ((0, 0), (1, 2), (2, 1), (3, 3))
+    rels = ((0, 0), (3, 3), (2, 1), (1, 2))
     parts = [total] + [send_by_core(total, (0, even), (0, odd)) for even, odd in rels[1:]]
     new_low = low_end_call(kinv_low, low_keep, low_got)
     new_top = top_end_call(parts, rels, kinv_top, m)

time: 54.5 us -> 54.5 us (level)
  transfers between devices with their start and end apart: 19 -> 19, of which waited for: 10 -> 9; matrix products, arithmetic and copies ran while one was open for 0% -> 0% of each run, Pallas kernels for 18% -> 17%
where the time goes in v7:
time: 54.5 us; the launch traced here: 54.4 us
  starting transfers between devices  27.2 us (50%)
  Pallas kernels  15.5 us (28%)
  waiting for transfers between devices  10.7 us (20%)
  between operations  0.87 us (2%)
    ppermute x12, starting transfers between devices, send_by_core(): return lax.ppermute(x, ('group', 'leaf'), pairs)  15.4 us
    ppermute x3, starting transfers between devices, send_leaf(): lax.ppermute(x, 'leaf', [(i, i ^ k) for i in range(lax.axis_size('leaf'))])  9.31 us
    ppermute x12, waiting for transfers between devices, send_by_core(): return lax.ppermute(x, ('group', 'leaf'), pairs)  6.1 us
    pallas_call x1, Pallas kernels, main_call(): pl.pallas_call(functools.partial(main_kernel, per_group, low_rels), in_sp...  5 us
    ppermute x3, waiting for transfers between devices, send_leaf(): lax.ppermute(x, 'leaf', [(i, i ^ k) for i in range(lax.axis_size('leaf'))])  3.89 us
    pallas_call x2, Pallas kernels, load_call(): pl.pallas_call(functools.partial(load_kernel, turned, step), in_specs=[HB...  3.58 us
    ppermute x4, starting transfers between devices, send_group(): lax.ppermute(x, 'group', [(i, i ^ k) for i in range(lax.axis_size('group'...  2.48 us
    pallas_call x1, Pallas kernels, first_call(): pl.pallas_call(functools.partial(first_kernel, len(tops)), in_specs=[SMEM...  1.99 us
  transfers between devices with their start and end apart: 19, of which 9 were waited for; matrix products, arithmetic and copies ran while one was open for 0% of the time, Pallas kernels for 17%

profile of v7, /device:TPU:0, one launch (start us, length us, event | category | flops | bytes accessed | tf_op | source)
XLA Modules:
  0.0 54.4 jit_solution(10055414439551919583)
XLA Ops:
  1.2 3.7 %collective-permute-start = (bf16[64,512]{1,0:T(8,128)(2,1)}, bf16[64,512]{1,0:T(8,128)(2,1)S(1)}, u32[]{:S(2)}, u32[]{:S(2)}) collective-permute-start(bf16[64,512]{1,0:T(8,128)(2,1)} %param.11), channel_id=1, source_target_pairs={{0,4},{1,5},{2,6},{3,7},{4,0},{5,1},{6,2},{7,3},{8,12},{9,13},{10,... | collective-permute-start | bytes 196616 | tf_op jit(solution)/shard_map/ppermute | solution.py:30
  4.8 1.5 %collective-permute-start.5 = (bf16[256,512]{1,0:T(8,128)(2,1)}, bf16[256,512]{1,0:T(8,128)(2,1)S(1)}, u32[]{:S(2)}, u32[]{:S(2)}) collective-permute-start(bf16[256,512]{1,0:T(8,128)(2,1)} %refs_0_.5), channel_id=1, source_target_pairs={{0,16},{8,24},{16,0},{24,8},{1,17},{9,25},{17,1},{25,9},{2,18},{10... | collective-permute-start | bytes 786440 | tf_op jit(solution)/shard_map/ppermute | solution.py:26
  6.3 1.3 %shard_map.122 = (bf16[1536,128]{1,0:T(8,128)(2,1)S(1)}, bf16[128,1536]{1,0:T(8,128)(2,1)S(1)}) custom-call(bf16[1536,128]{1,0:T(8,128)(2,1)} %refs_0_.4), custom_call_target="tpu_custom_call" | custom-call | flops 20000000000 | bytes 393216 | tf_op jit(solution)/shard_map/pallas_call | solution.py:72
  7.7 1.4 %collective-permute-done = bf16[64,512]{1,0:T(8,128)(2,1)S(1)} collective-permute-done((bf16[64,512]{1,0:T(8,128)(2,1)}, bf16[64,512]{1,0:T(8,128)(2,1)S(1)}, u32[]{:S(2)}, u32[]{:S(2)}) %collective-permute-start) | collective-permute-done | bytes 65568 | tf_op jit(solution)/shard_map/ppermute | solution.py:30
  9.2 1.9 %collective-permute-start.1 = (bf16[128,512]{1,0:T(8,128)(2,1)S(1)}, bf16[128,512]{1,0:T(8,128)(2,1)S(1)}, u32[]{:S(2)}, u32[]{:S(2)}) collective-permute-start(bf16[128,512]{1,0:T(8,128)(2,1)S(1)} %constant_dynamic-update-slice_fusion.refs_0_), channel_id=1, source_target_pairs={{0,3},{1,2},{2,1},{3,0},{4,7},{5,6},{6,5},{7,4},{8,11},{9,10},{10,... | collective-permute-start | bytes 393224 | tf_op jit(solution)/shard_map/ppermute | solution.py:39
  11.0 1.3 %collective-permute-start.2 = (bf16[128,512]{1,0:T(8,128)(2,1)S(1)}, bf16[128,512]{1,0:T(8,128)(2,1)S(1)}, u32[]{:S(2)}, u32[]{:S(2)}) collective-permute-start(bf16[128,512]{1,0:T(8,128)(2,1)S(1)} %constant_dynamic-update-slice_fusion.refs_0_), channel_id=1, source_target_pairs={{0,2},{1,3},{2,0},{3,1},{4,6},{5,7},{6,4},{7,5},{8,9},{9,8},{10,11... | collective-permute-start | bytes 393224 | tf_op jit(solution)/shard_map/ppermute | solution.py:39
  13.4 2.2 %shard_map.121 = (bf16[1536,1024]{1,0:T(8,128)(2,1)S(1)}, bf16[1024,1536]{1,0:T(8,128)(2,1)S(1)}) custom-call(bf16[1536,1024]{1,0:T(8,128)(2,1)} %refs_0_.3), custom_call_target="tpu_custom_call" | custom-call | flops 20000000000 | bytes 3145728 | tf_op jit(solution)/shard_map/pallas_call | solution.py:72
  15.7 2.0 %shard_map.123.refs_4_ = f32[1536,512]{1,0:T(8,128)S(1)} custom-call(s32[1,8]{1,0:T(1,128)S(1)} %copy-done.3, bf16[256,512]{1,0:T(8,128)(2,1)S(1)} %copy-done, bf16[256,512]{1,0:T(8,128)(2,1)S(1)} %collective-permute-done.4.refs_1_, bf16[256,512]{1,0:T(8,128)(2,1)S(1)} %collective-permute-done.5.refs_2_, ...), custom_call_target="tpu_custom_call" | custom-call | tf_op jit(solution)/shard_map/pallas_call | solution.py:113
  17.9 5.0 %shard_map.124 = (bf16[1024,256]{1,0:T(8,128)(2,1)S(1)}, f32[1024,256]{1,0:T(8,128)S(1)}, bf16[1536,512]{1,0:T(8,128)(2,1)S(1)}) custom-call(s32[1,8]{1,0:T(1,128)S(1)} %copy-done.3, s32[1,8]{1,0:T(1,128)S(1)} %copy-done.4, bf16[128,512]{1,0:T(8,128)(2,1)S(1)} %constant_dynamic-update-slice_fusion.refs_0_, ...), custom_call_target="tpu_custom_call" | custom-call | flops 4026531840 | bytes 6291456 | tf_op jit(solution)/shard_map/pallas_call | solution.py:179
  23.4 1.6 %shard_map.125 = (f32[256,512]{1,0:T(8,128)S(1)}, bf16[256,512]{1,0:T(8,128)(2,1)S(1)}) custom-call(s32[1,8]{1,0:T(1,128)S(1)} %copy-done.4, bf16[1024,1536]{1,0:T(8,128)(2,1)S(1)} %get-tuple-element.37.refs_7_.ct, bf16[1536,512]{1,0:T(8,128)(2,1)S(1)} %get-tuple-element.55.weighted), custom_call_target="tpu_custom_call" | custom-call | flops 805306368 | bytes 3145728 | tf_op jit(solution)/shard_map/pallas_call | solution.py:240
  25.1 1.6 %collective-permute-start.8 = (bf16[512,256]{1,0:T(8,128)(2,1)S(1)}, bf16[512,256]{1,0:T(8,128)(2,1)S(1)}, u32[]{:S(2)}, u32[]{:S(2)}) collective-permute-start(bf16[512,256]{1,0:T(8,128)(2,1)S(1)} %get-tuple-element.53), channel_id=1, source_target_pairs={{0,16},{1,17},{2,18},{3,19},{4,20},{5,21},{6,22},{7,23},{8,9},{9,8... | collective-permute-start | bytes 786440 | tf_op jit(solution)/shard_map/ppermute | solution.py:39
  26.6 1.6 %collective-permute-start.10 = (bf16[256,512]{1,0:T(8,128)(2,1)S(1)}, bf16[256,512]{1,0:T(8,128)(2,1)S(1)}, u32[]{:S(2)}, u32[]{:S(2)}) collective-permute-start(bf16[256,512]{1,0:T(8,128)(2,1)S(1)} %get-tuple-element.59), channel_id=1, source_target_pairs={{0,2},{1,3},{2,0},{3,1},{4,6},{5,7},{6,4},{7,5},{8,9},{9,8},{10,11... | collective-permute-start | bytes 786440 | tf_op jit(solution)/shard_map/ppermute | solution.py:39
  29.2 2.3 %collective-permute-done.8.got = bf16[512,256]{1,0:T(8,128)(2,1)S(1)} collective-permute-done((bf16[512,256]{1,0:T(8,128)(2,1)S(1)}, bf16[512,256]{1,0:T(8,128)(2,1)S(1)}, u32[]{:S(2)}, u32[]{:S(2)}) %collective-permute-start.8) | collective-permute-done | bytes 262176 | tf_op jit(solution)/shard_map/ppermute | solution.py:39
  31.5 1.6 %collective-permute-start.9 = (bf16[128,256]{1,0:T(8,128)(2,1)S(1)}, bf16[128,256]{1,0:T(8,128)(2,1)S(1)}, u32[]{:S(2)}, u32[]{:S(2)}) collective-permute-start(bf16[128,256]{1,0:T(8,128)(2,1)S(1)} %get-tuple-element.57), channel_id=1, source_target_pairs={{0,2},{1,3},{2,0},{3,1},{4,6},{5,7},{6,4},{7,5},{8,24},{9,25},{10,... | collective-permute-start | bytes 196616 | tf_op jit(solution)/shard_map/ppermute | solution.py:39
  33.2 1.4 %collective-permute-start.11 = (bf16[128,256]{1,0:T(8,128)(2,1)S(1)}, bf16[128,256]{1,0:T(8,128)(2,1)S(1)}, u32[]{:S(2)}, u32[]{:S(2)}) collective-permute-start(bf16[128,256]{1,0:T(8,128)(2,1)S(1)} %get-tuple-element.63), channel_id=1, source_target_pairs={{0,3},{1,2},{2,1},{3,0},{4,7},{5,6},{6,5},{7,4},{8,26},{9,27},{10,... | collective-permute-start | bytes 196616 | tf_op jit(solution)/shard_map/ppermute | solution.py:39
  35.1 1.2 %collective-permute-done.9.refs_0_ = bf16[128,256]{1,0:T(8,128)(2,1)S(1)} collective-permute-done((bf16[128,256]{1,0:T(8,128)(2,1)S(1)}, bf16[128,256]{1,0:T(8,128)(2,1)S(1)}, u32[]{:S(2)}, u32[]{:S(2)}) %collective-permute-start.9) | collective-permute-done | bytes 65568 | tf_op jit(solution)/shard_map/ppermute | solution.py:39
  36.4 1.6 %collective-permute-start.17 = (bf16[128,512]{1,0:T(8,128)(2,1)S(1)}, bf16[128,512]{1,0:T(8,128)(2,1)S(1)}, u32[]{:S(2)}, u32[]{:S(2)}) collective-permute-start(bf16[128,512]{1,0:T(8,128)(2,1)S(1)} %get-tuple-element.67), channel_id=1, source_target_pairs={{0,1},{1,0},{2,3},{3,2},{4,5},{5,4},{6,7},{7,6},{8,10},{9,11},{10,... | collective-permute-start | bytes 393224 | tf_op jit(solution)/shard_map/ppermute | solution.py:39
  39.3 2.8 %collective-permute-start.13 = (bf16[128,256]{1,0:T(8,128)(2,1)S(1)}, bf16[128,256]{1,0:T(8,128)(2,1)S(1)}, u32[]{:S(2)}, u32[]{:S(2)}) collective-permute-start(bf16[128,256]{1,0:T(8,128)(2,1)S(1)} %shard_map.130.keep), channel_id=1, source_target_pairs={{0,4},{1,5},{2,6},{3,7},{4,0},{5,1},{6,2},{7,3},{8,12},{9,13},{10,... | collective-permute-start | bytes 196616 | tf_op jit(solution)/shard_map/ppermute | solution.py:30
  42.1 2.5 %collective-permute-done.13.refs_0_ = bf16[128,256]{1,0:T(8,128)(2,1)S(1)} collective-permute-done((bf16[128,256]{1,0:T(8,128)(2,1)S(1)}, bf16[128,256]{1,0:T(8,128)(2,1)S(1)}, u32[]{:S(2)}, u32[]{:S(2)}) %collective-permute-start.13) | collective-permute-done | bytes 65568 | tf_op jit(solution)/shard_map/ppermute | solution.py:30
  44.6 1.9 %collective-permute-start.14 = (bf16[128,256]{1,0:T(8,128)(2,1)S(1)}, bf16[128,256]{1,0:T(8,128)(2,1)S(1)}, u32[]{:S(2)}, u32[]{:S(2)}) collective-permute-start(bf16[128,256]{1,0:T(8,128)(2,1)S(1)} %shard_map.131.refs_0_), channel_id=1, source_target_pairs={{0,3},{1,2},{2,1},{3,0},{4,7},{5,6},{6,5},{7,4},{8,11},{9,10},{10,... | collective-permute-start | bytes 196616 | tf_op jit(solution)/shard_map/ppermute | solution.py:39
  46.4 1.6 %collective-permute-start.15 = (bf16[128,256]{1,0:T(8,128)(2,1)S(1)}, bf16[128,256]{1,0:T(8,128)(2,1)S(1)}, u32[]{:S(2)}, u32[]{:S(2)}) collective-permute-start(bf16[128,256]{1,0:T(8,128)(2,1)S(1)} %shard_map.131.refs_0_), channel_id=1, source_target_pairs={{0,2},{1,3},{2,0},{3,1},{4,6},{5,7},{6,4},{7,5},{8,9},{9,8},{10,11... | collective-permute-start | bytes 196616 | tf_op jit(solution)/shard_map/ppermute | solution.py:39
  48.2 2.9 %collective-permute-start.18 = (bf16[64,512]{1,0:T(8,128)(2,1)S(1)}, bf16[64,512]{1,0:T(8,128)(2,1)S(1)}, u32[]{:S(2)}, u32[]{:S(2)}) collective-permute-start(bf16[64,512]{1,0:T(8,128)(2,1)S(1)} %get-tuple-element.69), channel_id=1, source_target_pairs={{0,4},{1,5},{2,6},{3,7},{4,0},{5,1},{6,2},{7,3},{8,12},{9,13},{10,... | collective-permute-start | bytes 196616 | tf_op jit(solution)/shard_map/ppermute | solution.py:30
  51.1 1.2 %collective-permute-done.16.refs_3_ = bf16[128,256]{1,0:T(8,128)(2,1)S(1)} collective-permute-done((bf16[128,256]{1,0:T(8,128)(2,1)S(1)}, bf16[128,256]{1,0:T(8,128)(2,1)S(1)}, u32[]{:S(2)}, u32[]{:S(2)}) %collective-permute-start.16) | collective-permute-done | bytes 65568 | tf_op jit(solution)/shard_map/ppermute | solution.py:39
  52.3 1.2 %shard_map.132 = f32[256,512]{1,0:T(8,128)} custom-call(f32[256,64]{1,0:T(8,128)S(1)} %copy.13.kinv, bf16[128,256]{1,0:T(8,128)(2,1)S(1)} %shard_map.131.refs_0_, bf16[128,256]{1,0:T(8,128)(2,1)S(1)} %collective-permute-done.14.refs_1_, bf16[128,256]{1,0:T(8,128)(2,1)S(1)} %collective-permute-done.15.refs_2_, ...), custom_call_target="tpu_custom_call" | custom-call | flops 100663296 | bytes 1048576 | tf_op jit(solution)/shard_map/pallas_call | solution.py:370
  (50 shorter events, 6.5 us)
Async XLA Ops:
  0.6 7.0 %copy-start.6 = (bf16[64,512]{1,0:T(8,128)(2,1)S(1)}, bf16[64,512]{1,0:T(8,128)(2,1)}, u32[]{:S(2)}) copy-start(bf16[64,512]{1,0:T(8,128)(2,1)} %param.11) | copy-start | bytes 196612
  0.6 4.2 %collective-permute-start.4 = (bf16[256,512]{1,0:T(8,128)(2,1)}, bf16[256,512]{1,0:T(8,128)(2,1)S(1)}, u32[]{:S(2)}, u32[]{:S(2)}) collective-permute-start(bf16[256,512]{1,0:T(8,128)(2,1)} %refs_0_.5), channel_id=1, source_target_pairs={{0,8},{8,0},{16,24},{24,16},{1,9},{9,1},{17,25},{25,17},{2,10},{10... | collective-permute-start | bytes 786440 | tf_op jit(solution)/shard_map/ppermute | solution.py:26
  1.2 8.0 %collective-permute-start = (bf16[64,512]{1,0:T(8,128)(2,1)}, bf16[64,512]{1,0:T(8,128)(2,1)S(1)}, u32[]{:S(2)}, u32[]{:S(2)}) collective-permute-start(bf16[64,512]{1,0:T(8,128)(2,1)} %param.11), channel_id=1, source_target_pairs={{0,4},{1,5},{2,6},{3,7},{4,0},{5,1},{6,2},{7,3},{8,12},{9,13},{10,... | collective-permute-start | bytes 196616 | tf_op jit(solution)/shard_map/ppermute | solution.py:30
  4.8 8.6 %collective-permute-start.5 = (bf16[256,512]{1,0:T(8,128)(2,1)}, bf16[256,512]{1,0:T(8,128)(2,1)S(1)}, u32[]{:S(2)}, u32[]{:S(2)}) collective-permute-start(bf16[256,512]{1,0:T(8,128)(2,1)} %refs_0_.5), channel_id=1, source_target_pairs={{0,16},{8,24},{16,0},{24,8},{1,17},{9,25},{17,1},{25,9},{2,18},{10... | collective-permute-start | bytes 786440 | tf_op jit(solution)/shard_map/ppermute | solution.py:26
  6.3 11.5 %slice-start = ((s8[4718592]{0:T(1024)(128)(4,1)}), s8[4194304]{0:T(1024)(128)(4,1)S(1)}, s32[]{:S(2)}) async-start(s8[4718592]{0:T(1024)(128)(4,1)} %bitcast), calls=%async_computation | async-start | bytes 8388608
  9.2 8.7 %slice-start.1 = ((s8[4718592]{0:T(1024)(128)(4,1)}), s8[524288]{0:T(1024)(128)(4,1)S(1)}, s32[]{:S(2)}) async-start(s8[4718592]{0:T(1024)(128)(4,1)} %bitcast), calls=%async_computation.1 | async-start | bytes 1048576
  9.2 8.5 %collective-permute-start.1 = (bf16[128,512]{1,0:T(8,128)(2,1)S(1)}, bf16[128,512]{1,0:T(8,128)(2,1)S(1)}, u32[]{:S(2)}, u32[]{:S(2)}) collective-permute-start(bf16[128,512]{1,0:T(8,128)(2,1)S(1)} %constant_dynamic-update-slice_fusion.refs_0_), channel_id=1, source_target_pairs={{0,3},{1,2},{2,1},{3,0},{4,7},{5,6},{6,5},{7,4},{8,11},{9,10},{10,... | collective-permute-start | bytes 393224 | tf_op jit(solution)/shard_map/ppermute | solution.py:39
  11.0 6.8 %collective-permute-start.2 = (bf16[128,512]{1,0:T(8,128)(2,1)S(1)}, bf16[128,512]{1,0:T(8,128)(2,1)S(1)}, u32[]{:S(2)}, u32[]{:S(2)}) collective-permute-start(bf16[128,512]{1,0:T(8,128)(2,1)S(1)} %constant_dynamic-update-slice_fusion.refs_0_), channel_id=1, source_target_pairs={{0,2},{1,3},{2,0},{3,1},{4,6},{5,7},{6,4},{7,5},{8,9},{9,8},{10,11... | collective-permute-start | bytes 393224 | tf_op jit(solution)/shard_map/ppermute | solution.py:39
  12.3 5.6 %collective-permute-start.3 = (bf16[128,512]{1,0:T(8,128)(2,1)S(1)}, bf16[128,512]{1,0:T(8,128)(2,1)S(1)}, u32[]{:S(2)}, u32[]{:S(2)}) collective-permute-start(bf16[128,512]{1,0:T(8,128)(2,1)S(1)} %constant_dynamic-update-slice_fusion.refs_0_), channel_id=1, source_target_pairs={{0,1},{1,0},{2,3},{3,2},{4,5},{5,4},{6,7},{7,6},{8,10},{9,11},{10,... | collective-permute-start | bytes 393224 | tf_op jit(solution)/shard_map/ppermute | solution.py:39
  13.4 2.2 %collective-permute-start.6 = (bf16[256,512]{1,0:T(8,128)(2,1)S(1)}, bf16[256,512]{1,0:T(8,128)(2,1)S(1)}, u32[]{:S(2)}, u32[]{:S(2)}) collective-permute-start(bf16[256,512]{1,0:T(8,128)(2,1)S(1)} %collective-permute-done.5.refs_2_), channel_id=1, source_target_pairs={{0,8},{8,0},{16,24},{24,16},{1,9},{9,1},{17,25},{25,17},{2,10},{10... | collective-permute-start | bytes 786440 | tf_op jit(solution)/shard_map/ppermute | solution.py:26
  22.9 2.1 %collective-permute-start.7 = (bf16[1024,256]{1,0:T(8,128)(2,1)S(1)}, bf16[1024,256]{1,0:T(8,128)(2,1)S(1)}, u32[]{:S(2)}, u32[]{:S(2)}) collective-permute-start(bf16[1024,256]{1,0:T(8,128)(2,1)S(1)} %get-tuple-element.47), channel_id=1, source_target_pairs={{0,8},{8,0},{16,24},{24,16},{1,9},{9,1},{17,25},{25,17},{2,10},{10... | collective-permute-start | bytes 1572872 | tf_op jit(solution)/shard_map/ppermute | solution.py:26
  25.0 26.0 %copy-start.5 = (f32[256,64]{0,1:T(8,128)S(1)}, f32[256,64]{0,1:T(8,128)}, u32[]{:S(2)}) copy-start(f32[256,64]{0,1:T(8,128)} %param.18) | copy-start | bytes 196612
  25.1 6.4 %collective-permute-start.8 = (bf16[512,256]{1,0:T(8,128)(2,1)S(1)}, bf16[512,256]{1,0:T(8,128)(2,1)S(1)}, u32[]{:S(2)}, u32[]{:S(2)}) collective-permute-start(bf16[512,256]{1,0:T(8,128)(2,1)S(1)} %get-tuple-element.53), channel_id=1, source_target_pairs={{0,16},{1,17},{2,18},{3,19},{4,20},{5,21},{6,22},{7,23},{8,9},{9,8... | collective-permute-start | bytes 786440 | tf_op jit(solution)/shard_map/ppermute | solution.py:39
  26.6 9.7 %collective-permute-start.10 = (bf16[256,512]{1,0:T(8,128)(2,1)S(1)}, bf16[256,512]{1,0:T(8,128)(2,1)S(1)}, u32[]{:S(2)}, u32[]{:S(2)}) collective-permute-start(bf16[256,512]{1,0:T(8,128)(2,1)S(1)} %get-tuple-element.59), channel_id=1, source_target_pairs={{0,2},{1,3},{2,0},{3,1},{4,6},{5,7},{6,4},{7,5},{8,9},{9,8},{10,11... | collective-permute-start | bytes 786440 | tf_op jit(solution)/shard_map/ppermute | solution.py:39
  29.2 24.2 %copy-start.2 = (f32[64,64]{1,0:T(8,128)S(1)}, f32[64,64]{1,0:T(8,128)}, u32[]{:S(2)}) copy-start(f32[64,64]{1,0:T(8,128)} %kinv.2) | copy-start | bytes 49156
  31.5 4.8 %collective-permute-start.9 = (bf16[128,256]{1,0:T(8,128)(2,1)S(1)}, bf16[128,256]{1,0:T(8,128)(2,1)S(1)}, u32[]{:S(2)}, u32[]{:S(2)}) collective-permute-start(bf16[128,256]{1,0:T(8,128)(2,1)S(1)} %get-tuple-element.57), channel_id=1, source_target_pairs={{0,2},{1,3},{2,0},{3,1},{4,6},{5,7},{6,4},{7,5},{8,24},{9,25},{10,... | collective-permute-start | bytes 196616 | tf_op jit(solution)/shard_map/ppermute | solution.py:39
  33.2 5.8 %collective-permute-start.11 = (bf16[128,256]{1,0:T(8,128)(2,1)S(1)}, bf16[128,256]{1,0:T(8,128)(2,1)S(1)}, u32[]{:S(2)}, u32[]{:S(2)}) collective-permute-start(bf16[128,256]{1,0:T(8,128)(2,1)S(1)} %get-tuple-element.63), channel_id=1, source_target_pairs={{0,3},{1,2},{2,1},{3,0},{4,7},{5,6},{6,5},{7,4},{8,26},{9,27},{10,... | collective-permute-start | bytes 196616 | tf_op jit(solution)/shard_map/ppermute | solution.py:39
  34.6 4.7 %collective-permute-start.12 = (bf16[128,256]{1,0:T(8,128)(2,1)S(1)}, bf16[128,256]{1,0:T(8,128)(2,1)S(1)}, u32[]{:S(2)}, u32[]{:S(2)}) collective-permute-start(bf16[128,256]{1,0:T(8,128)(2,1)S(1)} %get-tuple-element.64), channel_id=1, source_target_pairs={{0,1},{1,0},{2,3},{3,2},{4,5},{5,4},{6,7},{7,6},{8,10},{9,11},{10,... | collective-permute-start | bytes 196616 | tf_op jit(solution)/shard_map/ppermute | solution.py:39
  36.4 11.7 %collective-permute-start.17 = (bf16[128,512]{1,0:T(8,128)(2,1)S(1)}, bf16[128,512]{1,0:T(8,128)(2,1)S(1)}, u32[]{:S(2)}, u32[]{:S(2)}) collective-permute-start(bf16[128,512]{1,0:T(8,128)(2,1)S(1)} %get-tuple-element.67), channel_id=1, source_target_pairs={{0,1},{1,0},{2,3},{3,2},{4,5},{5,4},{6,7},{7,6},{8,10},{9,11},{10,... | collective-permute-start | bytes 393224 | tf_op jit(solution)/shard_map/ppermute | solution.py:39
  39.3 5.2 %collective-permute-start.13 = (bf16[128,256]{1,0:T(8,128)(2,1)S(1)}, bf16[128,256]{1,0:T(8,128)(2,1)S(1)}, u32[]{:S(2)}, u32[]{:S(2)}) collective-permute-start(bf16[128,256]{1,0:T(8,128)(2,1)S(1)} %shard_map.130.keep), channel_id=1, source_target_pairs={{0,4},{1,5},{2,6},{3,7},{4,0},{5,1},{6,2},{7,3},{8,12},{9,13},{10,... | collective-permute-start | bytes 196616 | tf_op jit(solution)/shard_map/ppermute | solution.py:30
  44.6 6.6 %collective-permute-start.14 = (bf16[128,256]{1,0:T(8,128)(2,1)S(1)}, bf16[128,256]{1,0:T(8,128)(2,1)S(1)}, u32[]{:S(2)}, u32[]{:S(2)}) collective-permute-start(bf16[128,256]{1,0:T(8,128)(2,1)S(1)} %shard_map.131.refs_0_), channel_id=1, source_target_pairs={{0,3},{1,2},{2,1},{3,0},{4,7},{5,6},{6,5},{7,4},{8,11},{9,10},{10,... | collective-permute-start | bytes 196616 | tf_op jit(solution)/shard_map/ppermute | solution.py:39
  46.4 4.7 %collective-permute-start.15 = (bf16[128,256]{1,0:T(8,128)(2,1)S(1)}, bf16[128,256]{1,0:T(8,128)(2,1)S(1)}, u32[]{:S(2)}, u32[]{:S(2)}) collective-permute-start(bf16[128,256]{1,0:T(8,128)(2,1)S(1)} %shard_map.131.refs_0_), channel_id=1, source_target_pairs={{0,2},{1,3},{2,0},{3,1},{4,6},{5,7},{6,4},{7,5},{8,9},{9,8},{10,11... | collective-permute-start | bytes 196616 | tf_op jit(solution)/shard_map/ppermute | solution.py:39
  48.1 4.3 %collective-permute-start.16 = (bf16[128,256]{1,0:T(8,128)(2,1)S(1)}, bf16[128,256]{1,0:T(8,128)(2,1)S(1)}, u32[]{:S(2)}, u32[]{:S(2)}) collective-permute-start(bf16[128,256]{1,0:T(8,128)(2,1)S(1)} %shard_map.131.refs_0_), channel_id=1, source_target_pairs={{0,1},{1,0},{2,3},{3,2},{4,5},{5,4},{6,7},{7,6},{8,10},{9,11},{10,... | collective-permute-start | bytes 196616 | tf_op jit(solution)/shard_map/ppermute | solution.py:39
  48.2 5.3 %collective-permute-start.18 = (bf16[64,512]{1,0:T(8,128)(2,1)S(1)}, bf16[64,512]{1,0:T(8,128)(2,1)S(1)}, u32[]{:S(2)}, u32[]{:S(2)}) collective-permute-start(bf16[64,512]{1,0:T(8,128)(2,1)S(1)} %get-tuple-element.69), channel_id=1, source_target_pairs={{0,4},{1,5},{2,6},{3,7},{4,0},{5,1},{6,2},{7,3},{8,12},{9,13},{10,... | collective-permute-start | bytes 196616 | tf_op jit(solution)/shard_map/ppermute | solution.py:30
  (4 other events, 21.8 us)
